TPU v7x, 32 devices: a whole 2x2x4 slice. The times are simulated.
32 devices in a mesh: heads: 4 (over y, x), blk: 8 (over z, core).
Axes of the slice: x: 2, y: 2, z: 4, core: 2. Of those that a mesh axis runs over, the one named last changes fastest.
Arguments:
- tokens: bfloat16 [2, 2048, 1024], P(None, ('blk', 'heads')), may hold values from -10.5 to 10.5
- cotangent: bfloat16 [2, 2048, 1024], P(None, ('blk', 'heads')), may hold values from -6 to 6
- doc_offsets: int32 [2, 16], replicated, may hold values from 0 to 2047, as said below
- valid_flags: int32 [2, 2048], replicated, may hold values 0 or 1
- w_query: bfloat16 [1024, 1024], P(('blk', 'heads')), may hold values from -0.1875 to 0.1875
- w_key: bfloat16 [1024, 1024], P(('blk', 'heads')), may hold values from -0.1875 to 0.1875
- w_value: bfloat16 [1024, 1024], P(('blk', 'heads')), may hold values from -0.1875 to 0.1875
- w_out: bfloat16 [1024, 1024], P(('blk', 'heads')), may hold values from -1.5 to 1.5
- w_fc1: bfloat16 [1024, 4096], P(('blk', 'heads')), may hold values from -0.1875 to 0.1875
- w_fc2: bfloat16 [4096, 1024], P(('blk', 'heads')), may hold values from -0.09375 to 0.09375
- b_query: bfloat16 [1024], P(('blk', 'heads')), may hold values from -3 to 3
- b_value: bfloat16 [1024], P(('blk', 'heads')), may hold values from -2 to 2
- b_out: bfloat16 [1024], P(('blk', 'heads')), may hold values from -2 to 2
- b_fc1: bfloat16 [4096], P(('blk', 'heads')), may hold values from -3 to 3
- b_fc2: bfloat16 [1024], P(('blk', 'heads')), may hold values from -2 to 2
- gain_attn: bfloat16 [1024], P(('blk', 'heads')), may hold values from 0.5 to 1.5
- bias_attn: bfloat16 [1024], P(('blk', 'heads')), may hold values from -2 to 2
- gain_ffn: bfloat16 [1024], P(('blk', 'heads')), may hold values from 0.5 to 1.5
- bias_ffn: bfloat16 [1024], P(('blk', 'heads')), may hold values from -2 to 2
Outputs:
- output: bfloat16 [2, 2048, 1024], P(None, ('blk', 'heads'))
- grad_tokens: float32 [2, 2048, 1024], P(None, ('blk', 'heads'))
- grad_w_query: float32 [1024, 1024], P(('blk', 'heads'))
- grad_w_key: float32 [1024, 1024], P(('blk', 'heads'))
- grad_w_value: float32 [1024, 1024], P(('blk', 'heads'))
- grad_w_out: float32 [1024, 1024], P(('blk', 'heads'))
- grad_w_fc1: float32 [1024, 4096], P(('blk', 'heads'))
- grad_w_fc2: float32 [4096, 1024], P(('blk', 'heads'))
- grad_b_query: float32 [1024], P(('blk', 'heads'))
- grad_b_value: float32 [1024], P(('blk', 'heads'))
- grad_b_out: float32 [1024], P(('blk', 'heads'))
- grad_b_fc1: float32 [4096], P(('blk', 'heads'))
- grad_b_fc2: float32 [1024], P(('blk', 'heads'))
- grad_gain_attn: float32 [1024], P(('blk', 'heads'))
- grad_bias_attn: float32 [1024], P(('blk', 'heads'))
- grad_gain_ffn: float32 [1024], P(('blk', 'heads'))
- grad_bias_ffn: float32 [1024], P(('blk', 'heads'))
- rms: float32 [4], replicated
Inputs may be any that keep to these rules, and one draw needn't show every extreme that they name: `doc_offsets`: each row starts with 0 and rises strictly; entry j is where document j of that sequence begins, and the last document runs to the end of the sequence.
All inputs are finite; a program needn't handle non-finite values.
Results may differ from a plain program's by a relative error of at most 0.015.
Values may be sent and summed in bfloat16 or wider, within the bound.
No kernel may reach another device: no remote copies, remote signals or barrier semaphores. Data moves between devices by JAX's collectives and lax.ppermute only.
A program may use at most 128 MiB of HBM per device.

v0:
```python
import jax
import jax.numpy as jnp
from jax import lax
from jax.sharding import PartitionSpec as P

HEAD_DIM = 64


norm_eps = 1e-05
neg_large = -1e30


def passed_along(block, axis, distance):
    devices = range(lax.axis_size(axis))
    route = [((i - distance) % len(devices), i) for i in devices]
    return lax.ppermute(block, axis, route)


def matmul(left, right):
    return jnp.dot(left, right, preferred_element_type=jnp.float32)


def matmul_tn(left, right):
    return lax.dot_general(
        left, right, (((0,), (0,)), ((), ())), preferred_element_type=jnp.float32
    )


def matmul_nt(left, right):
    return lax.dot_general(
        left, right, (((1,), (1,)), ((), ())), preferred_element_type=jnp.float32
    )


def layer_norm(resid, norm_gain, norm_bias):
    center = resid - jnp.mean(resid, axis=-1, keepdims=True)
    inv_std = lax.rsqrt(jnp.mean(center * center, axis=-1, keepdims=True) + norm_eps)
    normed = center * inv_std
    return (normed * norm_gain + norm_bias, normed, inv_std)


def norm_back(upstream, normed, inv_std, norm_gain):
    scaled = upstream * norm_gain
    return inv_std * (
        scaled
        - jnp.mean(scaled, axis=-1, keepdims=True)
        - normed * jnp.mean(scaled * normed, axis=-1, keepdims=True)
    )


def gelu_slope(hidden):
    cdf_part = 0.5 * (1.0 + lax.erf(hidden * 0.7071067811865476))
    pdf_part = jnp.exp(-0.5 * hidden * hidden) * 0.3989422804014327
    return cdf_part + hidden * pdf_part


def split_heads(block):
    return block.reshape(block.shape[0], block.shape[1] // HEAD_DIM, HEAD_DIM)


def head_scores(queries, keys):
    return jnp.einsum("qhd,khd->hqk", queries, keys, preferred_element_type=jnp.float32)


def segment_of(offsets, places):
    return jnp.sum((offsets[:, None, :] <= places[None, :, None]).astype(jnp.int32), axis=2) - 1


def pair_mask(seg_query, pos_query, seg_key, pos_key, valid_key):
    same_doc = seg_query[:, None] == seg_key[None, :]
    usable = (valid_key[None, :] > 0) | (pos_query[:, None] == pos_key[None, :])
    return same_doc & usable


def pass_grads(grads):
    return passed_along(grads.astype(jnp.bfloat16), "blk", 1).astype(grads.dtype)


def grad_work(allowed, queries_now, upstream_now, norm_now, delta_now, keys_now, values_now):

    def work(inner):
        grad_query, grad_key, grad_value = inner
        scores = head_scores(queries_now, keys_now)
        probs = jnp.where(allowed[None], jnp.exp(scores - norm_now[..., None]), 0.0)
        grad_probs = head_scores(upstream_now, values_now)
        grad_scores = (probs * (grad_probs - delta_now[..., None])).astype(jnp.bfloat16)
        grad_query = grad_query + jnp.einsum(
            "hqk,khd->hqd", grad_scores, keys_now, preferred_element_type=jnp.float32
        )
        grad_key = grad_key + jnp.einsum(
            "hqk,qhd->khd", grad_scores, queries_now, preferred_element_type=jnp.float32
        )
        grad_value = grad_value + jnp.einsum(
            "hqk,qhd->khd",
            probs.astype(jnp.bfloat16),
            upstream_now,
            preferred_element_type=jnp.float32,
        )
        return (grad_query, grad_key, grad_value)

    return work


def per_device(
    tokens,
    cotangent,
    doc_offsets,
    valid_flags,
    w_query,
    w_key,
    w_value,
    w_out,
    w_fc1,
    w_fc2,
    b_query,
    b_value,
    b_out,
    b_fc1,
    b_fc2,
    gain_attn,
    bias_attn,
    gain_ffn,
    bias_ffn,
):
    seq_count, seq_dev, width = tokens.shape
    head_groups = lax.axis_size("heads")
    cycle_size = lax.axis_size("blk")
    block_rows = seq_dev * head_groups
    row_count = seq_count * seq_dev
    span_index = lax.axis_index(("blk", "heads"))
    cycle_index = lax.axis_index("blk")
    qk_scale = HEAD_DIM ** (-0.5)
    shape_tok = (seq_count, seq_dev, width)
    params = (
        w_query,
        w_key,
        w_value,
        w_out,
        w_fc1,
        w_fc2,
        b_query,
        b_value,
        b_out,
        b_fc1,
        b_fc2,
        gain_attn,
        bias_attn,
        gain_ffn,
        bias_ffn,
    )
    full = (
        lax.all_gather(params[0], ("blk", "heads"), axis=0, tiled=True),
        lax.all_gather(params[1], ("blk", "heads"), axis=0, tiled=True),
        lax.all_gather(params[2], ("blk", "heads"), axis=0, tiled=True),
        lax.all_gather(params[3], ("blk", "heads"), axis=0, tiled=True),
        lax.all_gather(params[4], ("blk", "heads"), axis=0, tiled=True),
        lax.all_gather(params[5], ("blk", "heads"), axis=0, tiled=True),
        lax.all_gather(params[6], ("blk", "heads"), axis=0, tiled=True),
        lax.all_gather(params[7], ("blk", "heads"), axis=0, tiled=True),
        lax.all_gather(params[8], ("blk", "heads"), axis=0, tiled=True),
        lax.all_gather(params[9], ("blk", "heads"), axis=0, tiled=True),
        lax.all_gather(params[10], ("blk", "heads"), axis=0, tiled=True),
        lax.all_gather(params[11], ("blk", "heads"), axis=0, tiled=True),
        lax.all_gather(params[12], ("blk", "heads"), axis=0, tiled=True),
        lax.all_gather(params[13], ("blk", "heads"), axis=0, tiled=True),
        lax.all_gather(params[14], ("blk", "heads"), axis=0, tiled=True),
    )
    mat_query, mat_key, mat_value, mat_out, mat_up, mat_down = full[:6]
    vec_query, vec_value, vec_out, vec_up, vec_down, gain_one, bias_one, gain_two, bias_two = [
        item.astype(jnp.float32) for item in full[6:]
    ]
    token_rows = tokens.reshape(row_count, width)
    resid_in = token_rows.astype(jnp.float32)
    query_tok = ((matmul(token_rows, mat_query) + vec_query) * qk_scale).astype(jnp.bfloat16)
    key_tok = matmul(token_rows, mat_key).astype(jnp.bfloat16)
    value_tok = (matmul(token_rows, mat_value) + vec_value).astype(jnp.bfloat16)
    query_h, key_h, value_h = (
        lax.all_to_all(
            query_tok.reshape(shape_tok), "heads", split_axis=2, concat_axis=1, tiled=True
        ),
        lax.all_to_all(
            key_tok.reshape(shape_tok), "heads", split_axis=2, concat_axis=1, tiled=True
        ),
        lax.all_to_all(
            value_tok.reshape(shape_tok), "heads", split_axis=2, concat_axis=1, tiled=True
        ),
    )
    query_heads = [split_heads(query_h[which]) for which in range(seq_count)]
    heads_here = query_heads[0].shape[1]
    width_here = heads_here * HEAD_DIM

    def masks_between(query_source, key_source):
        query_pos = query_source * block_rows + jnp.arange(block_rows, dtype=jnp.int32)
        query_seg = segment_of(doc_offsets, query_pos)
        key_pos = key_source * block_rows + jnp.arange(block_rows, dtype=jnp.int32)
        key_seg = segment_of(doc_offsets, key_pos)
        key_valid = lax.dynamic_slice_in_dim(valid_flags, key_source * block_rows, block_rows, 1)
        return [
            pair_mask(query_seg[which], query_pos, key_seg[which], key_pos, key_valid[which])
            for which in range(seq_count)
        ]

    def block_masks(source):
        return masks_between(cycle_index, source)

    def norm_update(state, keys_block, masks):
        result = []
        for which in range(seq_count):

            def work(
                carry,
                allowed=masks[which],
                keys_now=split_heads(keys_block[which]),
                queries_now=query_heads[which],
            ):
                run_max, run_sum = carry
                scores = jnp.where(allowed[None], head_scores(queries_now, keys_now), neg_large)
                new_max = jnp.maximum(run_max, jnp.max(scores, axis=-1))
                terms = jnp.where(allowed[None], jnp.exp(scores - new_max[..., None]), 0.0)
                return (new_max, run_sum * jnp.exp(run_max - new_max) + jnp.sum(terms, axis=-1))

            result.append(work(state[which]))
        return tuple(result)

    start_state = tuple(
        (
            (
                jnp.full((heads_here, block_rows), neg_large, jnp.float32),
                jnp.zeros((heads_here, block_rows), jnp.float32),
            )
            for which in range(seq_count)
        )
    )
    state = norm_update(start_state, key_h, block_masks(cycle_index))

    def norm_turn(turn, carry):
        keys_block, inner = carry
        keys_block = passed_along(keys_block, "blk", 1)
        return (
            keys_block,
            norm_update(inner, keys_block, block_masks((cycle_index - turn) % cycle_size)),
        )

    state = lax.fori_loop(1, cycle_size, norm_turn, (key_h, state))[1]
    log_norm = [run_max + jnp.log(run_sum) for run_max, run_sum in state]

    def value_update(accums, pair_block, masks):
        result = []
        for which in range(seq_count):

            def work(
                accum,
                allowed=masks[which],
                keys_now=split_heads(pair_block[0, which]),
                values_now=split_heads(pair_block[1, which]),
                queries_now=query_heads[which],
                norm_now=log_norm[which],
            ):
                scores = head_scores(queries_now, keys_now)
                probs = jnp.where(allowed[None], jnp.exp(scores - norm_now[..., None]), 0.0)
                return accum + jnp.einsum(
                    "hqk,khd->hqd",
                    probs.astype(jnp.bfloat16),
                    values_now,
                    preferred_element_type=jnp.float32,
                )

            result.append(work(accums[which]))
        return tuple(result)

    kv_pair = jnp.stack([key_h, value_h])
    zero_accum = tuple(
        (jnp.zeros((heads_here, block_rows, HEAD_DIM), jnp.float32) for which in range(seq_count))
    )
    accums = value_update(zero_accum, kv_pair, block_masks(cycle_index))

    def value_turn(turn, carry):
        pair_block, inner = carry
        pair_block = passed_along(pair_block, "blk", 1)
        return (
            pair_block,
            value_update(inner, pair_block, block_masks((cycle_index - turn) % cycle_size)),
        )

    attn_f32 = lax.fori_loop(1, cycle_size, value_turn, (kv_pair, accums))[1]
    attn_heads = jnp.stack(
        [jnp.transpose(item, (1, 0, 2)).reshape(block_rows, width_here) for item in attn_f32]
    ).astype(jnp.bfloat16)
    attn_tok = lax.all_to_all(attn_heads, "heads", split_axis=1, concat_axis=2, tiled=True).reshape(
        row_count, width
    )
    branch = matmul(attn_tok, mat_out) + vec_out
    normed_one, unit_one, inv_one = layer_norm(resid_in + branch, gain_one, bias_one)
    normed_low = normed_one.astype(jnp.bfloat16)
    hidden = matmul(normed_low, mat_up) + vec_up
    act_low = jax.nn.gelu(hidden, approximate=False).astype(jnp.bfloat16)
    ffn = matmul(act_low, mat_down) + vec_down
    normed_two, unit_two, inv_two = layer_norm(normed_one + ffn, gain_two, bias_two)
    output = normed_two.astype(jnp.bfloat16).reshape(shape_tok)
    local_flags = (
        lax.dynamic_slice_in_dim(valid_flags, span_index * seq_dev, seq_dev, 1)
        .reshape(row_count)
        .astype(jnp.float32)
    )
    squares = jnp.stack(
        [
            jnp.sum(local_flags * jnp.sum(item * item, axis=1))
            for item in (resid_in, branch, normed_one, ffn)
        ]
    )
    totals = lax.psum(squares, ("blk", "heads"))
    real_count = jnp.maximum(jnp.sum(valid_flags.astype(jnp.float32)), 1.0)
    rms = jnp.sqrt(totals / (real_count * width))
    again = (
        lax.all_gather(w_query, ("blk", "heads"), axis=0, tiled=True),
        lax.all_gather(w_key, ("blk", "heads"), axis=0, tiled=True),
        lax.all_gather(w_value, ("blk", "heads"), axis=0, tiled=True),
        lax.all_gather(w_out, ("blk", "heads"), axis=0, tiled=True),
        lax.all_gather(w_fc1, ("blk", "heads"), axis=0, tiled=True),
        lax.all_gather(w_fc2, ("blk", "heads"), axis=0, tiled=True),
        lax.all_gather(gain_attn, ("blk", "heads"), axis=0, tiled=True),
        lax.all_gather(gain_ffn, ("blk", "heads"), axis=0, tiled=True),
    )
    back_query, back_key, back_value, back_out, back_up, back_down = again[:6]
    back_gain_one = again[6].astype(jnp.float32)
    back_gain_two = again[7].astype(jnp.float32)
    upstream = cotangent.reshape(row_count, width).astype(jnp.float32)
    grad_gain_two = jnp.sum(upstream * unit_two, axis=0)
    grad_bias_two = jnp.sum(upstream, axis=0)
    grad_resid_two = norm_back(upstream, unit_two, inv_two, back_gain_two)
    grad_ffn = grad_resid_two.astype(jnp.bfloat16)
    grad_vec_down = jnp.sum(grad_ffn.astype(jnp.float32), axis=0)
    grad_mat_down = matmul_tn(act_low, grad_ffn)
    grad_hidden = (matmul_nt(grad_ffn, back_down) * gelu_slope(hidden)).astype(jnp.bfloat16)
    grad_vec_up = jnp.sum(grad_hidden.astype(jnp.float32), axis=0)
    grad_mat_up = matmul_tn(normed_low, grad_hidden)
    grad_normed_one = grad_resid_two + matmul_nt(grad_hidden, back_up)
    grad_gain_one = jnp.sum(grad_normed_one * unit_one, axis=0)
    grad_bias_one = jnp.sum(grad_normed_one, axis=0)
    grad_resid_one = norm_back(grad_normed_one, unit_one, inv_one, back_gain_one)
    grad_branch = grad_resid_one.astype(jnp.bfloat16)
    grad_vec_out = jnp.sum(grad_branch.astype(jnp.float32), axis=0)
    grad_mat_out = matmul_tn(attn_tok, grad_branch)
    grad_attn = matmul_nt(grad_branch, back_out).astype(jnp.bfloat16)
    grad_attn_h = lax.all_to_all(
        grad_attn.reshape(shape_tok), "heads", split_axis=2, concat_axis=1, tiled=True
    )
    grad_heads = [split_heads(grad_attn_h[which]) for which in range(seq_count)]
    deltas = [
        jnp.sum(
            jnp.transpose(grad_heads[which], (1, 0, 2)).astype(jnp.float32) * attn_f32[which],
            axis=-1,
        )
        for which in range(seq_count)
    ]

    def grad_update(query_grads, pair_grads, pair_block, masks):
        new_query, new_keys, new_values = ([], [], [])
        for which in range(seq_count):
            work = grad_work(
                masks[which],
                query_heads[which],
                grad_heads[which],
                log_norm[which],
                deltas[which],
                split_heads(pair_block[0, which]),
                split_heads(pair_block[1, which]),
            )
            inner = (
                query_grads[which],
                split_heads(pair_grads[0, which]),
                split_heads(pair_grads[1, which]),
            )
            grad_query, grad_key, grad_value = work(inner)
            new_query.append(grad_query)
            new_keys.append(grad_key.reshape(block_rows, width_here))
            new_values.append(grad_value.reshape(block_rows, width_here))
        return (tuple(new_query), jnp.stack([jnp.stack(new_keys), jnp.stack(new_values)]))

    pair_zero = jnp.zeros((2, seq_count, block_rows, width_here), jnp.float32)
    query_grads, pair_grads = grad_update(zero_accum, pair_zero, kv_pair, block_masks(cycle_index))

    def grad_turn(turn, carry):
        pair_block, grads_query, grads_pair = carry
        grads_pair = pass_grads(grads_pair)
        pair_block = passed_along(pair_block, "blk", 1)
        grads_query, grads_pair = grad_update(
            grads_query, grads_pair, pair_block, block_masks((cycle_index - turn) % cycle_size)
        )
        return (pair_block, grads_query, grads_pair)

    loop_out = lax.fori_loop(1, cycle_size, grad_turn, (kv_pair, query_grads, pair_grads))
    query_grads = loop_out[1]
    pair_grads = pass_grads(loop_out[2])
    grad_query_heads = jnp.stack(
        [jnp.transpose(item, (1, 0, 2)).reshape(block_rows, width_here) for item in query_grads]
    ).astype(jnp.bfloat16)
    grad_pair_low = pair_grads.astype(jnp.bfloat16)
    grad_query_tok, grad_key_tok, grad_value_tok = (
        lax.all_to_all(grad_query_heads, "heads", split_axis=1, concat_axis=2, tiled=True),
        lax.all_to_all(grad_pair_low[0], "heads", split_axis=1, concat_axis=2, tiled=True),
        lax.all_to_all(grad_pair_low[1], "heads", split_axis=1, concat_axis=2, tiled=True),
    )
    grad_query_pre = grad_query_tok.reshape(row_count, width).astype(jnp.float32) * qk_scale
    grad_query_low = grad_query_pre.astype(jnp.bfloat16)
    grad_key_low = grad_key_tok.reshape(row_count, width)
    grad_value_low = grad_value_tok.reshape(row_count, width)
    grad_vec_query = jnp.sum(grad_query_pre, axis=0)
    grad_vec_value = jnp.sum(grad_value_low.astype(jnp.float32), axis=0)
    grad_mat_query = matmul_tn(token_rows, grad_query_low)
    grad_mat_key = matmul_tn(token_rows, grad_key_low)
    grad_mat_value = matmul_tn(token_rows, grad_value_low)
    grad_input = (
        grad_resid_one
        + matmul_nt(grad_query_low, back_query)
        + matmul_nt(grad_key_low, back_key)
        + matmul_nt(grad_value_low, back_value)
    )
    shards = (
        lax.psum_scatter(grad_mat_query, ("blk", "heads"), scatter_dimension=0, tiled=True),
        lax.psum_scatter(grad_mat_key, ("blk", "heads"), scatter_dimension=0, tiled=True),
        lax.psum_scatter(grad_mat_value, ("blk", "heads"), scatter_dimension=0, tiled=True),
        lax.psum_scatter(grad_mat_out, ("blk", "heads"), scatter_dimension=0, tiled=True),
        lax.psum_scatter(grad_mat_up, ("blk", "heads"), scatter_dimension=0, tiled=True),
        lax.psum_scatter(grad_mat_down, ("blk", "heads"), scatter_dimension=0, tiled=True),
        lax.psum_scatter(grad_vec_query, ("blk", "heads"), scatter_dimension=0, tiled=True),
        lax.psum_scatter(grad_vec_value, ("blk", "heads"), scatter_dimension=0, tiled=True),
        lax.psum_scatter(grad_vec_out, ("blk", "heads"), scatter_dimension=0, tiled=True),
        lax.psum_scatter(grad_vec_up, ("blk", "heads"), scatter_dimension=0, tiled=True),
        lax.psum_scatter(grad_vec_down, ("blk", "heads"), scatter_dimension=0, tiled=True),
        lax.psum_scatter(grad_gain_one, ("blk", "heads"), scatter_dimension=0, tiled=True),
        lax.psum_scatter(grad_bias_one, ("blk", "heads"), scatter_dimension=0, tiled=True),
        lax.psum_scatter(grad_gain_two, ("blk", "heads"), scatter_dimension=0, tiled=True),
        lax.psum_scatter(grad_bias_two, ("blk", "heads"), scatter_dimension=0, tiled=True),
    )
    return (output, grad_input.reshape(shape_tok)) + tuple(shards) + (rms,)


def solution(mesh):
    placed = (
        P(None, ("blk", "heads"), None),
        P(None, ("blk", "heads"), None),
        P(),
        P(),
        P(("blk", "heads"), None),
        P(("blk", "heads"), None),
        P(("blk", "heads"), None),
        P(("blk", "heads"), None),
        P(("blk", "heads"), None),
        P(("blk", "heads"), None),
        P(("blk", "heads")),
        P(("blk", "heads")),
        P(("blk", "heads")),
        P(("blk", "heads")),
        P(("blk", "heads")),
        P(("blk", "heads")),
        P(("blk", "heads")),
        P(("blk", "heads")),
        P(("blk", "heads")),
    )
    return jax.shard_map(
        per_device,
        mesh=mesh,
        in_specs=placed,
        out_specs=(
            P(None, ("blk", "heads"), None),
            P(None, ("blk", "heads"), None),
            P(("blk", "heads"), None),
            P(("blk", "heads"), None),
            P(("blk", "heads"), None),
            P(("blk", "heads"), None),
            P(("blk", "heads"), None),
            P(("blk", "heads"), None),
            P(("blk", "heads")),
            P(("blk", "heads")),
            P(("blk", "heads")),
            P(("blk", "heads")),
            P(("blk", "heads")),
            P(("blk", "heads")),
            P(("blk", "heads")),
            P(("blk", "heads")),
            P(("blk", "heads")),
            P(),
        ),
        check_vma=False,
    )
```

profile of v0, /device:TPU:0, one launch (start us, length us, event | category | flops | bytes accessed | tf_op | source)
XLA Modules:
  0.0 1785.9 jit_solution(4787241578859803358)
XLA Ops:
  20.7 42.3 %all-reduce.18 = (bf16[1024]{0:T(1024)(128)(2,1)S(1)}, bf16[1024]{0:T(1024)(128)(2,1)S(1)}, bf16[1024]{0:T(1024)(128)(2,1)S(1)}, bf16[1024]{0:T(1024)(128)(2,1)S...) all-reduce(bf16[1024]{0:T(1024)(128)(2,1)S(1)} %dynamic-update-slic, ...), channel_id=1, replica_groups=mesh['heads'=4,'blk'=8] {'blk','heads'}, use_global_device_ids=true, to_apply=%add.5 | all-reduce | flops 8192 | bytes 32768
  63.0 65.7 %all-gather = bf16[32,1,128]{2,1,0:T(2,128)(2,1)S(1)} all-gather(bf16[1,1,128]{2,1,0:T(2,128)(2,1)} %bitcast.511), channel_id=1, replica_groups=mesh['heads'=4,'blk'=8] {'blk','heads'}, dimensions={0}, use_global_device_ids=true | all-gather | bytes 8448 | tf_op jit(solution)/shard_map/all_gather | solution.py:161
  142.2 44.7 %all-gather.10.cloned.1.call-done = bf16[1024,1024]{1,0:T(8,128)(2,1)} async-done(((bf16[32,1024]{1,0:T(8,128)(2,1)}), bf16[1024,1024]{1,0:T(8,128)(2,1)}) %all-gather.10.cloned.1.call-update) | async-done | bytes 2097168 | tf_op jit(solution)/shard_map/all_gather | solution.py:154
  210.3 68.8 %while.66 = (s32[]{:T(128)}, bf16[2,256,256]{1,2,0:T(8,128)(2,1)S(1)}, f32[4,256]{1,0:T(4,128)S(1)}, f32[4,256]{1,0:T(4,128)S(1)}, f32[4,256]{1,0:T(4,128)S(1)},...) while((s32[]{:T(128)}, ...), condition=%wide.region_12.13_spmd, body=%wide.region_5.12_spmd.sunk | while | flops 70243344 | bytes 7349784 | solution.py:244
  284.2 122.3 %while.67 = (s32[]{:T(128)}, bf16[2,2,256,256]{2,3,1,0:T(8,128)(2,1)}, f32[4,256,64]{1,2,0:T(8,128)S(1)}, f32[4,256,64]{1,2,0:T(8,128)S(1)}, s32[2,16]{1,0:T(2,1...) while((s32[]{:T(128)}, ...), condition=%wide.region_16.17_spmd, body=%wide.region_13.16_spmd.sunk | while | flops 136430608 | bytes 6333976 | solution.py:285
  285.5 14.9 collective-permute-done.1
  303.6 20.4 %collective-permute-done.1 = bf16[2,2,256,256]{2,3,1,0:T(8,128)(2,1)S(1)} collective-permute-done((bf16[2,2,256,256]{2,3,1,0:T(8,128)(2,1)}, bf16[2,2,256,256]{2,3,1,0:T(8,128)(2,1)S(1)}, u32[]{:S(2)}, u32[]{:S(2)}) %collective-permute-start.1) | collective-permute-done | bytes 524320 | tf_op jit(solution)/shard_map/while/body/eval_jaxpr/ppermute | solution.py:16
  327.1 12.8 collective-permute-done.1
  369.6 18.2 %collective-permute-done.1 = bf16[2,2,256,256]{2,3,1,0:T(8,128)(2,1)S(1)} collective-permute-done((bf16[2,2,256,256]{2,3,1,0:T(8,128)(2,1)}, bf16[2,2,256,256]{2,3,1,0:T(8,128)(2,1)S(1)}, u32[]{:S(2)}, u32[]{:S(2)}) %collective-permute-start.1) | collective-permute-done | bytes 524320 | tf_op jit(solution)/shard_map/while/body/eval_jaxpr/ppermute | solution.py:16
  390.9 13.7 collective-permute-done.1
  475.9 140.7 %while.68 = (s32[]{:T(128)}, bf16[2,2,256,256]{2,3,1,0:T(8,128)(2,1)}, f32[4,256,64]{1,2,0:T(8,128)S(1)}, f32[4,256,64]{1,2,0:T(8,128)S(1)}, bf16[2,2,256,256]{2...) while((s32[]{:T(128)}, ...), condition=%wide.region_30.31_spmd, body=%wide.region_27.30_spmd.sunk | while | flops 340116480 | bytes 26789480 | solution.py:392
  497.4 11.6 collective-permute-done.2
  518.3 11.6 collective-permute-done.2
  538.2 11.6 collective-permute-done.2
  559.0 10.7 collective-permute-done.2
  579.1 11.1 collective-permute-done.2
  636.0 11.6 collective-permute-done.4
  665.6 10.8 all_to_all.119
  685.8 10.9 fusion.89
  716.4 39.2 %all-reduce.17 = (f32[1024]{0:T(1024)S(1)}, f32[1024]{0:T(1024)S(1)}, f32[1024]{0:T(1024)S(1)}, f32[4096]{0:T(1024)S(1)}, f32[1024]{0:T(1024)S(1)}, /*index=5*/f...) all-reduce(f32[1024]{0:T(1024)S(1)} %bitcast.507, ...), channel_id=8, replica_groups=mesh['heads'=4,'blk'=8] {'blk','heads'}, use_global_device_ids=true, to_apply=%region_38.39.clone | all-reduce | flops 12292 | bytes 98336
  773.1 143.1 %reduce-scatter.21.cloned.1.call-done = f32[32,1024]{1,0:T(8,128)} async-done(((f32[1024,1024]{1,0:T(8,128)}), f32[32,1024]{1,0:T(8,128)}) %reduce-scatter.21.cloned.1.call-update) | async-done | bytes 131088
  916.2 141.7 %reduce-scatter.23.cloned.1.call-done = f32[32,1024]{1,0:T(8,128)} async-done(((f32[1024,1024]{1,0:T(8,128)}), f32[32,1024]{1,0:T(8,128)}) %reduce-scatter.23.cloned.1.call-update) | async-done | bytes 131088
  1057.9 358.9 %reduce-scatter.17.cloned.1.call-done = f32[128,1024]{1,0:T(8,128)} async-done(((f32[4096,1024]{1,0:T(8,128)}), f32[128,1024]{1,0:T(8,128)}) %reduce-scatter.17.cloned.1.call-update) | async-done | bytes 524304 | tf_op jit(solution)/shard_map/reduce_scatter | solution.py:425
  1416.8 361.8 %reduce-scatter.15.cloned.1.call-done = f32[32,4096]{1,0:T(8,128)} async-done(((f32[1024,4096]{1,0:T(8,128)}), f32[32,4096]{1,0:T(8,128)}) %reduce-scatter.15.cloned.1.call-update) | async-done | bytes 524304 | tf_op jit(solution)/shard_map/reduce_scatter | solution.py:424
  (793 shorter events, 397.2 us)
Async XLA Ops:
  7.2 124.3 %all-gather.12.cloned.1.call-start = ((), (), s32[]{:S(2)}) async-start(), calls=%async_computation.16 | async-start | bytes 2162688 | tf_op jit(solution)/shard_map/all_gather | solution.py:152
  7.9 127.3 %all-gather.8.cloned.1.call-start = ((), (), s32[]{:S(2)}) async-start(), calls=%async_computation.14 | async-start | bytes 2162688 | tf_op jit(solution)/shard_map/all_gather | solution.py:153
  8.7 178.2 %all-gather.10.cloned.1.call-start = ((), (), s32[]{:S(2)}) async-start(), calls=%async_computation.15 | async-start | bytes 2162688 | tf_op jit(solution)/shard_map/all_gather | solution.py:154
  9.4 407.3 %all-gather.14.cloned.1.call-start = ((), (), s32[]{:S(2)}) async-start(), calls=%async_computation.17 | async-start | bytes 2162688 | tf_op jit(solution)/shard_map/all_gather | solution.py:155
  10.0 409.7 %all-gather.16.cloned.1.call-start = ((), (), s32[]{:S(2)}) async-start(), calls=%async_computation.18 | async-start | bytes 8650752 | tf_op jit(solution)/shard_map/all_gather | solution.py:156
  10.6 416.3 %all-gather.18.cloned.1.call-start = ((), (), s32[]{:S(2)}) async-start(), calls=%async_computation.19 | async-start | bytes 8650752 | tf_op jit(solution)/shard_map/all_gather | solution.py:157
  138.8 51.6 %all-to-all-start = ((bf16[4,2,16384]{2,1,0:T(2,128)(2,1)}), bf16[4,2,16384]{2,1,0:T(2,128)(2,1)S(1)}, u32[]{:S(2)}, u32[]{:S(2)}) async-start(bf16[4,2,16384]{2,1,0:T(2,128)(2,1)} %reshape.1115), calls=%async_computation | async-start | bytes 524288 | tf_op jit(solution)/shard_map/all_to_all | solution.py:181
  284.2 16.2 collective-permute-start.1
  302.4 21.6 %collective-permute-start.1 = (bf16[2,2,256,256]{2,3,1,0:T(8,128)(2,1)}, bf16[2,2,256,256]{2,3,1,0:T(8,128)(2,1)S(1)}, u32[]{:S(2)}, u32[]{:S(2)}) collective-permute-start(bf16[2,2,256,256]{2,3,1,0:T(8,128)(2,1)} %get-tuple-element.1982), channel_id=1, source_target_pairs={{7,0},{0,1},{1,2},{2,3},{3,4},{4,5},{5,6},{6,7},{15,8},{8,9},{9,10... | collective-permute-start | bytes 1572872 | tf_op jit(solution)/shard_map/while/body/eval_jaxpr/ppermute | solution.py:16
  368.4 19.4 %collective-permute-start.1 = (bf16[2,2,256,256]{2,3,1,0:T(8,128)(2,1)}, bf16[2,2,256,256]{2,3,1,0:T(8,128)(2,1)S(1)}, u32[]{:S(2)}, u32[]{:S(2)}) collective-permute-start(bf16[2,2,256,256]{2,3,1,0:T(8,128)(2,1)} %get-tuple-element.1982), channel_id=1, source_target_pairs={{7,0},{0,1},{1,2},{2,3},{3,4},{4,5},{5,6},{6,7},{15,8},{8,9},{9,10... | collective-permute-start | bytes 1572872 | tf_op jit(solution)/shard_map/while/body/eval_jaxpr/ppermute | solution.py:16
  389.7 14.9 collective-permute-start.1
  455.3 309.7 %reduce-scatter.13.cloned.1.call-start = ((), (), s32[]{:S(2)}) async-start(), calls=%async_computation.20 | async-start | bytes 4325376 | tf_op jit(solution)/shard_map/reduce_scatter | solution.py:423
  458.2 314.9 %reduce-scatter.19.cloned.1.call-start = ((), (), s32[]{:S(2)}) async-start(), calls=%async_computation.23 | async-start | bytes 4325376
  476.0 19.0 %collective-permute-start.3 = (bf16[2,2,256,256]{2,3,1,0:T(8,128)(2,1)}, bf16[2,2,256,256]{2,3,1,0:T(8,128)(2,1)S(1)}, u32[]{:S(2)}, u32[]{:S(2)}) collective-permute-start(bf16[2,2,256,256]{2,3,1,0:T(8,128)(2,1)} %get-tuple-element.2047), channel_id=1, source_target_pairs={{7,0},{0,1},{1,2},{2,3},{3,4},{4,5},{5,6},{6,7},{15,8},{8,9},{9,10... | collective-permute-start | bytes 1572872 | tf_op jit(solution)/shard_map/while/body/eval_jaxpr/ppermute | solution.py:16
  497.0 18.9 %collective-permute-start.3 = (bf16[2,2,256,256]{2,3,1,0:T(8,128)(2,1)}, bf16[2,2,256,256]{2,3,1,0:T(8,128)(2,1)S(1)}, u32[]{:S(2)}, u32[]{:S(2)}) collective-permute-start(bf16[2,2,256,256]{2,3,1,0:T(8,128)(2,1)} %get-tuple-element.2047), channel_id=1, source_target_pairs={{7,0},{0,1},{1,2},{2,3},{3,4},{4,5},{5,6},{6,7},{15,8},{8,9},{9,10... | collective-permute-start | bytes 1572872 | tf_op jit(solution)/shard_map/while/body/eval_jaxpr/ppermute | solution.py:16
  517.9 17.9 %collective-permute-start.3 = (bf16[2,2,256,256]{2,3,1,0:T(8,128)(2,1)}, bf16[2,2,256,256]{2,3,1,0:T(8,128)(2,1)S(1)}, u32[]{:S(2)}, u32[]{:S(2)}) collective-permute-start(bf16[2,2,256,256]{2,3,1,0:T(8,128)(2,1)} %get-tuple-element.2047), channel_id=1, source_target_pairs={{7,0},{0,1},{1,2},{2,3},{3,4},{4,5},{5,6},{6,7},{15,8},{8,9},{9,10... | collective-permute-start | bytes 1572872 | tf_op jit(solution)/shard_map/while/body/eval_jaxpr/ppermute | solution.py:16
  537.7 18.9 %collective-permute-start.3 = (bf16[2,2,256,256]{2,3,1,0:T(8,128)(2,1)}, bf16[2,2,256,256]{2,3,1,0:T(8,128)(2,1)S(1)}, u32[]{:S(2)}, u32[]{:S(2)}) collective-permute-start(bf16[2,2,256,256]{2,3,1,0:T(8,128)(2,1)} %get-tuple-element.2047), channel_id=1, source_target_pairs={{7,0},{0,1},{1,2},{2,3},{3,4},{4,5},{5,6},{6,7},{15,8},{8,9},{9,10... | collective-permute-start | bytes 1572872 | tf_op jit(solution)/shard_map/while/body/eval_jaxpr/ppermute | solution.py:16
  558.5 18.2 %collective-permute-start.3 = (bf16[2,2,256,256]{2,3,1,0:T(8,128)(2,1)}, bf16[2,2,256,256]{2,3,1,0:T(8,128)(2,1)S(1)}, u32[]{:S(2)}, u32[]{:S(2)}) collective-permute-start(bf16[2,2,256,256]{2,3,1,0:T(8,128)(2,1)} %get-tuple-element.2047), channel_id=1, source_target_pairs={{7,0},{0,1},{1,2},{2,3},{3,4},{4,5},{5,6},{6,7},{15,8},{8,9},{9,10... | collective-permute-start | bytes 1572872 | tf_op jit(solution)/shard_map/while/body/eval_jaxpr/ppermute | solution.py:16
  578.7 17.7 collective-permute-start.3
  598.4 16.2 collective-permute-start.3
  634.5 281.7 %reduce-scatter.21.cloned.1.call-start = ((), (), s32[]{:S(2)}) async-start(), calls=%async_computation.24 | async-start | bytes 4325376
  665.5 392.3 %reduce-scatter.23.cloned.1.call-start = ((), (), s32[]{:S(2)}) async-start(), calls=%async_computation.25 | async-start | bytes 4325376
  684.8 732.0 %reduce-scatter.17.cloned.1.call-start = ((), (), s32[]{:S(2)}) async-start(), calls=%async_computation.22 | async-start | bytes 17301504 | tf_op jit(solution)/shard_map/reduce_scatter | solution.py:425
  696.8 1081.8 %reduce-scatter.15.cloned.1.call-start = ((), (), s32[]{:S(2)}) async-start(), calls=%async_computation.21 | async-start | bytes 17301504 | tf_op jit(solution)/shard_map/reduce_scatter | solution.py:424
  (69 other events, 725.2 us)
Sparse Core Ops, SparseCore 0:
  10.9 59.4 all-gather.11
  73.2 55.4 all-gather.7
  131.6 55.2 all-gather.9
  189.6 60.1 all-gather.13
  252.5 83.8 all-gather.15
  339.1 87.6 all-gather.17
  459.0 145.5 reduce-scatter.12
  634.6 138.4 reduce-scatter.18
  776.0 140.1 reduce-scatter.20
  918.9 138.9 reduce-scatter.22
  1060.7 356.0 reduce-scatter.16
  1419.5 359.0 reduce-scatter.14
where the time goes:
time: 1790 us
  waiting for transfers between devices  1340 us (75%)
  blocking collectives  176 us (10%)
  matrix products  110 us (6%)
  local copies, waits for them, and re-layouts  72.2 us (4%)
  other arithmetic  48.1 us (3%)
  starting transfers between devices  20.4 us (1%)
  between operations  18.6 us (1%)
    reduce_scatter x1, waiting for transfers between devices, per_device(): lax.psum_scatter(grad_mat_up, ('blk', 'heads'), scatter_dimension=0, tile...  362 us
    reduce_scatter x1, waiting for transfers between devices, per_device(): lax.psum_scatter(grad_mat_down, ('blk', 'heads'), scatter_dimension=0, ti...  359 us
    unnamed x15, waiting for transfers between devices  297 us
    ppermute x29, waiting for transfers between devices, passed_along(): return lax.ppermute(block, axis, route)  263 us
    unnamed x2, blocking collectives  81.5 us
    all_gather x1, blocking collectives, per_device(): lax.all_gather(params[9], ('blk', 'heads'), axis=0, tiled=True)  65.7 us
    all_gather x1, waiting for transfers between devices, per_device(): lax.all_gather(params[2], ('blk', 'heads'), axis=0, tiled=True)  44.7 us
    unnamed x139, local copies, waits for them, and re-layouts  42 us
  transfers between devices with their start and end apart: 46, of which 40 were waited for; matrix products, arithmetic and copies ran while one was open for 11% of the time, Pallas kernels for 0%

commit v1 on v0

v1 whole, which is shorter than its diff:
```python
import functools

import jax
import jax.numpy as jnp
from jax import lax
from jax.experimental import pallas as pl
from jax.experimental.pallas import tpu as pltpu
from jax.sharding import PartitionSpec as P

HEAD_DIM = 64
NORM_EPS = 1e-05
NEG_LARGE = -1e30
QUERY_ROWS = 256
BF16 = jnp.bfloat16
F32 = jnp.float32
ALL = ("blk", "heads")


def vmem_limit(length):
    return 8 * 1024 * 1024 + 6 * 1024 * length


def matmul(left, right):
    return jnp.dot(left, right, preferred_element_type=F32)


def matmul_tn(left, right):
    return lax.dot_general(left, right, (((0,), (0,)), ((), ())), preferred_element_type=F32)


def matmul_nt(left, right):
    return lax.dot_general(left, right, (((1,), (1,)), ((), ())), preferred_element_type=F32)


def swapped(block, axis, mask):
    count = lax.axis_size(axis)
    return lax.ppermute(block, axis, [(i, i ^ mask) for i in range(count)])


def gather_parts(block, axis):
    index = lax.axis_index(axis)
    every = lax.all_gather(block, axis, axis=0, tiled=False)
    return [
        lax.dynamic_index_in_dim(every, index ^ k, 0, False) for k in range(lax.axis_size(axis))
    ]


def scatter_parts(parts, axis):
    stacked = xor_order(jnp.stack(parts), 0, lax.axis_index(axis))
    return lax.psum_scatter(stacked, axis, scatter_dimension=0, tiled=False)


def xor_order(array, dim, index):
    pieces = [
        lax.dynamic_index_in_dim(array, index ^ k, dim, True) for k in range(array.shape[dim])
    ]
    return jnp.concatenate(pieces, axis=dim)


def gather_blk(block):
    return lax.all_gather(block, "blk", axis=0, tiled=False)


def scatter_blk(blocks):
    return lax.psum_scatter(blocks.astype(F32), "blk", scatter_dimension=0, tiled=False)


def layer_norm(resid, norm_gain, norm_bias):
    center = resid - jnp.mean(resid, axis=-1, keepdims=True)
    inv_std = lax.rsqrt(jnp.mean(center * center, axis=-1, keepdims=True) + NORM_EPS)
    normed = center * inv_std
    return (normed * norm_gain + norm_bias, normed, inv_std)


def norm_back(upstream, normed, inv_std, norm_gain):
    scaled = upstream * norm_gain
    return inv_std * (
        scaled
        - jnp.mean(scaled, axis=-1, keepdims=True)
        - normed * jnp.mean(scaled * normed, axis=-1, keepdims=True)
    )


def gelu_slope(hidden):
    cdf_part = 0.5 * (1.0 + lax.erf(hidden * 0.7071067811865476))
    pdf_part = jnp.exp(-0.5 * hidden * hidden) * 0.3989422804014327
    return cdf_part + hidden * pdf_part


def two_halves(values):
    high = lax.reduce_precision(values, 8, 7)
    return jnp.stack([high, values - high], axis=-1).astype(BF16)


def left_lanes(block):
    lane = lax.broadcasted_iota(jnp.int32, block.shape, 1)
    return jnp.where(lane < HEAD_DIM, block, 0.0)


def masked_scores(seg_key, seg_query, scores):
    width = scores.shape[1] // seg_key.shape[1]
    same = jnp.concatenate([seg_key] * width, axis=1) == seg_query
    return jnp.where(same, scores, NEG_LARGE)


def own_scores(seg_key, seg_query, scores):
    width = scores.shape[1] // seg_key.shape[1]
    same = jnp.concatenate([seg_key] * width, axis=1) == seg_query
    rows = lax.broadcasted_iota(jnp.int32, scores.shape, 0)
    columns = lax.broadcasted_iota(jnp.int32, scores.shape, 1)
    return jnp.where(same | (rows == columns), scores, NEG_LARGE)


def score_all(turn, seg_query, seg_key_ref, qkv_ref, query_t, scores):
    sources, rows = qkv_ref.shape[0], qkv_ref.shape[1] * 2 // 3
    per_source = rows // QUERY_ROWS
    query_now = query_t[turn]
    for b in range(sources):
        spot = slice(b * rows, (b + 1) * rows)
        scores[spot, :] = masked_scores(
            seg_key_ref[spot, :], seg_query, matmul(qkv_ref[b, 0:rows, :], query_now)
        )
    own = pl.ds(pl.multiple_of(turn * QUERY_ROWS, QUERY_ROWS), QUERY_ROWS)
    inner = pl.ds(pl.multiple_of(turn % per_source * QUERY_ROWS, QUERY_ROWS), QUERY_ROWS)
    own_pair = qkv_ref[turn // per_source, inner, :]
    scores[own, :] = own_scores(seg_key_ref[own, :], seg_query, matmul(own_pair, query_now))
    return own, own_pair


def turn_queries(b, turned, query_t):
    per_source = turned.shape[1] // QUERY_ROWS
    low = jnp.concatenate([jnp.zeros_like(turned[0:HEAD_DIM]), turned[0:HEAD_DIM]], axis=0)
    for t in range(per_source):
        spot = slice(t * QUERY_ROWS, (t + 1) * QUERY_ROWS)
        query_t[b * per_source + t] = low[:, spot].astype(BF16)


def attend_kernel(
    part_ref, seg_row_ref, seg_key_ref, qkv_ref, low_ref, attn_ref, lse_ref,
    query_t, values_t, scores,
):
    step = pl.program_id(0)
    sources, rows = qkv_ref.shape[0], qkv_ref.shape[1] * 2 // 3
    half = rows // 2

    @pl.when(step == 0)
    def _():
        for b in range(sources):
            turn_queries(b, qkv_ref[b, 0:rows, :].astype(F32).T, query_t)
            turned = qkv_ref[b, rows : rows + half, :].astype(F32).T
            values_t[:, b * rows : b * rows + half] = turned[0:HEAD_DIM].astype(BF16)
            values_t[:, b * rows + half : (b + 1) * rows] = turned[
                HEAD_DIM : 2 * HEAD_DIM
            ].astype(BF16)

    turn = part_ref[0] + step
    score_all(turn, seg_row_ref[0], seg_key_ref, qkv_ref, query_t, scores)
    top = jnp.max(scores[...], axis=0, keepdims=True)
    total = jnp.zeros_like(top)
    result = jnp.zeros((HEAD_DIM, QUERY_ROWS), F32)
    for b in range(sources):
        spot = slice(b * rows, (b + 1) * rows)
        probs = jnp.exp(scores[spot, :] - top)
        total = total + jnp.sum(probs, axis=0, keepdims=True)
        result = result + matmul(values_t[:, spot], probs.astype(BF16))
    result = result / total
    attn_ref[...] = result
    lse_ref[0] = top + jnp.log(total)
    turned = result.T
    wide = low_ref.shape[1]
    for t in range(low_ref.shape[0]):
        left = turned[2 * t * wide : (2 * t + 1) * wide]
        right = turned[(2 * t + 1) * wide : (2 * t + 2) * wide]
        low_ref[t] = jnp.concatenate([left, right], axis=1).astype(BF16)


def attend(part, seg_row, seg_key, qkv, wide, query_length):
    sources, rows = qkv.shape[0], qkv.shape[1] * 2 // 3
    length = sources * rows
    steps = query_length // QUERY_ROWS
    blocks = QUERY_ROWS // (2 * wide)
    return pl.pallas_call(
        attend_kernel,
        grid_spec=pltpu.PrefetchScalarGridSpec(
            num_scalar_prefetch=1,
            grid=(steps,),
            in_specs=[
                pl.BlockSpec((1, 1, QUERY_ROWS), lambda i, part: (part[0] + i, 0, 0)),
                pl.BlockSpec(seg_key.shape, lambda i, part: (0, 0)),
                pl.BlockSpec(qkv.shape, lambda i, part: (0, 0, 0)),
            ],
            out_specs=[
                pl.BlockSpec((blocks, wide, 128), lambda i, part: (i, 0, 0)),
                pl.BlockSpec((HEAD_DIM, QUERY_ROWS), lambda i, part: (0, i)),
                pl.BlockSpec((1, 1, QUERY_ROWS), lambda i, part: (i, 0, 0)),
            ],
            scratch_shapes=[
                pltpu.VMEM((length // QUERY_ROWS, 128, QUERY_ROWS), BF16),
                pltpu.VMEM((HEAD_DIM, length), BF16),
                pltpu.VMEM((length, QUERY_ROWS), F32),
            ],
        ),
        out_shape=[
            jax.ShapeDtypeStruct((steps * blocks, wide, 128), BF16),
            jax.ShapeDtypeStruct((HEAD_DIM, query_length), F32),
            jax.ShapeDtypeStruct((steps, 1, QUERY_ROWS), F32),
        ],
        compiler_params=pltpu.CompilerParams(vmem_limit_bytes=vmem_limit(length)),
    )(part, seg_row, seg_key, qkv)


def attend_back_kernel(
    part_ref, seg_row_ref, seg_key_ref, qkv_ref, up_ref, attn_ref, lse_ref, grads_ref,
    query_t, keys_t, values, scores, grad_query, grad_key, grad_value,
):
    step = pl.program_id(0)
    sources, rows = qkv_ref.shape[0], qkv_ref.shape[1] * 2 // 3
    half = rows // 2
    lane = lax.broadcasted_iota(jnp.int32, (rows, 128), 1)

    @pl.when(step == 0)
    def _():
        for b in range(sources):
            turned = qkv_ref[b, 0:rows, :].astype(F32).T
            turn_queries(b, turned, query_t)
            keys_t[:, b * rows : (b + 1) * rows] = turned[HEAD_DIM : 2 * HEAD_DIM].astype(BF16)
            packed = qkv_ref[b, rows : rows + half, :].astype(F32)
            values[b * rows : b * rows + half, :] = left_lanes(packed).astype(BF16)
            values[b * rows + half : (b + 1) * rows, :] = left_lanes(
                pltpu.roll(packed, HEAD_DIM, 1)
            ).astype(BF16)
        grad_query[...] = jnp.zeros_like(grad_query)
        grad_key[...] = jnp.zeros_like(grad_key)
        grad_value[...] = jnp.zeros_like(grad_value)

    turn = part_ref[0] + step
    lse = lse_ref[0]
    pieces = []
    for t in range(up_ref.shape[0]):
        packed = up_ref[t].astype(F32)
        pieces.append(left_lanes(packed))
        pieces.append(left_lanes(pltpu.roll(packed, HEAD_DIM, 1)))
    up_now = jnp.concatenate(pieces, axis=0)
    up_turned = up_now.T
    delta = jnp.sum(up_turned[0:HEAD_DIM] * attn_ref[...], axis=0, keepdims=True)
    up_now = up_now.astype(BF16)
    up_turned = up_turned.astype(BF16)
    own, own_pair = score_all(turn, seg_row_ref[0], seg_key_ref, qkv_ref, query_t, scores)
    query_now = pltpu.roll(own_pair.astype(F32), HEAD_DIM, 1).astype(BF16)
    result = jnp.zeros((HEAD_DIM, QUERY_ROWS), F32)
    for b in range(sources):
        spot = slice(b * rows, (b + 1) * rows)
        probs = jnp.exp(scores[spot, :] - lse)
        grad_probs = matmul(values[spot, :], up_turned)
        grad_scores = (probs * (grad_probs - delta)).astype(BF16)
        grad_value[spot, :] += matmul(probs.astype(BF16), up_now)
        grad_key[spot, :] += matmul(grad_scores, query_now)
        result = result + matmul(keys_t[:, spot], grad_scores)
    grad_query[own, :] = jnp.concatenate([result, jnp.zeros_like(result)], axis=0).T

    @pl.when(step == pl.num_programs(0) - 1)
    def _():
        for b in range(sources):
            spot = slice(b * rows, (b + 1) * rows)
            grads_ref[b, 0:rows, :] = jnp.where(
                lane < HEAD_DIM, grad_query[spot, :], grad_key[spot, :]
            ).astype(BF16)
            upper = grad_value[b * rows : b * rows + half, :]
            lower = grad_value[b * rows + half : (b + 1) * rows, :]
            grads_ref[b, rows : rows + half, :] = (
                upper + pltpu.roll(lower, HEAD_DIM, 1)
            ).astype(BF16)


def attend_back(part, seg_row, seg_key, qkv, upstream, attn_t, lse):
    sources, rows = qkv.shape[0], qkv.shape[1] * 2 // 3
    length = sources * rows
    steps = lse.shape[0]
    wide = upstream.shape[1]
    blocks = QUERY_ROWS // (2 * wide)
    return pl.pallas_call(
        attend_back_kernel,
        grid_spec=pltpu.PrefetchScalarGridSpec(
            num_scalar_prefetch=1,
            grid=(steps,),
            in_specs=[
                pl.BlockSpec((1, 1, QUERY_ROWS), lambda i, part: (part[0] + i, 0, 0)),
                pl.BlockSpec(seg_key.shape, lambda i, part: (0, 0)),
                pl.BlockSpec(qkv.shape, lambda i, part: (0, 0, 0)),
                pl.BlockSpec((blocks, wide, 128), lambda i, part: (part[0] + i, 0, 0)),
                pl.BlockSpec((HEAD_DIM, QUERY_ROWS), lambda i, part: (0, i)),
                pl.BlockSpec((1, 1, QUERY_ROWS), lambda i, part: (i, 0, 0)),
            ],
            out_specs=pl.BlockSpec(qkv.shape, lambda i, part: (0, 0, 0)),
            scratch_shapes=[
                pltpu.VMEM((length // QUERY_ROWS, 128, QUERY_ROWS), BF16),
                pltpu.VMEM((HEAD_DIM, length), BF16),
                pltpu.VMEM((length, 128), BF16),
                pltpu.VMEM((length, QUERY_ROWS), F32),
                pltpu.VMEM((length, 128), F32),
                pltpu.VMEM((length, 128), F32),
                pltpu.VMEM((length, 128), F32),
            ],
        ),
        out_shape=jax.ShapeDtypeStruct(qkv.shape, BF16),
        compiler_params=pltpu.CompilerParams(vmem_limit_bytes=vmem_limit(length)),
    )(part, seg_row, seg_key, qkv, upstream, attn_t, lse)


def per_device(
    tokens,
    cotangent,
    doc_offsets,
    valid_flags,
    w_query,
    w_key,
    w_value,
    w_out,
    w_fc1,
    w_fc2,
    b_query,
    b_value,
    b_out,
    b_fc1,
    b_fc2,
    gain_attn,
    bias_attn,
    gain_ffn,
    bias_ffn,
):
    seqs, span, width = tokens.shape
    groups = lax.axis_size("heads")
    blocks = lax.axis_size("blk")
    devices = groups * blocks
    my_group = lax.axis_index("heads")
    my_block = lax.axis_index("blk")
    rows = seqs * span
    block_rows = span * groups
    length = block_rows * blocks
    heads = width // HEAD_DIM
    heads_here = heads // groups
    pairs = seqs * heads_here
    repeats = blocks // pairs
    parts_length = length // repeats
    width_here = heads_here * HEAD_DIM
    dim_rows = w_query.shape[0]
    unit_rows = w_fc2.shape[0]
    hidden_size = w_fc1.shape[1]
    units_here = hidden_size // groups
    qk_scale = HEAD_DIM ** (-0.5)
    half = block_rows // 2
    wide = span // 2

    w_three = jnp.concatenate(
        [w.reshape(dim_rows, groups, width_here) for w in (w_query, w_key, w_value)], axis=-1
    )
    w_three = jnp.transpose(w_three, (1, 0, 2))
    vectors = jnp.stack(
        [b_query, b_value, b_out, b_fc2, gain_attn, bias_attn, gain_ffn, bias_ffn], axis=1
    )
    vectors = jnp.concatenate([vectors, b_fc1.reshape(dim_rows, unit_rows // dim_rows)], axis=1)
    vector_count = vectors.shape[1]
    vectors = jnp.pad(vectors, ((0, 0), (0, 128 - vector_count)))
    first = jnp.concatenate(
        [w_three, jnp.broadcast_to(vectors[None], (groups,) + vectors.shape)], axis=-1
    )
    first = lax.all_to_all(first, "heads", split_axis=0, concat_axis=0, tiled=True)
    first = gather_blk(first.reshape(groups * dim_rows, first.shape[-1]))
    first = first.reshape(width, first.shape[-1])
    mat_three = first[:, : 3 * width_here]
    vectors = first[:, 3 * width_here : 3 * width_here + vector_count]
    (vec_query, vec_value, vec_out, vec_down, gain_one, bias_one, gain_two, bias_two) = [
        vectors[:, i].astype(F32) for i in range(8)
    ]
    vec_up = vectors[:, 8:].reshape(blocks, groups, unit_rows)
    vec_up = lax.dynamic_index_in_dim(vec_up, my_group, 1, False).reshape(units_here).astype(F32)
    w_up = w_fc1.reshape(dim_rows, blocks, groups, unit_rows)
    w_up = jnp.transpose(w_up, (2, 0, 1, 3)).reshape(groups, dim_rows, units_here)
    second = jnp.concatenate(
        [w_up, jnp.broadcast_to(w_out[None], (groups,) + w_out.shape)], axis=-1
    )
    second = lax.all_to_all(second, "heads", split_axis=0, concat_axis=0, tiled=True)
    second = lax.all_gather(
        second.reshape(groups * dim_rows, second.shape[-1]), "blk", axis=0, tiled=True
    )
    mat_up = second[:, :units_here]
    mat_out = second[:, units_here:]
    mat_down = lax.all_gather(w_fc2, "blk", axis=0, tiled=True)

    token_rows = tokens.reshape(rows, width)
    token_parts = gather_parts(token_rows, "heads")
    token_all = jnp.stack([part.reshape(tokens.shape) for part in token_parts], axis=1)
    token_all = token_all.reshape(seqs * block_rows, width)
    projected = matmul(token_all, mat_three)
    group_query = lax.dynamic_slice_in_dim(vec_query, my_group * width_here, width_here)
    group_value = lax.dynamic_slice_in_dim(vec_value, my_group * width_here, width_here)
    head_shape = (seqs, block_rows, heads_here, HEAD_DIM)
    query_tok = ((projected[:, :width_here] + group_query) * qk_scale).astype(BF16)
    key_tok = projected[:, width_here : 2 * width_here].astype(BF16)
    pair_tok = jnp.concatenate([query_tok.reshape(head_shape), key_tok.reshape(head_shape)], axis=3)
    pair_tok = jnp.transpose(pair_tok, (0, 2, 1, 3))
    value_tok = (projected[:, 2 * width_here :] + group_value).astype(BF16)
    value_tok = value_tok.reshape(seqs, 2, half, heads_here, HEAD_DIM)
    value_tok = jnp.transpose(value_tok, (0, 3, 2, 1, 4))
    value_tok = value_tok.reshape(seqs, heads_here, half, 2 * HEAD_DIM)
    sent = jnp.concatenate([pair_tok, value_tok], axis=2)
    sent = sent.reshape(pairs, 1, block_rows + half, 2 * HEAD_DIM)
    sent = jnp.broadcast_to(sent, (pairs, repeats) + sent.shape[2:])
    sent = sent.reshape(blocks, block_rows + half, 2 * HEAD_DIM)
    qkv = lax.all_to_all(sent, "blk", split_axis=0, concat_axis=0, tiled=True)

    my_pair = my_block // repeats
    my_part = my_block % repeats
    my_seq = my_pair // heads_here
    inner = jnp.arange(length, dtype=jnp.int32)
    place = (inner // block_rows) * block_rows + inner % span
    place = place + (((inner // span) % groups) ^ my_group) * span
    offsets = lax.dynamic_index_in_dim(doc_offsets, my_seq, 0, False)
    flags = lax.dynamic_index_in_dim(valid_flags, my_seq, 0, False)
    flags = xor_order(flags.reshape(blocks, groups, span), 1, my_group).reshape(length)
    segment = jnp.sum((offsets[None, :] <= place[:, None]).astype(jnp.int32), axis=1) - 1
    seg_row = segment.reshape(length // QUERY_ROWS, 1, QUERY_ROWS)
    seg_key = jnp.where(flags > 0, segment, -1)
    seg_key = jnp.broadcast_to(seg_key[:, None], (length, 128))
    first_turn = (my_part * (parts_length // QUERY_ROWS)).reshape(1).astype(jnp.int32)
    attn_low, attn_t, lse = attend(first_turn, seg_row, seg_key, qkv, wide, parts_length)

    part_blocks = blocks // repeats
    sent = attn_low.reshape(part_blocks, groups, wide, 2 * HEAD_DIM)
    sent = xor_order(sent, 1, my_group)
    sent = jnp.broadcast_to(sent[None], (repeats,) + sent.shape)
    sent = sent.reshape(devices, wide, 2 * HEAD_DIM)
    got = lax.all_to_all(sent, ALL, split_axis=0, concat_axis=0, tiled=True)
    got = got.reshape(seqs, heads_here, repeats, groups, wide, 2, HEAD_DIM)
    got = lax.dynamic_index_in_dim(got, my_block // part_blocks, 2, False)
    attn_tok = jnp.transpose(got, (0, 4, 3, 2, 1, 5)).reshape(rows, width)

    resid_in = token_rows.astype(F32)
    branch = matmul(attn_tok, mat_out) + vec_out
    normed_one, unit_one, inv_one = layer_norm(resid_in + branch, gain_one, bias_one)
    normed_low = normed_one.astype(BF16)
    normed_all = jnp.concatenate(gather_parts(normed_low, "heads"), axis=0)
    hidden = matmul(normed_all, mat_up) + vec_up
    act_low = jax.nn.gelu(hidden, approximate=False).astype(BF16)
    ffn_all = matmul(act_low, mat_down)
    ffn = scatter_parts(jnp.split(ffn_all, groups), "heads") + vec_down
    normed_two, unit_two, inv_two = layer_norm(normed_one + ffn, gain_two, bias_two)
    output = normed_two.astype(BF16).reshape(tokens.shape)
    my_span = my_block * groups + my_group
    local_flags = lax.dynamic_slice_in_dim(valid_flags, my_span * span, span, 1)
    local_flags = local_flags.reshape(rows).astype(F32)
    squares = jnp.stack(
        [
            jnp.sum(local_flags * jnp.sum(item * item, axis=1))
            for item in (resid_in, branch, normed_one, ffn)
        ]
    )

    upstream = cotangent.reshape(rows, width).astype(F32)
    grad_gain_two = jnp.sum(upstream * unit_two, axis=0)
    grad_bias_two = jnp.sum(upstream, axis=0)
    grad_resid_two = norm_back(upstream, unit_two, inv_two, gain_two)
    grad_ffn = grad_resid_two.astype(BF16)
    grad_vec_down = jnp.sum(grad_ffn.astype(F32), axis=0)
    grad_ffn_all = jnp.concatenate(gather_parts(grad_ffn, "heads"), axis=0)
    grad_hidden = (matmul_nt(grad_ffn_all, mat_down) * gelu_slope(hidden)).astype(BF16)
    grad_vec_up = jnp.sum(grad_hidden.astype(F32), axis=0)
    grad_normed_all = matmul_nt(grad_hidden, mat_up)
    grad_normed_one = grad_resid_two + scatter_parts(jnp.split(grad_normed_all, groups), "heads")
    grad_mat_down = matmul_tn(act_low, grad_ffn_all).astype(BF16)
    grad_mat_up = matmul_tn(normed_all, grad_hidden).astype(BF16)
    ffn_grads = jnp.concatenate(
        [
            grad_mat_down.reshape(blocks, unit_rows, width),
            grad_mat_up.reshape(blocks, -1, width),
        ],
        axis=1,
    )
    ffn_grads = lax.psum_scatter(
        ffn_grads.reshape(-1, width), "blk", scatter_dimension=0, tiled=True
    )
    shard_down = ffn_grads[:unit_rows].astype(F32)
    shard_up = lax.all_to_all(
        ffn_grads[unit_rows:].reshape(groups, dim_rows, units_here),
        "heads",
        split_axis=0,
        concat_axis=0,
        tiled=True,
    )
    shard_up = jnp.transpose(
        shard_up.reshape(groups, dim_rows, blocks, unit_rows), (1, 2, 0, 3)
    ).reshape(dim_rows, hidden_size)
    shard_up = shard_up.astype(F32)

    grad_gain_one = jnp.sum(grad_normed_one * unit_one, axis=0)
    grad_bias_one = jnp.sum(grad_normed_one, axis=0)
    grad_resid_one = norm_back(grad_normed_one, unit_one, inv_one, gain_one)
    grad_branch = grad_resid_one.astype(BF16)
    grad_vec_out = jnp.sum(grad_branch.astype(F32), axis=0)
    grad_attn = matmul_nt(grad_branch, mat_out).astype(BF16)

    sent = grad_attn.reshape(seqs, 2, wide, groups, heads_here, HEAD_DIM)
    sent = jnp.transpose(sent, (0, 4, 3, 2, 1, 5))
    sent = sent.reshape(pairs, 1, groups, wide, 2 * HEAD_DIM)
    sent = jnp.broadcast_to(sent, (pairs, repeats) + sent.shape[2:])
    sent = sent.reshape(devices, wide, 2 * HEAD_DIM)
    small = jnp.stack(
        [grad_vec_out, grad_vec_down, grad_gain_one, grad_bias_one, grad_gain_two, grad_bias_two]
    )
    small = jnp.transpose(small.reshape(6, devices, dim_rows), (1, 0, 2)).reshape(devices, -1)
    up_sums = jnp.zeros((blocks, groups, unit_rows), F32)
    up_sums = lax.dynamic_update_slice_in_dim(
        up_sums, grad_vec_up.reshape(blocks, 1, unit_rows), my_group, 1
    ).reshape(devices, unit_rows)
    small = jnp.concatenate(
        [small, up_sums, jnp.broadcast_to(squares[None], (devices, 4))], axis=1
    )
    small_count = small.shape[1]
    small = two_halves(small).reshape(devices, 2 * small_count)
    extra = 16 * (-(-2 * small_count // 2048))
    small = jnp.pad(small, ((0, 0), (0, extra * 128 - 2 * small_count)))
    sent = jnp.concatenate([sent, small.reshape(devices, extra, 128)], axis=1)
    got = lax.all_to_all(sent, ALL, split_axis=0, concat_axis=0, tiled=True)
    up_heads = got[:, :wide].reshape(blocks, groups, wide, 2 * HEAD_DIM)
    up_heads = xor_order(up_heads, 1, my_group).reshape(devices, wide, 2 * HEAD_DIM)
    small = jnp.sum(got[:, wide:].reshape(devices, extra * 128).astype(F32), axis=0)
    small = jnp.sum(small[: 2 * small_count].reshape(small_count, 2), axis=1)
    vector_sums = small[: 6 * dim_rows].reshape(6, dim_rows)
    shard_vec_up = small[6 * dim_rows : 6 * dim_rows + unit_rows]
    totals = small[6 * dim_rows + unit_rows :]
    real_count = jnp.maximum(jnp.sum(valid_flags.astype(F32)), 1.0)
    rms = jnp.sqrt(totals / (real_count * width))

    attn_columns = jnp.transpose(
        attn_tok.reshape(rows, blocks, groups, dim_rows), (2, 0, 1, 3)
    ).reshape(groups, rows, blocks * dim_rows)
    attn_columns = lax.all_to_all(
        attn_columns, "heads", split_axis=0, concat_axis=0, tiled=True
    )
    attn_columns = xor_order(attn_columns, 0, my_group)
    branch_parts = gather_parts(grad_branch, "heads")
    grad_mat_out = matmul_tn(
        attn_columns.reshape(groups * rows, blocks * dim_rows),
        jnp.concatenate(branch_parts, axis=0),
    ).astype(BF16)
    shard_out = scatter_blk(grad_mat_out.reshape(blocks, dim_rows, width))

    grads = attend_back(first_turn, seg_row, seg_key, qkv, up_heads, attn_t, lse)
    got = lax.all_to_all(grads, "blk", split_axis=0, concat_axis=0, tiled=True)
    got = got.reshape(pairs, repeats, block_rows + half, 2 * HEAD_DIM)
    got = jnp.sum(got.astype(F32), axis=1).astype(BF16) if repeats > 1 else got[:, 0]
    got = got.reshape(seqs, heads_here, block_rows + half, 2 * HEAD_DIM)
    grad_pair = got[:, :, :block_rows].reshape(seqs, heads_here, block_rows, 2, HEAD_DIM)
    grad_pair = jnp.transpose(grad_pair, (3, 0, 2, 1, 4))
    grad_pair = grad_pair.reshape(2, seqs * block_rows, width_here)
    grad_value = got[:, :, block_rows:].reshape(seqs, heads_here, half, 2, HEAD_DIM)
    grad_value = jnp.transpose(grad_value, (0, 3, 2, 1, 4)).reshape(seqs * block_rows, width_here)
    grad_query = grad_pair[0] * jnp.asarray(qk_scale, BF16)
    grad_three = jnp.concatenate([grad_query, grad_pair[1], grad_value], axis=1)
    grad_input = matmul_nt(grad_three, mat_three)
    grad_input = grad_input.reshape(seqs, groups, span, width)
    grad_input = scatter_parts([grad_input[:, k].reshape(rows, width) for k in range(groups)], "heads")
    grad_input = (grad_resid_one + grad_input).reshape(tokens.shape)
    grad_mat_three = matmul_tn(token_all, grad_three)
    sums = jnp.sum(grad_three.astype(F32), axis=0)
    query_sums = sums[:width_here]
    value_sums = sums[2 * width_here :]
    chunks = blocks // groups
    sums = jnp.concatenate(
        [
            query_sums.reshape(chunks, groups * dim_rows),
            value_sums.reshape(chunks, groups * dim_rows),
            jnp.zeros((chunks, 3 * width_here - 2 * groups * dim_rows), F32),
        ],
        axis=1,
    )
    sums = jnp.concatenate([sums] * groups, axis=0)
    is_owner = jnp.arange(blocks, dtype=jnp.int32) // chunks == my_group
    sums = jnp.where(is_owner[:, None], sums, 0.0)
    row = lax.broadcasted_iota(jnp.int32, (1, 16, 1), 1)
    sum_rows = jnp.where(row == 0, sums[:, None, :], 0.0)
    three_grads = jnp.concatenate(
        [grad_mat_three.reshape(blocks, groups * dim_rows, 3 * width_here), sum_rows], axis=1
    ).astype(BF16)
    three_grads = scatter_blk(three_grads)
    own_rows = three_grads[: groups * dim_rows].reshape(groups, dim_rows, 3 * width_here)
    own_sums = three_grads[groups * dim_rows, : 2 * groups * dim_rows]
    own_sums = jnp.transpose(own_sums.reshape(2, groups, dim_rows), (1, 0, 2))
    own_sums = jnp.concatenate(
        [
            own_sums.reshape(groups, 2 * dim_rows),
            jnp.zeros((groups, 3 * width_here - 2 * dim_rows), F32),
        ],
        axis=1,
    )
    own_sums = jnp.where(row == 0, own_sums[:, None, :], 0.0)
    own = jnp.concatenate([own_rows, own_sums], axis=1).astype(BF16)
    own = lax.all_to_all(own, "heads", split_axis=0, concat_axis=0, tiled=True).astype(F32)
    shard_sums = jnp.sum(own[:, dim_rows, : 2 * dim_rows], axis=0)
    shards_three = [
        jnp.transpose(
            own[:, :dim_rows, which * width_here : (which + 1) * width_here], (1, 0, 2)
        ).reshape(dim_rows, width)
        for which in range(3)
    ]

    return (
        output,
        grad_input,
        shards_three[0],
        shards_three[1],
        shards_three[2],
        shard_out,
        shard_up,
        shard_down,
        shard_sums[:dim_rows],
        shard_sums[dim_rows:],
        vector_sums[0],
        shard_vec_up,
        vector_sums[1],
        vector_sums[2],
        vector_sums[3],
        vector_sums[4],
        vector_sums[5],
        rms,
    )


def solution(mesh):
    token_spec = P(None, ALL, None)
    matrix_spec = P(ALL, None)
    vector_spec = P(ALL)
    return jax.shard_map(
        per_device,
        mesh=mesh,
        in_specs=(token_spec,) * 2 + (P(),) * 2 + (matrix_spec,) * 6 + (vector_spec,) * 9,
        out_specs=(token_spec,) * 2 + (matrix_spec,) * 6 + (vector_spec,) * 9 + (P(),),
        check_vma=False,
    )
```

time: 1790 us -> 568 us (0.32)
  waiting for transfers between devices: 1340 us -> 318 us
  blocking collectives: 176 us -> 47.3 us
  matrix products: 110 us -> 33.3 us
  Pallas kernels: 0 us -> 27.5 us
    reduce_scatter x3, waiting for transfers between devices: 721 us -> 37.4 us  [the longest x2 37.4 us: scatter_blk(): lax.psum_scatter(blocks.astype(F32), 'blk', scatter_dimension=0, tiled=Fa...]
    ppermute x29 -> x0, waiting for transfers between devices: 263 us -> none  [passed_along(): return lax.ppermute(block, axis, route)]
    unnamed x15 -> x16, waiting for transfers between devices: 297 us -> 98 us
    unnamed x2 -> x0, blocking collectives: 81.5 us -> none
    all_to_all x5 -> x6, waiting for transfers between devices: 12 us -> 88.5 us  [the longest x1 41.7 us: per_device(): qkv = lax.all_to_all(sent, 'blk', split_axis=0, concat_axis=0, tiled=True)]
    all_gather x1 -> x0, blocking collectives: 65.7 us -> none  [per_device(): lax.all_gather(params[9], ('blk', 'heads'), axis=0, tiled=True)]
    all_gather x6 -> x7, waiting for transfers between devices: 45.7 us -> 94.5 us  [the longest x4 48.6 us: gather_parts(): every = lax.all_gather(block, axis, axis=0, tiled=False)]
    dot_general x118 -> x4, matrix products: 64.2 us -> 16.5 us  [matmul(): return jnp.dot(left, right, preferred_element_type=F32)]
  transfers between devices with their start and end apart: 46 -> 19, of which waited for: 40 -> 14; matrix products, arithmetic and copies ran while one was open for 11% -> 17% of each run, Pallas kernels for 0% -> 5%
where the time goes in v1:
time: 568 us; the launch traced here: 559 us
  waiting for transfers between devices  318 us (56%)
  local copies, waits for them, and re-layouts  56.3 us (10%)
  blocking collectives  47.3 us (8%)
  other arithmetic  37.5 us (7%)
  matrix products  33.3 us (6%)
  Pallas kernels  27.5 us (5%)
  starting transfers between devices  22.3 us (4%)
  between operations  16.2 us (3%)
    unnamed x16, waiting for transfers between devices  98 us
    all_gather x4, waiting for transfers between devices, gather_parts(): every = lax.all_gather(block, axis, axis=0, tiled=False)  48.6 us
    all_to_all x1, waiting for transfers between devices, per_device(): qkv = lax.all_to_all(sent, 'blk', split_axis=0, concat_axis=0, tiled=True)  41.7 us
    reduce_scatter x2, waiting for transfers between devices, scatter_blk(): lax.psum_scatter(blocks.astype(F32), 'blk', scatter_dimension=0, tiled=Fa...  37.4 us
    all_to_all x1, waiting for transfers between devices, per_device(): got = lax.all_to_all(grads, 'blk', split_axis=0, concat_axis=0, tiled=True)  28.6 us
    all_gather x1, waiting for transfers between devices, gather_blk(): return lax.all_gather(block, 'blk', axis=0, tiled=False)  26.3 us
    all_to_all x1, blocking collectives, per_device(): got = lax.all_to_all(sent, ALL, split_axis=0, concat_axis=0, tiled=True)  20.2 us
    all_gather x1, waiting for transfers between devices, per_device(): mat_down = lax.all_gather(w_fc2, 'blk', axis=0, tiled=True)  19.7 us
  transfers between devices with their start and end apart: 19, of which 14 were waited for; matrix products, arithmetic and copies ran while one was open for 17% of the time, Pallas kernels for 5%

profile of v1, /device:TPU:0, one launch (start us, length us, event | category | flops | bytes accessed | tf_op | source)
XLA Modules:
  0.0 558.8 jit_solution(2806110152569447192)
XLA Ops:
  17.8 10.9 %all_to_all.45 = bf16[4,32,896]{2,1,0:T(8,128)(2,1)} all-to-all(bf16[4,32,896]{2,1,0:T(8,128)(2,1)S(1)} %copy.195), channel_id=1, replica_groups=mesh['heads'=4,'blk'=8] {'heads'}, dimensions={0} | all-to-all | bytes 458752 | tf_op jit(solution)/shard_map/all_to_all | solution.py:367
  29.2 16.2 %all_to_all.46 = bf16[4,32,2048]{2,1,0:T(8,128)(2,1)} all-to-all(bf16[4,32,2048]{2,1,0:T(8,128)(2,1)S(1)} %pad_maximum_fusion.11), channel_id=1, replica_groups=mesh['heads'=4,'blk'=8] {'heads'}, dimensions={0} | all-to-all | bytes 1048576 | tf_op jit(solution)/shard_map/all_to_all | solution.py:382
  47.0 26.3 %all-gather.13.cloned.1.call-done = bf16[8,128,896]{2,1,0:T(8,128)(2,1)} async-done(((bf16[1,128,896]{2,1,0:T(8,128)(2,1)}), bf16[8,128,896]{2,1,0:T(8,128)(2,1)}) %all-gather.13.cloned.1.call-update) | async-done | bytes 1835024 | tf_op jit(solution)/shard_map/all_gather | solution.py:61
  81.9 3.5 all-to-all-start.1
  85.9 41.7 %all-to-all-done.1.qkv_ref = bf16[8,384,128]{2,1,0:T(8,128)(2,1)S(1)} async-done(((bf16[8,384,128]{2,1,0:T(8,128)(2,1)}), bf16[8,384,128]{2,1,0:T(8,128)(2,1)S(1)}, u32[]{:S(2)}, u32[]{:S(2)}) %all-to-all-start.1) | async-done | bytes 786464 | tf_op jit(solution)/shard_map/all_to_all | solution.py:410
  128.0 10.8 %shard_map.322 = (bf16[32,32,128]{2,1,0:T(8,128)(2,1)S(1)}, f32[64,2048]{1,0:T(8,128)S(1)}, f32[8,1,256]{2,1,0:T(1,128)S(1)}) custom-call(s32[1]{0:T(128)} %constant.278.clone.1.part_ref, s32[8,1,256]{2,1,0:T(1,128)S(1)} %bitcast.220, s32[2048,128]{1,0:T(8,128)S(1)} %broadcast_in_dim.52.seg_key_ref, bf16[8,384,128]{2,1,0:T(8,128)(2,1)S(1)} %all-to-all-done.1.qkv_ref), custom_call_target="tpu_custom_call" | custom-call | tf_op jit(solution)/shard_map/pallas_call | solution.py:182
  144.3 9.1 %all-to-all-done.2 = bf16[32,32,128]{2,1,0:T(8,128)(2,1)S(1)} async-done(((bf16[32,32,128]{2,1,0:T(8,128)(2,1)}), bf16[32,32,128]{2,1,0:T(8,128)(2,1)S(1)}, u32[]{:S(2)}, u32[]{:S(2)}) %all-to-all-start.2) | async-done | bytes 262176 | tf_op jit(solution)/shard_map/all_to_all | solution.py:433
  161.8 22.0 %all-gather.19.cloned.1.call-done = bf16[512,1024]{1,0:T(8,128)(2,1)} async-done(((bf16[128,1024]{1,0:T(8,128)(2,1)}), bf16[512,1024]{1,0:T(8,128)(2,1)}) %all-gather.19.cloned.1.call-update) | async-done | bytes 1048592 | tf_op jit(solution)/shard_map/all_gather | solution.py:42
  186.1 8.7 %fusion.2 = (bf16[512,1024]{1,0:T(8,128)(2,1)}, f32[512,1024]{1,0:T(8,128)}) fusion(f32[1024]{0:T(1024)S(1)} %bitcast.285, bf16[1024,2048]{1,0:T(8,128)(2,1)} %all-gather.15.cloned.1.call-done, bf16[128,1024]{1,0:T(8,128)(2,1)S(1)} %get-tuple-element.91, bf16[128,1024]{1,0:T(8,128)(2,1)S(1)} %get-tuple-element.92, ...), kind=kOutput, calls=%fused_computation.5 | convolution fusion | flops 1112539136 | bytes 6295552 | tf_op jit(solution)/shard_map/dot_general | solution.py:24
  194.8 19.7 %all-gather.17.cloned.1.call-done = bf16[1024,1024]{1,0:T(8,128)(2,1)} async-done(((bf16[128,1024]{1,0:T(8,128)(2,1)}), bf16[1024,1024]{1,0:T(8,128)(2,1)}) %all-gather.17.cloned.1.call-update) | async-done | bytes 2097168 | tf_op jit(solution)/shard_map/all_gather | solution.py:388
  222.7 32.1 %reduce-scatter.19.cloned.1.call-done = f32[1,128,1024]{2,1,0:T(8,128)} async-done(((f32[4,128,1024]{2,1,0:T(8,128)}), f32[1,128,1024]{2,1,0:T(8,128)}) %reduce-scatter.19.cloned.1.call-update) | async-done | bytes 524304
  259.6 26.5 %all-gather.21.cloned.1.call-done = bf16[512,1024]{1,0:T(8,128)(2,1)} async-done(((bf16[128,1024]{1,0:T(8,128)(2,1)}), bf16[512,1024]{1,0:T(8,128)(2,1)}) %all-gather.21.cloned.1.call-update) | async-done | bytes 1048592 | tf_op jit(solution)/shard_map/all_gather | solution.py:42
  288.1 4.6 convert_reduce_fusion
  297.4 34.0 %reduce-scatter.21.cloned.1.call-done = f32[1,128,1024]{2,1,0:T(8,128)} async-done(((f32[4,128,1024]{2,1,0:T(8,128)}), f32[1,128,1024]{2,1,0:T(8,128)}) %reduce-scatter.21.cloned.1.call-update) | async-done | bytes 524304
  359.6 20.2 %all_to_all.47 = bf16[32,48,128]{2,1,0:T(8,128)(2,1)S(1)} all-to-all(bf16[32,48,128]{2,1,0:T(8,128)(2,1)S(1)} %pad_maximum_fusion.12), channel_id=1, replica_groups=mesh['heads'=4,'blk'=8] {'blk','heads'}, dimensions={0} | all-to-all | bytes 786432 | tf_op jit(solution)/shard_map/all_to_all | solution.py:523
  379.8 16.7 %shard_map.323 = bf16[8,384,128]{2,1,0:T(8,128)(2,1)} custom-call(s32[1]{0:T(128)} %constant.278.clone.1.part_ref, s32[8,1,256]{2,1,0:T(1,128)S(1)} %bitcast.221, s32[2048,128]{1,0:T(8,128)S(1)} %broadcast_in_dim.52.seg_key_ref, bf16[8,384,128]{2,1,0:T(8,128)(2,1)S(1)} %all-to-all-done.1.qkv_ref, bf16[32,32,128]{2,1,0:T(8,128)(2,1)S(1)} %bitcast.218, ...), custom_call_target="tpu_custom_call" | custom-call | tf_op jit(solution)/shard_map/pallas_call | solution.py:281
  396.5 4.5 all-to-all-start.5
  402.5 28.6 %all-to-all-done.5 = bf16[8,384,128]{2,1,0:T(8,128)(2,1)S(1)} async-done(((bf16[8,384,128]{2,1,0:T(8,128)(2,1)}), bf16[8,384,128]{2,1,0:T(8,128)(2,1)S(1)}, u32[]{:S(2)}, u32[]{:S(2)}) %all-to-all-start.5) | async-done | bytes 786464 | tf_op jit(solution)/shard_map/all_to_all | solution.py:549
  451.4 4.4 all-to-all-done.7
  466.7 4.7 all-to-all-done.8
  472.9 7.1 %reduce-scatter.13.cloned.1.call-done = f32[1,144,768]{2,1,0:T(8,128)} async-done(((f32[8,144,768]{2,1,0:T(8,128)}), f32[1,144,768]{2,1,0:T(8,128)}) %reduce-scatter.13.cloned.1.call-update) | async-done | bytes 442384 | tf_op jit(solution)/shard_map/reduce_scatter | solution.py:65
  482.8 3.6 all-to-all-start.6
  486.4 30.5 %reduce-scatter.23.cloned.1.call-done = f32[1,128,1024]{2,1,0:T(8,128)} async-done(((f32[4,128,1024]{2,1,0:T(8,128)}), f32[1,128,1024]{2,1,0:T(8,128)}) %reduce-scatter.23.cloned.1.call-update) | async-done | bytes 524304
  521.6 30.3 %reduce-scatter.15.cloned.1.call-done = f32[1,32,1024]{2,1,0:T(8,128)} async-done(((f32[8,32,1024]{2,1,0:T(8,128)}), f32[1,32,1024]{2,1,0:T(8,128)}) %reduce-scatter.15.cloned.1.call-update) | async-done | bytes 131088 | tf_op jit(solution)/shard_map/reduce_scatter | solution.py:65
  (300 shorter events, 125.9 us)
Async XLA Ops:
  7.2 78.6 %copy-start = (s32[2,16]{1,0:T(2,128)S(1)}, s32[2,16]{1,0:T(2,128)}, u32[]{:S(2)}) copy-start(s32[2,16]{1,0:T(2,128)} %param.21) | copy-start | bytes 388
  7.2 21.6 %copy-start.30 = (bf16[32,4096]{1,0:T(8,128)(2,1)S(1)}, bf16[32,4096]{1,0:T(8,128)(2,1)}, u32[]{:S(2)}) copy-start(bf16[32,4096]{1,0:T(8,128)(2,1)} %param.27) | copy-start | bytes 786436
  7.2 38.3 %all-gather.11.cloned.1.call-start = ((), (), s32[]{:S(2)}) async-start(), calls=%async_computation.15 | async-start | bytes 1310720 | tf_op jit(solution)/shard_map/all_gather | solution.py:42
  8.0 65.4 %all-gather.13.cloned.1.call-start = ((), (), s32[]{:S(2)}) async-start(), calls=%async_computation.16 | async-start | bytes 2064384 | tf_op jit(solution)/shard_map/all_gather | solution.py:61
  28.7 127.6 %all-gather.15.cloned.1.call-start = ((), (), s32[]{:S(2)}) async-start(), calls=%async_computation.17 | async-start | bytes 4718592 | tf_op jit(solution)/shard_map/all_gather | solution.py:383
  47.0 28.9 %copy-start.6 = (bf16[2,4,64,1024]{3,2,1,0:T(8,128)(2,1)}, bf16[2,4,64,1024]{3,2,1,0:T(8,128)(2,1)S(1)}, u32[]{:S(2)}) copy-start(bf16[2,4,64,1024]{3,2,1,0:T(8,128)(2,1)S(1)} %copy.186) | copy-start | bytes 3145732
  81.9 45.7 %all-to-all-start.1 = ((bf16[8,384,128]{2,1,0:T(8,128)(2,1)}), bf16[8,384,128]{2,1,0:T(8,128)(2,1)S(1)}, u32[]{:S(2)}, u32[]{:S(2)}) async-start(bf16[8,384,128]{2,1,0:T(8,128)(2,1)} %pad_maximum_fusion.10), calls=%async_computation.1 | async-start | bytes 1572864 | tf_op jit(solution)/shard_map/all_to_all | solution.py:410
  139.6 13.8 %all-to-all-start.2 = ((bf16[32,32,128]{2,1,0:T(8,128)(2,1)}), bf16[32,32,128]{2,1,0:T(8,128)(2,1)S(1)}, u32[]{:S(2)}, u32[]{:S(2)}) async-start(bf16[32,32,128]{2,1,0:T(8,128)(2,1)} %bitcast.25), calls=%async_computation.2 | async-start | bytes 524288 | tf_op jit(solution)/shard_map/all_to_all | solution.py:433
  142.4 41.4 %all-gather.19.cloned.1.call-start = ((), (), s32[]{:S(2)}) async-start(), calls=%async_computation.22 | async-start | bytes 1310720 | tf_op jit(solution)/shard_map/all_gather | solution.py:42
  159.6 54.8 %all-gather.17.cloned.1.call-start = ((), (), s32[]{:S(2)}) async-start(), calls=%async_computation.18 | async-start | bytes 2359296 | tf_op jit(solution)/shard_map/all_gather | solution.py:388
  160.2 94.5 %reduce-scatter.19.cloned.1.call-start = ((), (), s32[]{:S(2)}) async-start(), calls=%async_computation.25 | async-start | bytes 2621440
  219.9 66.3 %all-gather.21.cloned.1.call-start = ((), (), s32[]{:S(2)}) async-start(), calls=%async_computation.23 | async-start | bytes 1310720 | tf_op jit(solution)/shard_map/all_gather | solution.py:42
  259.3 72.1 %reduce-scatter.21.cloned.1.call-start = ((), (), s32[]{:S(2)}) async-start(), calls=%async_computation.26 | async-start | bytes 2621440
  296.1 160.4 %all-gather.23.cloned.1.call-start = ((), (), s32[]{:S(2)}) async-start(), calls=%async_computation.24 | async-start | bytes 1310720 | tf_op jit(solution)/shard_map/all_gather | solution.py:42
  335.5 125.2 %reduce-scatter.17.cloned.1.call-start = ((), (), s32[]{:S(2)}) async-start(), calls=%async_computation.21 | async-start | bytes 4718592 | tf_op jit(solution)/shard_map/reduce_scatter | solution.py:479
  396.5 34.6 %all-to-all-start.5 = ((bf16[8,384,128]{2,1,0:T(8,128)(2,1)}), bf16[8,384,128]{2,1,0:T(8,128)(2,1)S(1)}, u32[]{:S(2)}, u32[]{:S(2)}) async-start(bf16[8,384,128]{2,1,0:T(8,128)(2,1)} %shard_map.323), calls=%async_computation.5 | async-start | bytes 1572864 | tf_op jit(solution)/shard_map/all_to_all | solution.py:549
  401.0 79.0 %reduce-scatter.13.cloned.1.call-start = ((), (), s32[]{:S(2)}) async-start(), calls=%async_computation.19 | async-start | bytes 3981312 | tf_op jit(solution)/shard_map/reduce_scatter | solution.py:65
  437.7 79.2 %reduce-scatter.23.cloned.1.call-start = ((), (), s32[]{:S(2)}) async-start(), calls=%async_computation.27 | async-start | bytes 2621440
  446.7 9.1 %all-to-all-start.7 = ((bf16[4,128,256]{1,2,0:T(8,128)(2,1)}), bf16[4,128,256]{1,2,0:T(8,128)(2,1)S(1)}, u32[]{:S(2)}, u32[]{:S(2)}) async-start(bf16[4,128,256]{1,2,0:T(8,128)(2,1)} %bitcast.92), calls=%async_computation.8 | async-start | bytes 524288 | tf_op jit(solution)/shard_map/all_to_all | solution.py:537
  450.1 101.8 %reduce-scatter.15.cloned.1.call-start = ((), (), s32[]{:S(2)}) async-start(), calls=%async_computation.20 | async-start | bytes 1179648 | tf_op jit(solution)/shard_map/reduce_scatter | solution.py:65
  462.7 8.8 %all-to-all-start.8 = ((bf16[4,32,1024]{2,1,0:T(8,128)(2,1)}), bf16[4,32,1024]{2,1,0:T(8,128)(2,1)S(1)}, u32[]{:S(2)}, u32[]{:S(2)}) async-start(bf16[4,32,1024]{2,1,0:T(8,128)(2,1)} %bitcast.104), calls=%async_computation.11 | async-start | bytes 524288 | tf_op jit(solution)/shard_map/all_to_all | solution.py:483
  471.5 45.3 %copy-start.5 = (f32[128,1024]{1,0:T(8,128)S(1)}, f32[128,1024]{1,0:T(8,128)}, u32[]{:S(2)}) copy-start(f32[128,1024]{1,0:T(8,128)} %copy-done.4) | copy-start | bytes 1572868
  482.8 36.1 %all-to-all-start.6 = ((bf16[4,48,768]{2,1,0:T(8,128)(2,1)}), bf16[4,48,768]{2,1,0:T(8,128)(2,1)S(1)}, u32[]{:S(2)}, u32[]{:S(2)}) async-start(bf16[4,48,768]{2,1,0:T(8,128)(2,1)} %pad_maximum_fusion.13), calls=%async_computation.7 | async-start | bytes 589824 | tf_op jit(solution)/shard_map/all_to_all | solution.py:598
  486.4 65.4 %copy-start.1 = (s32[2,16]{1,0:T(2,128)S(1)}, s32[2,16]{1,0:T(2,128)}, u32[]{:S(2)}) copy-start(s32[2,16]{1,0:T(2,128)} %param.21) | copy-start | bytes 388
  (32 other events, 120.6 us)
Sparse Core Ops, SparseCore 0:
  9.9 34.8 all-gather.10
  46.4 26.9 all-gather.12
  75.0 63.3 all-gather.14
  159.7 24.0 all-gather.18
  185.3 29.0 all-gather.16
  220.0 34.6 reduce-scatter.18
  259.5 26.6 all-gather.20
  296.3 35.1 reduce-scatter.20
  335.6 26.6 all-gather.22
  364.5 59.3 reduce-scatter.16
  437.8 42.1 reduce-scatter.12
  483.1 33.7 reduce-scatter.22
  519.7 32.0 reduce-scatter.14

commit v2 on v1

--- a/solution.py
+++ b/solution.py
@@ -38,16 +38,14 @@
 
 
 def gather_parts(block, axis):
-    index = lax.axis_index(axis)
-    every = lax.all_gather(block, axis, axis=0, tiled=False)
-    return [
-        lax.dynamic_index_in_dim(every, index ^ k, 0, False) for k in range(lax.axis_size(axis))
-    ]
+    return [block] + [swapped(block, axis, k) for k in range(1, lax.axis_size(axis))]
 
 
 def scatter_parts(parts, axis):
-    stacked = xor_order(jnp.stack(parts), 0, lax.axis_index(axis))
-    return lax.psum_scatter(stacked, axis, scatter_dimension=0, tiled=False)
+    total = parts[0].astype(F32)
+    for k in range(1, len(parts)):
+        total = total + swapped(parts[k].astype(BF16), axis, k).astype(F32)
+    return total
 
 
 def xor_order(array, dim, index):
@@ -58,11 +56,25 @@
 
 
 def gather_blk(block):
-    return lax.all_gather(block, "blk", axis=0, tiled=False)
+    count = lax.axis_size("blk")
+    index = lax.axis_index("blk")
+    parts = [block] + [swapped(block, "blk", k) for k in range(2, count, 2)]
+    mine = jnp.stack(parts)
+    other = swapped(mine, "blk", 1)
+    both = jnp.stack([mine, other], axis=1).reshape((count,) + block.shape)
+    return xor_order(both, 0, index)
 
 
 def scatter_blk(blocks):
-    return lax.psum_scatter(blocks.astype(F32), "blk", scatter_dimension=0, tiled=False)
+    index = lax.axis_index("blk")
+    ordered = xor_order(blocks, 0, index)
+    pairs = ordered.reshape((ordered.shape[0] // 2, 2) + ordered.shape[1:])
+    total = pairs[:, 0].astype(F32) + swapped(pairs[:, 1], "blk", 1).astype(F32)
+    low = total.astype(BF16)
+    result = total[0]
+    for k in range(1, low.shape[0]):
+        result = result + swapped(low[k], "blk", 2 * k).astype(F32)
+    return result
 
 
 def layer_norm(resid, norm_gain, norm_bias):

time: 568 us -> 424 us (0.75)
  waiting for transfers between devices: 318 us -> 160 us
  starting transfers between devices: 22.3 us -> 63.9 us
  blocking collectives: 47.3 us -> 21.6 us
    ppermute x0 -> x33, waiting for transfers between devices: none -> 99.4 us  [swapped(): return lax.ppermute(block, axis, [(i, i ^ mask) for i in range(count)])]
    unnamed x16 -> x3, waiting for transfers between devices: 98 us -> 0.73 us
    all_gather x5 -> x0, waiting for transfers between devices: 74.9 us -> none  [the longest x4 48.6 us: gather_parts(): every = lax.all_gather(block, axis, axis=0, tiled=False)]
    ppermute x0 -> x33, starting transfers between devices: none -> 38.2 us  [swapped(): return lax.ppermute(block, axis, [(i, i ^ mask) for i in range(count)])]
    reduce_scatter x2 -> x0, waiting for transfers between devices: 37.4 us -> none  [scatter_blk(): lax.psum_scatter(blocks.astype(F32), 'blk', scatter_dimension=0, tiled=Fa...]
    all_to_all x1, waiting for transfers between devices: 28.6 us -> 0.01 us  [per_device(): got = lax.all_to_all(grads, 'blk', split_axis=0, concat_axis=0, tiled=True)]
    all_to_all x1 -> x0, blocking collectives: 20.2 us -> none  [per_device(): got = lax.all_to_all(sent, ALL, split_axis=0, concat_axis=0, tiled=True)]
    all_gather x1, waiting for transfers between devices: 19.7 us -> 0.01 us  [per_device(): mat_down = lax.all_gather(w_fc2, 'blk', axis=0, tiled=True)]
  transfers between devices with their start and end apart: 19 -> 43, of which waited for: 14 -> 24; matrix products, arithmetic and copies ran while one was open for 17% -> 25% of each run, Pallas kernels for 5% -> 7%
where the time goes in v2:
time: 424 us; the launch traced here: 416 us
  waiting for transfers between devices  160 us (38%)
  starting transfers between devices  63.9 us (15%)
  local copies, waits for them, and re-layouts  54.5 us (13%)
  other arithmetic  36.3 us (9%)
  matrix products  36 us (8%)
  Pallas kernels  27.4 us (6%)
  blocking collectives  21.6 us (5%)
  between operations  16.3 us (4%)
    ppermute x33, waiting for transfers between devices, swapped(): return lax.ppermute(block, axis, [(i, i ^ mask) for i in range(count)])  99.4 us
    ppermute x33, starting transfers between devices, swapped(): return lax.ppermute(block, axis, [(i, i ^ mask) for i in range(count)])  38.2 us
    all_to_all x1, waiting for transfers between devices, per_device(): qkv = lax.all_to_all(sent, 'blk', split_axis=0, concat_axis=0, tiled=True)  29.6 us
    all_to_all x2, waiting for transfers between devices, per_device(): got = lax.all_to_all(sent, ALL, split_axis=0, concat_axis=0, tiled=True)  21 us
    dot_general x4, matrix products, matmul(): return jnp.dot(left, right, preferred_element_type=F32)  16.8 us
    pallas_call x1, Pallas kernels, attend_back(): pl.pallas_call(attend_back_kernel, grid_spec=pltpu.PrefetchScalarGridSpec...  16.7 us
    all_to_all x1, blocking collectives, per_device(): lax.all_to_all(second, 'heads', split_axis=0, concat_axis=0, tiled=True)  13.6 us
    unnamed x108, local copies, waits for them, and re-layouts  11.6 us
  transfers between devices with their start and end apart: 43, of which 24 were waited for; matrix products, arithmetic and copies ran while one was open for 25% of the time, Pallas kernels for 7%

profile of v2, /device:TPU:0, one launch (start us, length us, event | category | flops | bytes accessed | tf_op | source)
XLA Modules:
  0.0 415.9 jit_solution(4009017428218448101)
XLA Ops:
  9.6 13.6 %all_to_all.45 = bf16[4,32,2048]{2,1,0:T(8,128)(2,1)} all-to-all(bf16[4,32,2048]{2,1,0:T(8,128)(2,1)S(1)} %pad_maximum_fusion.7), channel_id=1, replica_groups=mesh['heads'=4,'blk'=8] {'heads'}, dimensions={0} | all-to-all | bytes 1048576 | tf_op jit(solution)/shard_map/all_to_all | solution.py:394
  24.7 8.0 %all_to_all.46 = bf16[4,32,896]{2,1,0:T(8,128)(2,1)S(1)} all-to-all(bf16[4,32,896]{2,1,0:T(8,128)(2,1)S(1)} %copy.251), channel_id=1, replica_groups=mesh['heads'=4,'blk'=8] {'heads'}, dimensions={0} | all-to-all | bytes 458752 | tf_op jit(solution)/shard_map/all_to_all | solution.py:379
  37.1 10.8 %collective-permute-done.5 = bf16[128,896]{1,0:T(8,128)(2,1)S(1)} collective-permute-done((bf16[128,896]{1,0:T(8,128)(2,1)S(1)}, bf16[128,896]{1,0:T(8,128)(2,1)S(1)}, u32[]{:S(2)}, u32[]{:S(2)}) %collective-permute-start.5) | collective-permute-done | bytes 229408 | tf_op jit(solution)/shard_map/ppermute | solution.py:37
  47.9 29.4 %collective-permute-done.4 = bf16[128,896]{1,0:T(8,128)(2,1)S(1)} collective-permute-done((bf16[128,896]{1,0:T(8,128)(2,1)S(1)}, bf16[128,896]{1,0:T(8,128)(2,1)S(1)}, u32[]{:S(2)}, u32[]{:S(2)}) %collective-permute-start.4) | collective-permute-done | bytes 229408 | tf_op jit(solution)/shard_map/ppermute | solution.py:37
  81.1 5.2 %collective-permute-done.1 = bf16[128,1024]{1,0:T(8,128)(2,1)S(1)} collective-permute-done((bf16[128,1024]{1,0:T(8,128)(2,1)S(1)}, bf16[128,1024]{1,0:T(8,128)(2,1)S(1)}, u32[]{:S(2)}, u32[]{:S(2)}) %collective-permute-start.1) | collective-permute-done | bytes 262176 | tf_op jit(solution)/shard_map/ppermute | solution.py:37
  87.5 5.6 %collective-permute-done.2 = bf16[128,1024]{1,0:T(8,128)(2,1)} collective-permute-done((bf16[128,1024]{1,0:T(8,128)(2,1)S(1)}, bf16[128,1024]{1,0:T(8,128)(2,1)}, u32[]{:S(2)}, u32[]{:S(2)}) %collective-permute-start.2) | collective-permute-done | bytes 262176 | tf_op jit(solution)/shard_map/ppermute | solution.py:37
  102.4 4.8 %all-to-all-start.1 = ((bf16[8,384,128]{2,1,0:T(8,128)(2,1)}), bf16[8,384,128]{2,1,0:T(8,128)(2,1)S(1)}, u32[]{:S(2)}, u32[]{:S(2)}) async-start(bf16[8,384,128]{2,1,0:T(8,128)(2,1)} %pad_maximum_fusion.6), calls=%async_computation.1 | async-start | bytes 1572864 | tf_op jit(solution)/shard_map/all_to_all | solution.py:422
  108.4 29.6 %all-to-all-done.1.qkv_ref = bf16[8,384,128]{2,1,0:T(8,128)(2,1)S(1)} async-done(((bf16[8,384,128]{2,1,0:T(8,128)(2,1)}), bf16[8,384,128]{2,1,0:T(8,128)(2,1)S(1)}, u32[]{:S(2)}, u32[]{:S(2)}) %all-to-all-start.1) | async-done | bytes 786464 | tf_op jit(solution)/shard_map/all_to_all | solution.py:422
  138.3 10.8 %shard_map.322 = (bf16[32,32,128]{2,1,0:T(8,128)(2,1)S(1)}, f32[64,2048]{1,0:T(8,128)S(1)}, f32[8,1,256]{2,1,0:T(1,128)S(1)}) custom-call(s32[1]{0:T(128)} %constant.275.clone.1.part_ref, s32[8,1,256]{2,1,0:T(1,128)S(1)} %bitcast.229, s32[2048,128]{1,0:T(8,128)S(1)} %broadcast_in_dim.52.seg_key_ref, bf16[8,384,128]{2,1,0:T(8,128)(2,1)S(1)} %all-to-all-done.1.qkv_ref), custom_call_target="tpu_custom_call" | custom-call | tf_op jit(solution)/shard_map/pallas_call | solution.py:194
  154.7 9.0 %all-to-all-done.2 = bf16[32,32,128]{2,1,0:T(8,128)(2,1)S(1)} async-done(((bf16[32,32,128]{2,1,0:T(8,128)(2,1)}), bf16[32,32,128]{2,1,0:T(8,128)(2,1)S(1)}, u32[]{:S(2)}, u32[]{:S(2)}) %all-to-all-start.2) | async-done | bytes 262176 | tf_op jit(solution)/shard_map/all_to_all | solution.py:445
  184.2 9.0 %fusion.2 = (bf16[512,1024]{1,0:T(8,128)(2,1)}, f32[512,1024]{1,0:T(8,128)}) fusion(f32[1024]{0:T(1024)S(1)} %bitcast.313, bf16[1024,2048]{1,0:T(8,128)(2,1)} %all-gather.3.cloned.1.call-done, bf16[128,1024]{1,0:T(8,128)(2,1)} %collective-permute-done.9, bf16[128,1024]{1,0:T(8,128)(2,1)} %collective-permute-done.8, ...), kind=kOutput, calls=%fused_computation.13 | convolution fusion | flops 1112539136 | bytes 6295552 | tf_op jit(solution)/shard_map/dot_general | solution.py:24
  193.3 4.6 %fusion.128 = (bf16[512,1024]{1,0:T(8,128)(2,1)S(1)}, f32[512,1024]{1,0:T(8,128)}) fusion(bf16[512,1024]{1,0:T(8,128)(2,1)} %get-tuple-element.120, bf16[1024,1024]{1,0:T(8,128)(2,1)} %all-gather.5.cloned.1.call-done), kind=kOutput, calls=%fused_computation.314 | convolution fusion | flops 1074266112 | bytes 6291456 | tf_op jit(solution)/shard_map/dot_general | solution.py:24
  209.3 4.1 all-to-all-start.7
  233.2 4.6 %convert_reduce_fusion = (f32[1024]{0:T(1024)S(1)}, bf16[512,1024]{1,0:T(8,128)(2,1)S(1)}) fusion(f32[512,1024]{1,0:T(8,128)} %get-tuple-element.121, f32[1024]{0:T(1024)S(1)} %bitcast.314, bf16[1024,1024]{1,0:T(8,128)(2,1)} %all-gather.5.cloned.1.call-done, bf16[128,1024]{1,0:T(8,128)(2,1)} %collective-permute-done.15, ...), kind=kOutput, calls=%fused_computation.20 | convolution fusion | flops 1084750848 | bytes 6299648 | tf_op jit(solution)/shard_map/dot_general | solution.py:32
  252.4 4.1 collective-permute-done.18
  293.2 12.0 %all-to-all-done.4 = bf16[32,48,128]{2,1,0:T(8,128)(2,1)S(1)} async-done(((bf16[32,48,128]{2,1,0:T(8,128)(2,1)}), bf16[32,48,128]{2,1,0:T(8,128)(2,1)S(1)}, u32[]{:S(2)}, u32[]{:S(2)}) %all-to-all-start.4) | async-done | bytes 393248 | tf_op jit(solution)/shard_map/all_to_all | solution.py:535
  305.2 16.7 %shard_map.323 = bf16[8,384,128]{2,1,0:T(8,128)(2,1)} custom-call(s32[1]{0:T(128)} %constant.275.clone.1.part_ref, s32[8,1,256]{2,1,0:T(1,128)S(1)} %bitcast.230, s32[2048,128]{1,0:T(8,128)S(1)} %broadcast_in_dim.52.seg_key_ref, bf16[8,384,128]{2,1,0:T(8,128)(2,1)S(1)} %all-to-all-done.1.qkv_ref, bf16[32,32,128]{2,1,0:T(8,128)(2,1)S(1)} %bitcast.227, ...), custom_call_target="tpu_custom_call" | custom-call | tf_op jit(solution)/shard_map/pallas_call | solution.py:293
  336.5 4.6 %collective-permute-done.30 = bf16[32,1024]{1,0:T(8,128)(2,1)S(1)} collective-permute-done((bf16[32,1024]{1,0:T(8,128)(2,1)}, bf16[32,1024]{1,0:T(8,128)(2,1)S(1)}, u32[]{:S(2)}, u32[]{:S(2)}) %collective-permute-start.30) | collective-permute-done | bytes 65568 | tf_op jit(solution)/shard_map/ppermute | solution.py:37
  341.0 5.6 %collective-permute-done.32 = bf16[32,1024]{1,0:T(8,128)(2,1)S(1)} collective-permute-done((bf16[32,1024]{1,0:T(8,128)(2,1)}, bf16[32,1024]{1,0:T(8,128)(2,1)S(1)}, u32[]{:S(2)}, u32[]{:S(2)}) %collective-permute-start.32) | collective-permute-done | bytes 65568 | tf_op jit(solution)/shard_map/ppermute | solution.py:37
  346.6 5.5 %collective-permute-done.31 = bf16[32,1024]{1,0:T(8,128)(2,1)S(1)} collective-permute-done((bf16[32,1024]{1,0:T(8,128)(2,1)S(1)}, bf16[32,1024]{1,0:T(8,128)(2,1)S(1)}, u32[]{:S(2)}, u32[]{:S(2)}) %collective-permute-start.31) | collective-permute-done | bytes 65568 | tf_op jit(solution)/shard_map/ppermute | solution.py:37
  367.9 5.9 %collective-permute-done.23 = bf16[144,768]{1,0:T(8,128)(2,1)S(1)} collective-permute-done((bf16[144,768]{1,0:T(8,128)(2,1)S(1)}, bf16[144,768]{1,0:T(8,128)(2,1)S(1)}, u32[]{:S(2)}, u32[]{:S(2)}) %collective-permute-start.23) | collective-permute-done | bytes 221216 | tf_op jit(solution)/shard_map/ppermute | solution.py:37
  375.2 9.2 %collective-permute-done.24 = bf16[144,768]{1,0:T(8,128)(2,1)S(1)} collective-permute-done((bf16[144,768]{1,0:T(8,128)(2,1)S(1)}, bf16[144,768]{1,0:T(8,128)(2,1)S(1)}, u32[]{:S(2)}, u32[]{:S(2)}) %collective-permute-start.24) | collective-permute-done | bytes 221216 | tf_op jit(solution)/shard_map/ppermute | solution.py:37
  390.3 4.4 %all-to-all-done.6 = bf16[4,48,768]{2,1,0:T(8,128)(2,1)S(1)} async-done(((bf16[4,48,768]{2,1,0:T(8,128)(2,1)}), bf16[4,48,768]{2,1,0:T(8,128)(2,1)S(1)}, u32[]{:S(2)}, u32[]{:S(2)}) %all-to-all-start.6) | async-done | bytes 294944 | tf_op jit(solution)/shard_map/all_to_all | solution.py:610
  402.8 4.8 %all-to-all-done.8 = bf16[4,32,1024]{2,1,0:T(8,128)(2,1)S(1)} async-done(((bf16[4,32,1024]{2,1,0:T(8,128)(2,1)}), bf16[4,32,1024]{2,1,0:T(8,128)(2,1)S(1)}, u32[]{:S(2)}, u32[]{:S(2)}) %all-to-all-start.8) | async-done | bytes 262176 | tf_op jit(solution)/shard_map/all_to_all | solution.py:495
  (368 shorter events, 178.2 us)
Async XLA Ops:
  7.2 159.5 %all-gather.3.cloned.1.call-start = ((), (), s32[]{:S(2)}) async-start(), calls=%async_computation.10 | async-start | bytes 4718592 | tf_op jit(solution)/shard_map/all_gather | solution.py:395
  32.7 15.1 %collective-permute-start.5 = (bf16[128,896]{1,0:T(8,128)(2,1)S(1)}, bf16[128,896]{1,0:T(8,128)(2,1)S(1)}, u32[]{:S(2)}, u32[]{:S(2)}) collective-permute-start(bf16[128,896]{1,0:T(8,128)(2,1)S(1)} %bitcast.275), channel_id=1, source_target_pairs={{0,6},{1,7},{2,4},{3,5},{4,2},{5,3},{6,0},{7,1},{8,14},{9,15},{10,... | collective-permute-start | bytes 688136 | tf_op jit(solution)/shard_map/ppermute | solution.py:37
  36.3 40.9 %collective-permute-start.4 = (bf16[128,896]{1,0:T(8,128)(2,1)S(1)}, bf16[128,896]{1,0:T(8,128)(2,1)S(1)}, u32[]{:S(2)}, u32[]{:S(2)}) collective-permute-start(bf16[128,896]{1,0:T(8,128)(2,1)S(1)} %bitcast.276), channel_id=1, source_target_pairs={{0,4},{1,5},{2,6},{3,7},{4,0},{5,1},{6,2},{7,3},{8,12},{9,13},{10,... | collective-permute-start | bytes 688136 | tf_op jit(solution)/shard_map/ppermute | solution.py:37
  36.3 40.9 %collective-permute-start.3 = (bf16[128,896]{1,0:T(8,128)(2,1)S(1)}, bf16[128,896]{1,0:T(8,128)(2,1)S(1)}, u32[]{:S(2)}, u32[]{:S(2)}) collective-permute-start(bf16[128,896]{1,0:T(8,128)(2,1)S(1)} %bitcast.277), channel_id=1, source_target_pairs={{0,2},{1,3},{2,0},{3,1},{4,6},{5,7},{6,4},{7,5},{8,10},{9,11},{10,... | collective-permute-start | bytes 688136 | tf_op jit(solution)/shard_map/ppermute | solution.py:37
  77.5 16.9 %collective-permute-start.6 = (bf16[4,128,896]{2,1,0:T(8,128)(2,1)S(1)}, bf16[4,128,896]{2,1,0:T(8,128)(2,1)S(1)}, u32[]{:S(2)}, u32[]{:S(2)}) collective-permute-start(bf16[4,128,896]{2,1,0:T(8,128)(2,1)S(1)} %get-tuple-element.71), channel_id=1, source_target_pairs={{0,1},{1,0},{2,3},{3,2},{4,5},{5,4},{6,7},{7,6},{8,9},{9,8},{10,11... | collective-permute-start | bytes 2752520 | tf_op jit(solution)/shard_map/ppermute | solution.py:37
  78.9 14.3 %collective-permute-start.2 = (bf16[128,1024]{1,0:T(8,128)(2,1)S(1)}, bf16[128,1024]{1,0:T(8,128)(2,1)}, u32[]{:S(2)}, u32[]{:S(2)}) collective-permute-start(bf16[128,1024]{1,0:T(8,128)(2,1)S(1)} %bitcast.246), channel_id=1, source_target_pairs={{0,24},{8,16},{16,8},{24,0},{1,25},{9,17},{17,9},{25,1},{2,26},{10... | collective-permute-start | bytes 786440 | tf_op jit(solution)/shard_map/ppermute | solution.py:37
  102.4 35.6 %all-to-all-start.1 = ((bf16[8,384,128]{2,1,0:T(8,128)(2,1)}), bf16[8,384,128]{2,1,0:T(8,128)(2,1)S(1)}, u32[]{:S(2)}, u32[]{:S(2)}) async-start(bf16[8,384,128]{2,1,0:T(8,128)(2,1)} %pad_maximum_fusion.6), calls=%async_computation.1 | async-start | bytes 1572864 | tf_op jit(solution)/shard_map/all_to_all | solution.py:422
  107.2 86.1 %all-gather.5.cloned.1.call-start = ((), (), s32[]{:S(2)}) async-start(), calls=%async_computation.11 | async-start | bytes 2359296 | tf_op jit(solution)/shard_map/all_gather | solution.py:400
  198.8 14.9 %collective-permute-start.10 = (bf16[128,1024]{1,0:T(8,128)(2,1)}, bf16[128,1024]{1,0:T(8,128)(2,1)}, u32[]{:S(2)}, u32[]{:S(2)}) collective-permute-start(bf16[128,1024]{1,0:T(8,128)(2,1)} %get-tuple-element.67), channel_id=1, source_target_pairs={{0,8},{8,0},{16,24},{24,16},{1,9},{9,1},{17,25},{25,17},{2,10},{10... | collective-permute-start | bytes 786440 | tf_op jit(solution)/shard_map/ppermute | solution.py:37
  199.9 13.9 %collective-permute-start.12 = (bf16[128,1024]{1,0:T(8,128)(2,1)}, bf16[128,1024]{1,0:T(8,128)(2,1)}, u32[]{:S(2)}, u32[]{:S(2)}) collective-permute-start(bf16[128,1024]{1,0:T(8,128)(2,1)} %get-tuple-element.68), channel_id=1, source_target_pairs={{0,24},{8,16},{16,8},{24,0},{1,25},{9,17},{17,9},{25,1},{2,26},{10... | collective-permute-start | bytes 786440 | tf_op jit(solution)/shard_map/ppermute | solution.py:37
  209.3 15.8 %all-to-all-start.7 = ((bf16[4,128,256]{1,2,0:T(8,128)(2,1)}), bf16[4,128,256]{1,2,0:T(8,128)(2,1)}, u32[]{:S(2)}, u32[]{:S(2)}) async-start(bf16[4,128,256]{1,2,0:T(8,128)(2,1)} %bitcast.86), calls=%async_computation.7 | async-start | bytes 524288 | tf_op jit(solution)/shard_map/all_to_all | solution.py:549
  213.4 183.4 %reduce-scatter.2.cloned.1.call-start = ((), (), s32[]{:S(2)}) async-start(), calls=%async_computation.12 | async-start | bytes 4718592 | tf_op jit(solution)/shard_map/reduce_scatter | solution.py:491
  262.6 23.6 %collective-permute-start.28 = (bf16[128,1024]{1,0:T(8,128)(2,1)}, bf16[128,1024]{1,0:T(8,128)(2,1)}, u32[]{:S(2)}, u32[]{:S(2)}) collective-permute-start(bf16[128,1024]{1,0:T(8,128)(2,1)} %get-tuple-element.45), channel_id=1, source_target_pairs={{0,24},{8,16},{16,8},{24,0},{1,25},{9,17},{17,9},{25,1},{2,26},{10... | collective-permute-start | bytes 786440 | tf_op jit(solution)/shard_map/ppermute | solution.py:37
  264.1 22.1 %collective-permute-start.27 = (bf16[128,1024]{1,0:T(8,128)(2,1)}, bf16[128,1024]{1,0:T(8,128)(2,1)}, u32[]{:S(2)}, u32[]{:S(2)}) collective-permute-start(bf16[128,1024]{1,0:T(8,128)(2,1)} %get-tuple-element.45), channel_id=1, source_target_pairs={{0,16},{8,24},{16,0},{24,8},{1,17},{9,25},{17,1},{25,9},{2,18},{10... | collective-permute-start | bytes 786440 | tf_op jit(solution)/shard_map/ppermute | solution.py:37
  264.5 21.8 %collective-permute-start.26 = (bf16[128,1024]{1,0:T(8,128)(2,1)}, bf16[128,1024]{1,0:T(8,128)(2,1)}, u32[]{:S(2)}, u32[]{:S(2)}) collective-permute-start(bf16[128,1024]{1,0:T(8,128)(2,1)} %get-tuple-element.45), channel_id=1, source_target_pairs={{0,8},{8,0},{16,24},{24,16},{1,9},{9,1},{17,25},{25,17},{2,10},{10... | collective-permute-start | bytes 786440 | tf_op jit(solution)/shard_map/ppermute | solution.py:37
  283.3 21.8 %all-to-all-start.4 = ((bf16[32,48,128]{2,1,0:T(8,128)(2,1)}), bf16[32,48,128]{2,1,0:T(8,128)(2,1)S(1)}, u32[]{:S(2)}, u32[]{:S(2)}) async-start(bf16[32,48,128]{2,1,0:T(8,128)(2,1)} %pad_maximum_fusion.8), calls=%async_computation.4 | async-start | bytes 786432 | tf_op jit(solution)/shard_map/all_to_all | solution.py:535
  321.9 31.4 %all-to-all-start.5 = ((bf16[8,384,128]{2,1,0:T(8,128)(2,1)}), bf16[8,384,128]{2,1,0:T(8,128)(2,1)S(1)}, u32[]{:S(2)}, u32[]{:S(2)}) async-start(bf16[8,384,128]{2,1,0:T(8,128)(2,1)} %shard_map.323), calls=%async_computation.5 | async-start | bytes 1572864 | tf_op jit(solution)/shard_map/all_to_all | solution.py:561
  332.2 14.4 %collective-permute-start.32 = (bf16[32,1024]{1,0:T(8,128)(2,1)}, bf16[32,1024]{1,0:T(8,128)(2,1)S(1)}, u32[]{:S(2)}, u32[]{:S(2)}) collective-permute-start(bf16[32,1024]{1,0:T(8,128)(2,1)} %get-tuple-element.86), channel_id=1, source_target_pairs={{0,6},{1,7},{2,4},{3,5},{4,2},{5,3},{6,0},{7,1},{8,14},{9,15},{10,... | collective-permute-start | bytes 196616 | tf_op jit(solution)/shard_map/ppermute | solution.py:37
  334.6 17.5 %collective-permute-start.31 = (bf16[32,1024]{1,0:T(8,128)(2,1)S(1)}, bf16[32,1024]{1,0:T(8,128)(2,1)S(1)}, u32[]{:S(2)}, u32[]{:S(2)}) collective-permute-start(bf16[32,1024]{1,0:T(8,128)(2,1)S(1)} %get-tuple-element.87), channel_id=1, source_target_pairs={{0,4},{1,5},{2,6},{3,7},{4,0},{5,1},{6,2},{7,3},{8,12},{9,13},{10,... | collective-permute-start | bytes 196616 | tf_op jit(solution)/shard_map/ppermute | solution.py:37
  361.2 14.0 %collective-permute-start.25 = (bf16[144,768]{1,0:T(8,128)(2,1)S(1)}, bf16[144,768]{1,0:T(8,128)(2,1)S(1)}, u32[]{:S(2)}, u32[]{:S(2)}) collective-permute-start(bf16[144,768]{1,0:T(8,128)(2,1)S(1)} %get-tuple-element.73), channel_id=1, source_target_pairs={{0,6},{1,7},{2,4},{3,5},{4,2},{5,3},{6,0},{7,1},{8,14},{9,15},{10,... | collective-permute-start | bytes 663560 | tf_op jit(solution)/shard_map/ppermute | solution.py:37
  362.6 21.8 %collective-permute-start.24 = (bf16[144,768]{1,0:T(8,128)(2,1)S(1)}, bf16[144,768]{1,0:T(8,128)(2,1)S(1)}, u32[]{:S(2)}, u32[]{:S(2)}) collective-permute-start(bf16[144,768]{1,0:T(8,128)(2,1)S(1)} %get-tuple-element.74), channel_id=1, source_target_pairs={{0,4},{1,5},{2,6},{3,7},{4,0},{5,1},{6,2},{7,3},{8,12},{9,13},{10,... | collective-permute-start | bytes 663560 | tf_op jit(solution)/shard_map/ppermute | solution.py:37
  364.9 24.4 %collective-permute-start.21 = (bf16[128,1024]{1,0:T(8,128)(2,1)S(1)}, bf16[128,1024]{1,0:T(8,128)(2,1)S(1)}, u32[]{:S(2)}, u32[]{:S(2)}) collective-permute-start(bf16[128,1024]{1,0:T(8,128)(2,1)S(1)} %bitcast.297), channel_id=1, source_target_pairs={{0,24},{8,16},{16,8},{24,0},{1,25},{9,17},{17,9},{25,1},{2,26},{10... | collective-permute-start | bytes 786440 | tf_op jit(solution)/shard_map/ppermute | solution.py:37
  367.3 21.9 %collective-permute-start.19 = (bf16[128,1024]{1,0:T(8,128)(2,1)S(1)}, bf16[128,1024]{1,0:T(8,128)(2,1)S(1)}, u32[]{:S(2)}, u32[]{:S(2)}) collective-permute-start(bf16[128,1024]{1,0:T(8,128)(2,1)S(1)} %bitcast.296), channel_id=1, source_target_pairs={{0,8},{8,0},{16,24},{24,16},{1,9},{9,1},{17,25},{25,17},{2,10},{10... | collective-permute-start | bytes 786440 | tf_op jit(solution)/shard_map/ppermute | solution.py:37
  373.7 15.5 %collective-permute-start.20 = (bf16[128,1024]{1,0:T(8,128)(2,1)S(1)}, bf16[128,1024]{1,0:T(8,128)(2,1)S(1)}, u32[]{:S(2)}, u32[]{:S(2)}) collective-permute-start(bf16[128,1024]{1,0:T(8,128)(2,1)S(1)} %bitcast.295), channel_id=1, source_target_pairs={{0,16},{8,24},{16,0},{24,8},{1,17},{9,25},{17,1},{25,9},{2,18},{10... | collective-permute-start | bytes 786440 | tf_op jit(solution)/shard_map/ppermute | solution.py:37
  (61 other events, 995.3 us)
Sparse Core Ops, SparseCore 0:
  23.3 65.1 all-gather.2
  109.6 36.9 all-gather.4
  252.4 54.4 reduce-scatter.1

commit v3 on v2

v3 whole, which is shorter than its diff:
```python
import functools

import jax
import jax.numpy as jnp
from jax import lax
from jax.experimental import pallas as pl
from jax.experimental.pallas import tpu as pltpu
from jax.sharding import PartitionSpec as P

HEAD_DIM = 64
NORM_EPS = 1e-05
NEG_LARGE = -1e30
QUERY_ROWS = 256
BF16 = jnp.bfloat16
F32 = jnp.float32
ALL = ("blk", "heads")


def vmem_limit(length):
    return 8 * 1024 * 1024 + 6 * 1024 * length


def matmul(left, right):
    return jnp.dot(left, right, preferred_element_type=F32)


def matmul_tn(left, right):
    return lax.dot_general(left, right, (((0,), (0,)), ((), ())), preferred_element_type=F32)


def matmul_nt(left, right):
    return lax.dot_general(left, right, (((1,), (1,)), ((), ())), preferred_element_type=F32)


def after(block, other):
    spot = lax.slice(other, (0,) * other.ndim, (1,) * other.ndim).reshape(())
    return block + (spot * 0).astype(block.dtype)


def swapped(block, axis, mask):
    count = lax.axis_size(axis)
    return lax.ppermute(block, axis, [(i, i ^ mask) for i in range(count)])


def gather_parts(block, axis):
    return [block] + [swapped(block, axis, k) for k in range(1, lax.axis_size(axis))]


def scatter_parts(parts, axis):
    total = parts[0].astype(F32)
    for k in range(1, len(parts)):
        total = total + swapped(parts[k].astype(BF16), axis, k).astype(F32)
    return total


def xor_order(array, dim, index):
    pieces = [
        lax.dynamic_index_in_dim(array, index ^ k, dim, True) for k in range(array.shape[dim])
    ]
    return jnp.concatenate(pieces, axis=dim)


def gather_blk_parts(block, first_needs):
    count = lax.axis_size("blk")
    mine = jnp.stack([block] + [swapped(block, "blk", k) for k in range(2, count, 2)])
    mine = after(mine, first_needs)
    return mine, swapped(mine, "blk", 1)


def gather_blk(block, first_needs):
    mine, other = gather_blk_parts(block, first_needs)
    both = jnp.stack([mine, other], axis=1).reshape((-1,) + block.shape)
    return xor_order(both, 0, lax.axis_index("blk"))


def scatter_blk(blocks):
    index = lax.axis_index("blk")
    ordered = xor_order(blocks, 0, index)
    pairs = ordered.reshape((ordered.shape[0] // 2, 2) + ordered.shape[1:])
    total = pairs[:, 0].astype(F32) + swapped(pairs[:, 1], "blk", 1).astype(F32)
    low = total.astype(BF16)
    result = total[0]
    for k in range(1, low.shape[0]):
        result = result + swapped(low[k], "blk", 2 * k).astype(F32)
    return result


def layer_norm(resid, norm_gain, norm_bias):
    center = resid - jnp.mean(resid, axis=-1, keepdims=True)
    inv_std = lax.rsqrt(jnp.mean(center * center, axis=-1, keepdims=True) + NORM_EPS)
    normed = center * inv_std
    return (normed * norm_gain + norm_bias, normed, inv_std)


def norm_back(upstream, normed, inv_std, norm_gain):
    scaled = upstream * norm_gain
    return inv_std * (
        scaled
        - jnp.mean(scaled, axis=-1, keepdims=True)
        - normed * jnp.mean(scaled * normed, axis=-1, keepdims=True)
    )


def gelu_slope(hidden):
    cdf_part = 0.5 * (1.0 + lax.erf(hidden * 0.7071067811865476))
    pdf_part = jnp.exp(-0.5 * hidden * hidden) * 0.3989422804014327
    return cdf_part + hidden * pdf_part


def two_halves(values):
    high = lax.reduce_precision(values, 8, 7)
    return jnp.stack([high, values - high], axis=-1).astype(BF16)


def left_lanes(block):
    lane = lax.broadcasted_iota(jnp.int32, block.shape, 1)
    return jnp.where(lane < HEAD_DIM, block, 0.0)


def masked_scores(seg_key, seg_query, scores):
    width = scores.shape[1] // seg_key.shape[1]
    same = jnp.concatenate([seg_key] * width, axis=1) == seg_query
    return jnp.where(same, scores, NEG_LARGE)


def own_scores(seg_key, seg_query, scores):
    width = scores.shape[1] // seg_key.shape[1]
    same = jnp.concatenate([seg_key] * width, axis=1) == seg_query
    rows = lax.broadcasted_iota(jnp.int32, scores.shape, 0)
    columns = lax.broadcasted_iota(jnp.int32, scores.shape, 1)
    return jnp.where(same | (rows == columns), scores, NEG_LARGE)


def score_all(turn, seg_query, seg_key_ref, qkv_ref, query_t, scores):
    sources, rows = qkv_ref.shape[0], qkv_ref.shape[1] * 2 // 3
    per_source = rows // QUERY_ROWS
    query_now = query_t[turn]
    for b in range(sources):
        spot = slice(b * rows, (b + 1) * rows)
        scores[spot, :] = masked_scores(
            seg_key_ref[spot, :], seg_query, matmul(qkv_ref[b, 0:rows, :], query_now)
        )
    own = pl.ds(pl.multiple_of(turn * QUERY_ROWS, QUERY_ROWS), QUERY_ROWS)
    inner = pl.ds(pl.multiple_of(turn % per_source * QUERY_ROWS, QUERY_ROWS), QUERY_ROWS)
    own_pair = qkv_ref[turn // per_source, inner, :]
    scores[own, :] = own_scores(seg_key_ref[own, :], seg_query, matmul(own_pair, query_now))
    return own, own_pair


def turn_queries(b, turned, query_t):
    per_source = turned.shape[1] // QUERY_ROWS
    low = jnp.concatenate([jnp.zeros_like(turned[0:HEAD_DIM]), turned[0:HEAD_DIM]], axis=0)
    for t in range(per_source):
        spot = slice(t * QUERY_ROWS, (t + 1) * QUERY_ROWS)
        query_t[b * per_source + t] = low[:, spot].astype(BF16)


def attend_kernel(
    spot_ref, seg_row_ref, seg_key_ref, qkv_ref, low_ref, attn_ref, lse_ref,
    query_t, values_t, scores,
):
    step = pl.program_id(0)
    sources, rows = qkv_ref.shape[0], qkv_ref.shape[1] * 2 // 3
    half = rows // 2

    @pl.when(step == 0)
    def _():
        for b in range(sources):
            turn_queries(b, qkv_ref[b, 0:rows, :].astype(F32).T, query_t)
            turned = qkv_ref[b, rows : rows + half, :].astype(F32).T
            values_t[:, b * rows : b * rows + half] = turned[0:HEAD_DIM].astype(BF16)
            values_t[:, b * rows + half : (b + 1) * rows] = turned[
                HEAD_DIM : 2 * HEAD_DIM
            ].astype(BF16)

    turn = spot_ref[2] + step
    score_all(turn, seg_row_ref[0], seg_key_ref, qkv_ref, query_t, scores)
    top = jnp.max(scores[...], axis=0, keepdims=True)
    total = jnp.zeros_like(top)
    result = jnp.zeros((HEAD_DIM, QUERY_ROWS), F32)
    for b in range(sources):
        spot = slice(b * rows, (b + 1) * rows)
        probs = jnp.exp(scores[spot, :] - top)
        total = total + jnp.sum(probs, axis=0, keepdims=True)
        result = result + matmul(values_t[:, spot], probs.astype(BF16))
    result = result / total
    attn_ref[...] = result
    lse_ref[0] = top + jnp.log(total)
    turned = result.T
    wide = low_ref.shape[1]
    spans = QUERY_ROWS // (2 * wide)
    first = turn % (rows // QUERY_ROWS) * spans
    for t in range(spans):
        left = turned[2 * t * wide : (2 * t + 1) * wide]
        right = turned[(2 * t + 1) * wide : (2 * t + 2) * wide]
        low_ref[spot_ref[1] ^ (first + t)] = jnp.concatenate([left, right], axis=1).astype(BF16)


def attend(spot, seg_row, seg_key, qkv, wide, query_length):
    sources, rows = qkv.shape[0], qkv.shape[1] * 2 // 3
    length = sources * rows
    steps = query_length // QUERY_ROWS
    spans = rows // (2 * wide)
    per_source = rows // QUERY_ROWS
    return pl.pallas_call(
        attend_kernel,
        grid_spec=pltpu.PrefetchScalarGridSpec(
            num_scalar_prefetch=1,
            grid=(steps,),
            in_specs=[
                pl.BlockSpec((1, 1, QUERY_ROWS), lambda i, spot: (spot[2] + i, 0, 0)),
                pl.BlockSpec(seg_key.shape, lambda i, spot: (0, 0)),
                pl.BlockSpec(qkv.shape, lambda i, spot: (0, 0, 0)),
            ],
            out_specs=[
                pl.BlockSpec((spans, wide, 128), lambda i, spot: (i // per_source, 0, 0)),
                pl.BlockSpec((HEAD_DIM, QUERY_ROWS), lambda i, spot: (0, i)),
                pl.BlockSpec((1, 1, QUERY_ROWS), lambda i, spot: (i, 0, 0)),
            ],
            scratch_shapes=[
                pltpu.VMEM((length // QUERY_ROWS, 128, QUERY_ROWS), BF16),
                pltpu.VMEM((HEAD_DIM, length), BF16),
                pltpu.VMEM((length, QUERY_ROWS), F32),
            ],
        ),
        out_shape=[
            jax.ShapeDtypeStruct((steps // per_source * spans, wide, 128), BF16),
            jax.ShapeDtypeStruct((HEAD_DIM, query_length), F32),
            jax.ShapeDtypeStruct((steps, 1, QUERY_ROWS), F32),
        ],
        compiler_params=pltpu.CompilerParams(vmem_limit_bytes=vmem_limit(length)),
    )(spot, seg_row, seg_key, qkv)


def attend_back_kernel(
    spot_ref, seg_row_ref, seg_key_ref, qkv_ref, up_ref, attn_ref, lse_ref, grads_ref,
    query_t, keys_t, values, scores, grad_query, grad_key, grad_value,
):
    step = pl.program_id(0)
    sources, rows = qkv_ref.shape[0], qkv_ref.shape[1] * 2 // 3
    half = rows // 2
    lane = lax.broadcasted_iota(jnp.int32, (rows, 128), 1)

    @pl.when(step == 0)
    def _():
        for b in range(sources):
            turned = qkv_ref[b, 0:rows, :].astype(F32).T
            turn_queries(b, turned, query_t)
            keys_t[:, b * rows : (b + 1) * rows] = turned[HEAD_DIM : 2 * HEAD_DIM].astype(BF16)
            packed = qkv_ref[b, rows : rows + half, :].astype(F32)
            values[b * rows : b * rows + half, :] = left_lanes(packed).astype(BF16)
            values[b * rows + half : (b + 1) * rows, :] = left_lanes(
                pltpu.roll(packed, HEAD_DIM, 1)
            ).astype(BF16)
        grad_query[...] = jnp.zeros_like(grad_query)
        grad_key[...] = jnp.zeros_like(grad_key)
        grad_value[...] = jnp.zeros_like(grad_value)

    turn = spot_ref[2] + step
    lse = lse_ref[0]
    pieces = []
    spans = QUERY_ROWS // (rows // up_ref.shape[0])
    first = turn % (rows // QUERY_ROWS) * spans
    for t in range(spans):
        packed = up_ref[spot_ref[1] ^ (first + t), 0 : rows // up_ref.shape[0] // 2, :].astype(F32)
        pieces.append(left_lanes(packed))
        pieces.append(left_lanes(pltpu.roll(packed, HEAD_DIM, 1)))
    up_now = jnp.concatenate(pieces, axis=0)
    up_turned = up_now.T
    delta = jnp.sum(up_turned[0:HEAD_DIM] * attn_ref[...], axis=0, keepdims=True)
    up_now = up_now.astype(BF16)
    up_turned = up_turned.astype(BF16)
    own, own_pair = score_all(turn, seg_row_ref[0], seg_key_ref, qkv_ref, query_t, scores)
    query_now = pltpu.roll(own_pair.astype(F32), HEAD_DIM, 1).astype(BF16)
    result = jnp.zeros((HEAD_DIM, QUERY_ROWS), F32)
    for b in range(sources):
        spot = slice(b * rows, (b + 1) * rows)
        probs = jnp.exp(scores[spot, :] - lse)
        grad_probs = matmul(values[spot, :], up_turned)
        grad_scores = (probs * (grad_probs - delta)).astype(BF16)
        grad_value[spot, :] += matmul(probs.astype(BF16), up_now)
        grad_key[spot, :] += matmul(grad_scores, query_now)
        result = result + matmul(keys_t[:, spot], grad_scores)
    grad_query[own, :] = jnp.concatenate([result, jnp.zeros_like(result)], axis=0).T

    @pl.when(step == pl.num_programs(0) - 1)
    def _():
        for b in range(sources):
            spot = slice(b * rows, (b + 1) * rows)
            grads_ref[b, 0:rows, :] = jnp.where(
                lane < HEAD_DIM, grad_query[spot, :], grad_key[spot, :]
            ).astype(BF16)
            upper = grad_value[b * rows : b * rows + half, :]
            lower = grad_value[b * rows + half : (b + 1) * rows, :]
            grads_ref[b, rows : rows + half, :] = (
                upper + pltpu.roll(lower, HEAD_DIM, 1)
            ).astype(BF16)


def attend_back(spot, seg_row, seg_key, qkv, upstream, attn_t, lse):
    sources, rows = qkv.shape[0], qkv.shape[1] * 2 // 3
    length = sources * rows
    steps = lse.shape[0]
    groups = upstream.shape[0] // sources
    per_source = rows // QUERY_ROWS
    return pl.pallas_call(
        attend_back_kernel,
        grid_spec=pltpu.PrefetchScalarGridSpec(
            num_scalar_prefetch=1,
            grid=(steps,),
            in_specs=[
                pl.BlockSpec((1, 1, QUERY_ROWS), lambda i, spot: (spot[2] + i, 0, 0)),
                pl.BlockSpec(seg_key.shape, lambda i, spot: (0, 0)),
                pl.BlockSpec(qkv.shape, lambda i, spot: (0, 0, 0)),
                pl.BlockSpec(
                    (groups,) + upstream.shape[1:],
                    lambda i, spot: ((spot[2] + i) // per_source, 0, 0),
                ),
                pl.BlockSpec((HEAD_DIM, QUERY_ROWS), lambda i, spot: (0, i)),
                pl.BlockSpec((1, 1, QUERY_ROWS), lambda i, spot: (i, 0, 0)),
            ],
            out_specs=pl.BlockSpec(qkv.shape, lambda i, spot: (0, 0, 0)),
            scratch_shapes=[
                pltpu.VMEM((length // QUERY_ROWS, 128, QUERY_ROWS), BF16),
                pltpu.VMEM((HEAD_DIM, length), BF16),
                pltpu.VMEM((length, 128), BF16),
                pltpu.VMEM((length, QUERY_ROWS), F32),
                pltpu.VMEM((length, 128), F32),
                pltpu.VMEM((length, 128), F32),
                pltpu.VMEM((length, 128), F32),
            ],
        ),
        out_shape=jax.ShapeDtypeStruct(qkv.shape, BF16),
        compiler_params=pltpu.CompilerParams(vmem_limit_bytes=vmem_limit(length)),
    )(spot, seg_row, seg_key, qkv, upstream, attn_t, lse)


def left_pair(first, second):
    lane = lax.broadcasted_iota(jnp.int32, first.shape, 1)
    return jnp.where(lane < HEAD_DIM, first, pltpu.roll(second, HEAD_DIM, 1))


def right_pair(first, second):
    lane = lax.broadcasted_iota(jnp.int32, first.shape, 1)
    return jnp.where(lane < HEAD_DIM, pltpu.roll(first, HEAD_DIM, 1), second)


def join_kernel(
    seqs, heads_here, repeats, spot_ref, got_ref, tokens_ref, flags_ref, mat_ref, vectors_ref,
    sent_ref, normed_ref, unit_ref, inv_ref, squares_ref, attn,
):
    my_group, part = spot_ref[1], spot_ref[3]
    groups = sent_ref.shape[0]
    wide = got_ref.shape[1]
    width = tokens_ref.shape[1]
    width_here = heads_here * HEAD_DIM
    for which in range(seqs):
        for group in range(groups):
            for head in range(0, heads_here, 2):
                first, second = [
                    got_ref[
                        ((which * heads_here + i) * repeats + part) * groups + group
                    ].astype(F32)
                    for i in (head, head + 1)
                ]
                start = group * width_here + head * HEAD_DIM
                top = 2 * which * wide
                attn[top : top + wide, start : start + 128] = left_pair(first, second).astype(BF16)
                attn[top + wide : top + 2 * wide, start : start + 128] = right_pair(
                    first, second
                ).astype(BF16)
    branch = matmul(attn[...], mat_ref[...]) + vectors_ref[0:1, :]
    resid_in = tokens_ref[...].astype(F32)
    normed, unit, inv_std = layer_norm(resid_in + branch, vectors_ref[2:3, :], vectors_ref[3:4, :])
    normed_ref[...] = normed
    unit_ref[...] = unit
    inv_ref[...] = jnp.broadcast_to(inv_std, inv_ref.shape)
    low = normed.astype(BF16)
    for k in range(groups):
        sent_ref[k, :, 0:width] = low
        for group in range(groups):

            @pl.when((my_group ^ k) == group)
            def _():
                sent_ref[k, :, width:] = attn[:, group * width_here : (group + 1) * width_here]

    lane = lax.broadcasted_iota(jnp.int32, squares_ref.shape, 1)
    total = jnp.zeros(squares_ref.shape, F32)
    for i, item in enumerate((resid_in, branch, normed)):
        size = flags_ref[...] * jnp.sum(item * item, axis=1, keepdims=True)
        total = total + jnp.where(lane == i, jnp.sum(size, axis=0, keepdims=True), 0.0)
    squares_ref[...] = total


def join(spot, got, tokens, flags, mat_out, vectors, seqs, heads_here, repeats):
    groups = tokens.shape[1] // (heads_here * HEAD_DIM)
    rows, width = tokens.shape
    vmem = pl.BlockSpec(memory_space=pltpu.VMEM)
    return pl.pallas_call(
        functools.partial(join_kernel, seqs, heads_here, repeats),
        in_specs=[pl.BlockSpec(memory_space=pltpu.SMEM)] + [vmem] * 5,
        out_specs=[vmem] * 5,
        out_shape=[
            jax.ShapeDtypeStruct((groups, rows, width + heads_here * HEAD_DIM), BF16),
            jax.ShapeDtypeStruct((rows, width), F32),
            jax.ShapeDtypeStruct((rows, width), F32),
            jax.ShapeDtypeStruct((rows, 128), F32),
            jax.ShapeDtypeStruct((1, 128), F32),
        ],
        scratch_shapes=[pltpu.VMEM((rows, width), BF16)],
        compiler_params=pltpu.CompilerParams(vmem_limit_bytes=32 * 1024 * 1024),
    )(spot, got, tokens, flags, mat_out, vectors)


def branch_back_kernel(
    seqs, heads_here, repeats, spot_ref, *refs,
):
    (own_ref, resid_ref, unit_ref, inv_ref, gain_ref, mat_ref, early_ref, up_sums_ref,
     squares_ref), others, (sent_ref, grad_ref, low_ref) = refs[:9], refs[9:-3], refs[-3:]
    my_group = spot_ref[1]
    groups = len(others) + 1
    rows, width = own_ref.shape
    span = rows // seqs
    wide = span // 2
    devices = sent_ref.shape[0]
    blocks = devices // groups
    grad_normed = own_ref[...]
    for other in others:
        grad_normed = grad_normed + other[...].astype(F32)
    grad_normed = grad_normed + resid_ref[...]
    unit = unit_ref[...]
    grad_resid = norm_back(grad_normed, unit, inv_ref[:, 0:1], gain_ref[...])
    grad_ref[...] = grad_resid
    low = grad_resid.astype(BF16)
    low_ref[...] = low
    grad_attn = matmul_nt(low, mat_ref[...])
    for which in range(seqs):
        top = which * span
        for group in range(groups):
            for head in range(0, heads_here, 2):
                start = (group * heads_here + head) * HEAD_DIM
                upper = grad_attn[top : top + wide, start : start + 128]
                lower = grad_attn[top + wide : top + span, start : start + 128]
                blocks_two = (left_pair(upper, lower), right_pair(upper, lower))
                for i in range(2):
                    for copy in range(repeats):
                        pair = which * heads_here + head + i
                        place = (pair * repeats + copy) * groups + group
                        sent_ref[place, 0:wide, :] = blocks_two[i].astype(BF16)
    sums = [
        jnp.sum(low.astype(F32), axis=0, keepdims=True),
        jnp.sum(grad_normed * unit, axis=0, keepdims=True),
        jnp.sum(grad_normed, axis=0, keepdims=True),
    ] + [early_ref[i : i + 1, :] for i in range(3)]
    row = lax.broadcasted_iota(jnp.int32, (8, 128), 0)
    dim_rows = width // devices
    unit_rows = up_sums_ref.shape[1] // blocks
    for tile in range(width // 128):
        base = jnp.where(row == 7, squares_ref[...], 0.0)
        for i in range(6):
            base = base + jnp.where(row == i, sums[i][:, tile * 128 : (tile + 1) * 128], 0.0)
        for place in range(tile * 128 // dim_rows, (tile + 1) * 128 // dim_rows):
            start = place // groups * unit_rows // 128 * 128
            mine = jnp.where(my_group == place % groups, up_sums_ref[:, start : start + 128], 0.0)
            block = base + jnp.where(row == 6, mine, 0.0)
            high = block.astype(BF16)
            rest = block - high.astype(F32)
            sent_ref[place, wide : wide + 16, :] = jnp.concatenate(
                [high.astype(F32), rest], axis=0
            ).astype(BF16)


def branch_back(spot, own, others, resid, unit, inv_std, gain, mat_out, early, up_sums, squares,
                seqs, heads_here, repeats, devices):
    rows, width = own.shape
    vmem = pl.BlockSpec(memory_space=pltpu.VMEM)
    return pl.pallas_call(
        functools.partial(branch_back_kernel, seqs, heads_here, repeats),
        in_specs=[pl.BlockSpec(memory_space=pltpu.SMEM)] + [vmem] * (9 + len(others)),
        out_specs=[vmem] * 3,
        out_shape=[
            jax.ShapeDtypeStruct((devices, rows // seqs // 2 + 16, 128), BF16),
            jax.ShapeDtypeStruct((rows, width), F32),
            jax.ShapeDtypeStruct((rows, width), BF16),
        ],
        compiler_params=pltpu.CompilerParams(vmem_limit_bytes=32 * 1024 * 1024),
    )(spot, own, resid, unit, inv_std, gain, mat_out, early, up_sums, squares, *others)


def project_kernel(groups, heads_here, repeats, spot_ref, *refs):
    tokens, (mine_ref, other_ref, sent_ref, all_ref, mat_ref, values) = refs[:groups], refs[groups:]
    my_block, my_group = spot_ref[0], spot_ref[1]
    halves, chip_rows, _ = mine_ref.shape
    blocks = 2 * halves
    dim_rows = chip_rows // groups
    rows, width = tokens[0].shape
    width_here = heads_here * HEAD_DIM
    seqs = sent_ref.shape[0] // (repeats * heads_here)
    span = rows // seqs
    block_rows = span * groups
    for k in range(groups):
        all_ref[k * rows : (k + 1) * rows, :] = tokens[k][...]
    for b in range(blocks):
        place = my_block ^ b
        spot = slice(b * chip_rows, (b + 1) * chip_rows)

        @pl.when(place % 2 == 0)
        def _():
            mat_ref[spot, :] = mine_ref[place // 2, :, 0 : 3 * width_here]

        @pl.when(place % 2 == 1)
        def _():
            mat_ref[spot, :] = other_ref[place // 2, :, 0 : 3 * width_here]

    lane = lax.broadcasted_iota(jnp.int32, (1, 128), 1)
    tiles = width_here // 128
    biases = [[jnp.zeros((1, 128), F32) for _ in range(tiles)] for _ in range(2)]
    for t in range(blocks):
        place = my_block ^ (my_group * (blocks // groups) + t // groups)
        piece = jnp.where(
            place % 2 == 0,
            mine_ref[place // 2, :, 3 * width_here :].astype(F32),
            other_ref[place // 2, :, 3 * width_here :].astype(F32),
        )
        piece = piece[t % groups * dim_rows : t % groups * dim_rows + 1]
        tile, start = t * dim_rows // 128, t * dim_rows % 128
        inside = (lane >= start) & (lane < start + dim_rows)
        for which in range(2):
            shift = (start - which * dim_rows) % 128
            moved = pltpu.roll(piece, shift, 1) if shift else piece
            biases[which][tile] = biases[which][tile] + jnp.where(inside, moved, 0.0)
    query_bias, value_bias = [jnp.concatenate(item, axis=1) for item in biases]
    result = matmul(all_ref[...], mat_ref[...])
    query = (result[:, :width_here] + query_bias) * HEAD_DIM ** (-0.5)
    key = result[:, width_here : 2 * width_here]
    values[...] = result[:, 2 * width_here :] + value_bias
    half_parts = groups // 2
    for pair in range(seqs * heads_here):
        which, head = pair // heads_here, pair % heads_here
        columns = slice(head * HEAD_DIM, (head + 1) * HEAD_DIM)
        for k in range(groups):
            spot = slice(k * rows + which * span, k * rows + (which + 1) * span)
            block = jnp.concatenate([query[spot, columns], key[spot, columns]], axis=1)
            for copy in range(repeats):
                sent_ref[pair * repeats + copy, k * span : (k + 1) * span, :] = block.astype(BF16)
        for k in range(half_parts):
            upper = slice(k * rows + which * span, k * rows + (which + 1) * span)
            lower = slice(upper.start + half_parts * rows, upper.stop + half_parts * rows)
            block = jnp.concatenate([values[upper, columns], values[lower, columns]], axis=1)
            for copy in range(repeats):
                sent_ref[
                    pair * repeats + copy, block_rows + k * span : block_rows + (k + 1) * span, :
                ] = block.astype(BF16)


def project(spot, token_parts, mine, other, seqs, heads_here, repeats):
    groups = len(token_parts)
    rows, width = token_parts[0].shape
    blocks = seqs * heads_here * repeats
    block_rows = rows // seqs * groups
    vmem = pl.BlockSpec(memory_space=pltpu.VMEM)
    return pl.pallas_call(
        functools.partial(project_kernel, groups, heads_here, repeats),
        in_specs=[pl.BlockSpec(memory_space=pltpu.SMEM)] + [vmem] * (groups + 2),
        out_specs=[vmem] * 3,
        out_shape=[
            jax.ShapeDtypeStruct((blocks, block_rows * 3 // 2, 128), BF16),
            jax.ShapeDtypeStruct((groups * rows, width), BF16),
            jax.ShapeDtypeStruct((width, 3 * heads_here * HEAD_DIM), BF16),
        ],
        scratch_shapes=[pltpu.VMEM((groups * rows, heads_here * HEAD_DIM), F32)],
        compiler_params=pltpu.CompilerParams(vmem_limit_bytes=40 * 1024 * 1024),
    )(spot, *token_parts, mine, other)


def input_kernel(
    groups, heads_here, repeats, spot_ref, got_ref, mat_ref, all_ref,
    own_ref, others_ref, keep_ref, send_ref, grads, mat_grads,
):
    my_block, my_group = spot_ref[0], spot_ref[1]
    blocks = got_ref.shape[0]
    seqs = blocks // (repeats * heads_here)
    rows = all_ref.shape[0] // groups
    span = rows // seqs
    block_rows = span * groups
    width_here = heads_here * HEAD_DIM
    chip_rows = keep_ref.shape[1] - 16
    half_parts = groups // 2

    def received(pair, start):
        spot = slice(start, start + span)
        total = got_ref[pair * repeats, spot, :].astype(F32)
        for copy in range(1, repeats):
            total = total + got_ref[pair * repeats + copy, spot, :].astype(F32)
        return total

    for which in range(seqs):
        for head in range(0, heads_here, 2):
            pair = which * heads_here + head
            start = head * HEAD_DIM
            for k in range(groups):
                spot = slice(k * rows + which * span, k * rows + (which + 1) * span)
                first, second = received(pair, k * span), received(pair + 1, k * span)
                grads[spot, start : start + 128] = (
                    left_pair(first, second) * HEAD_DIM ** (-0.5)
                ).astype(BF16)
                grads[spot, width_here + start : width_here + start + 128] = right_pair(
                    first, second
                ).astype(BF16)
                inner = block_rows + k % half_parts * span
                first, second = received(pair, inner), received(pair + 1, inner)
                grads[spot, 2 * width_here + start : 2 * width_here + start + 128] = (
                    left_pair(first, second) if k < half_parts else right_pair(first, second)
                ).astype(BF16)
    back = matmul_nt(grads[...], mat_ref[...])
    own_ref[...] = back[:rows]
    for k in range(1, groups):
        others_ref[k - 1] = back[k * rows : (k + 1) * rows].astype(BF16)
    mat_grads[...] = matmul_tn(all_ref[...], grads[...])
    query_sums = jnp.sum(grads[:, :width_here].astype(F32), axis=0, keepdims=True)
    value_sums = jnp.sum(grads[:, 2 * width_here :].astype(F32), axis=0, keepdims=True)
    chunks = blocks // groups
    chunk = width_here // chunks
    row = lax.broadcasted_iota(jnp.int32, (16, 128), 0)
    for k in range(blocks):
        owner = my_block ^ k
        spot = pl.ds(pl.multiple_of(owner * chip_rows, chip_rows), chip_rows)
        block = mat_grads[spot, :]
        sums = []
        for total in (query_sums, value_sums):
            chosen = jnp.zeros((1, chunk), F32)
            for i in range(chunks):
                piece = total[:, i * chunk : (i + 1) * chunk]
                chosen = chosen + jnp.where(owner == my_group * chunks + i, piece, 0.0)
            sums.append(jnp.concatenate([chosen, jnp.zeros((1, 128 - chunk), F32)], axis=1) if chunk < 128 else chosen)
        if k % 2 == 0:
            keep_ref[k // 2, 0:chip_rows, :] = block
        else:
            send_ref[k // 2, 0:chip_rows, :] = block.astype(BF16)
        for i in range(3 * width_here // 128):
            value = jnp.where(row == 0, sums[i], 0.0) if i < 2 else jnp.zeros((16, 128), F32)
            columns = slice(i * 128, (i + 1) * 128)
            if k % 2 == 0:
                keep_ref[k // 2, chip_rows : chip_rows + 16, columns] = value
            else:
                send_ref[k // 2, chip_rows : chip_rows + 16, columns] = value.astype(BF16)


def input_grads(spot, got, mat_three, token_all, heads_here, groups, repeats):
    blocks = got.shape[0]
    total_rows, width = token_all.shape
    rows = total_rows // groups
    chip_rows = width // blocks
    columns = mat_three.shape[1]
    vmem = pl.BlockSpec(memory_space=pltpu.VMEM)
    shape = (blocks // 2, chip_rows + 16, columns)
    return pl.pallas_call(
        functools.partial(input_kernel, groups, heads_here, repeats),
        in_specs=[pl.BlockSpec(memory_space=pltpu.SMEM)] + [vmem] * 3,
        out_specs=[vmem] * 4,
        out_shape=[
            jax.ShapeDtypeStruct((rows, width), F32),
            jax.ShapeDtypeStruct((groups - 1, rows, width), BF16),
            jax.ShapeDtypeStruct(shape, F32),
            jax.ShapeDtypeStruct(shape, BF16),
        ],
        scratch_shapes=[
            pltpu.VMEM((total_rows, columns), BF16),
            pltpu.VMEM((width, columns), F32),
        ],
        compiler_params=pltpu.CompilerParams(vmem_limit_bytes=40 * 1024 * 1024),
    )(spot, got, mat_three, token_all)


def per_device(
    tokens,
    cotangent,
    doc_offsets,
    valid_flags,
    w_query,
    w_key,
    w_value,
    w_out,
    w_fc1,
    w_fc2,
    b_query,
    b_value,
    b_out,
    b_fc1,
    b_fc2,
    gain_attn,
    bias_attn,
    gain_ffn,
    bias_ffn,
):
    seqs, span, width = tokens.shape
    groups = lax.axis_size("heads")
    blocks = lax.axis_size("blk")
    devices = groups * blocks
    my_group = lax.axis_index("heads")
    my_block = lax.axis_index("blk")
    rows = seqs * span
    block_rows = span * groups
    length = block_rows * blocks
    heads = width // HEAD_DIM
    heads_here = heads // groups
    pairs = seqs * heads_here
    repeats = blocks // pairs
    parts_length = length // repeats
    width_here = heads_here * HEAD_DIM
    dim_rows = w_query.shape[0]
    unit_rows = w_fc2.shape[0]
    hidden_size = w_fc1.shape[1]
    units_here = hidden_size // groups
    qk_scale = HEAD_DIM ** (-0.5)
    half = block_rows // 2
    wide = span // 2

    token_rows = tokens.reshape(rows, width)
    token_parts = gather_parts(token_rows, "heads")
    w_three = jnp.concatenate(
        [w.reshape(dim_rows, groups, width_here) for w in (w_query, w_key, w_value)], axis=-1
    )
    w_three = jnp.transpose(w_three, (1, 0, 2))
    def lanes_of(pieces):
        flat = jnp.concatenate(pieces)
        return jnp.pad(flat, (0, dim_rows * 128 - flat.shape[0])).reshape(dim_rows, 128)

    vectors = lanes_of([b_query, b_value])
    w_up = w_fc1.reshape(dim_rows, blocks, groups, unit_rows)
    w_up = jnp.transpose(w_up, (2, 0, 1, 3)).reshape(groups, dim_rows, units_here)
    first = jnp.concatenate(
        [w_three, jnp.broadcast_to(vectors[None], (groups,) + vectors.shape), w_up], axis=-1
    )
    first = lax.all_to_all(first, "heads", split_axis=0, concat_axis=0, tiled=True)
    first = first.reshape(groups * dim_rows, first.shape[-1])
    second = first[:, 3 * width_here + 128 :].reshape(-1, width)
    second = jnp.concatenate([second, w_fc2])
    third = lanes_of([b_out, b_fc2, gain_attn, bias_attn, gain_ffn, bias_ffn, b_fc1])
    third = after(jnp.concatenate([w_out, third], axis=1), first)
    third = lax.all_gather(third, ALL, axis=0, tiled=False)

    first = first[:, : 3 * width_here + 128]
    for part in token_parts[1:]:
        first = after(first, part)
    mine, other = gather_blk_parts(first, second)
    part_blocks = blocks // repeats
    first_turn = my_block % repeats * (parts_length // QUERY_ROWS)
    spot = jnp.stack([my_block, my_group, first_turn, my_block // part_blocks]).astype(jnp.int32)
    sent, token_all, mat_three = project(
        spot, token_parts, mine, other, seqs, heads_here, repeats
    )
    qkv = lax.all_to_all(sent, "blk", split_axis=0, concat_axis=0, tiled=True)


    mat_out = third[..., :width].reshape(width, width)
    vectors = third[..., width:].reshape(devices, dim_rows * 128)[:, : 6 * dim_rows + unit_rows]
    short = jnp.transpose(vectors[:, : 6 * dim_rows].reshape(devices, 6, dim_rows), (1, 0, 2))
    short = short.reshape(6, width).astype(F32)
    vec_out, vec_down, gain_one, bias_one, gain_two, bias_two = [short[i] for i in range(6)]
    vec_up = vectors[:, 6 * dim_rows :].reshape(blocks, groups, unit_rows)
    vec_up = lax.dynamic_index_in_dim(vec_up, my_group, 1, False).reshape(units_here).astype(F32)

    second = lax.all_gather(after(second, qkv), "blk", axis=0, tiled=False)
    up_rows = groups * dim_rows * units_here // width
    mat_up = second[:, :up_rows].reshape(width, units_here)
    mat_down = second[:, up_rows:].reshape(units_here, width)

    my_pair = my_block // repeats
    my_part = my_block % repeats
    my_seq = my_pair // heads_here
    inner = jnp.arange(length, dtype=jnp.int32)
    place = (inner // block_rows) * block_rows + inner % span
    place = place + (((inner // span) % groups) ^ my_group) * span
    offsets = lax.dynamic_index_in_dim(doc_offsets, my_seq, 0, False)
    flags = lax.dynamic_index_in_dim(valid_flags, my_seq, 0, False)
    flags = xor_order(flags.reshape(blocks, groups, span), 1, my_group).reshape(length)
    segment = jnp.sum((offsets[None, :] <= place[:, None]).astype(jnp.int32), axis=1) - 1
    seg_row = segment.reshape(length // QUERY_ROWS, 1, QUERY_ROWS)
    seg_key = jnp.where(flags > 0, segment, -1)
    seg_key = jnp.broadcast_to(seg_key[:, None], (length, 128))
    attn_low, attn_t, lse = attend(spot, seg_row, seg_key, qkv, wide, parts_length)

    sent = jnp.concatenate([attn_low] * repeats, axis=0) if repeats > 1 else attn_low
    got = lax.all_to_all(sent, ALL, split_axis=0, concat_axis=0, tiled=True)
    my_span = my_block * groups + my_group
    local_flags = lax.dynamic_slice_in_dim(valid_flags, my_span * span, span, 1)
    local_flags = local_flags.reshape(rows, 1).astype(F32)
    sent, normed_one, unit_one, inv_one, squares = join(
        spot, got, token_rows, local_flags, mat_out, short, seqs, heads_here, repeats
    )
    joint_parts = [sent[0]] + [swapped(sent[k], "heads", k) for k in range(1, groups)]
    normed_parts = [part[:, :width] for part in joint_parts]
    attn_parts = [part[:, width:] for part in joint_parts]
    hidden_parts = [matmul(part, mat_up) + vec_up for part in normed_parts]
    act_parts = [jax.nn.gelu(part, approximate=False).astype(BF16) for part in hidden_parts]
    ffn_parts = [matmul(part, mat_down) for part in act_parts]
    ffn = scatter_parts(ffn_parts, "heads") + vec_down
    normed_two, unit_two, inv_two = layer_norm(normed_one + ffn, gain_two, bias_two)
    output = normed_two.astype(BF16).reshape(tokens.shape)
    last = jnp.sum(local_flags * jnp.sum(ffn * ffn, axis=1, keepdims=True))
    squares = squares + jnp.where(jnp.arange(128) == 3, last, 0.0)[None]

    upstream = cotangent.reshape(rows, width).astype(F32)
    grad_gain_two = jnp.sum(upstream * unit_two, axis=0)
    grad_bias_two = jnp.sum(upstream, axis=0)
    grad_resid_two = norm_back(upstream, unit_two, inv_two, gain_two)
    grad_ffn = grad_resid_two.astype(BF16)
    grad_vec_down = jnp.sum(grad_ffn.astype(F32), axis=0)
    grad_ffn_parts = gather_parts(grad_ffn, "heads")
    grad_hidden_parts = [
        (matmul_nt(part, mat_down) * gelu_slope(hidden)).astype(BF16)
        for part, hidden in zip(grad_ffn_parts, hidden_parts)
    ]
    grad_normed_parts = [matmul_nt(part, mat_up) for part in grad_hidden_parts]
    grad_normed_others = [
        swapped(grad_normed_parts[k].astype(BF16), "heads", k) for k in range(1, groups)
    ]
    grad_ffn_all = jnp.concatenate(grad_ffn_parts, axis=0)
    grad_hidden = jnp.concatenate(grad_hidden_parts, axis=0)
    grad_vec_up = jnp.sum(grad_hidden.astype(F32), axis=0)
    act_low = jnp.concatenate(act_parts, axis=0)
    normed_all = jnp.concatenate(normed_parts, axis=0)
    grad_mat_down = matmul_tn(act_low, grad_ffn_all).astype(BF16)
    grad_mat_up = matmul_tn(normed_all, grad_hidden).astype(BF16)
    ffn_grads = jnp.concatenate(
        [
            grad_mat_down.reshape(blocks, unit_rows, width),
            grad_mat_up.reshape(blocks, -1, width),
        ],
        axis=1,
    )
    ffn_grads = lax.psum_scatter(
        ffn_grads.reshape(-1, width), "blk", scatter_dimension=0, tiled=True
    )
    shard_down = ffn_grads[:unit_rows].astype(F32)
    shard_up = lax.all_to_all(
        ffn_grads[unit_rows:].reshape(groups, dim_rows, units_here),
        "heads",
        split_axis=0,
        concat_axis=0,
        tiled=True,
    )
    shard_up = jnp.transpose(
        shard_up.reshape(groups, dim_rows, blocks, unit_rows), (1, 2, 0, 3)
    ).reshape(dim_rows, hidden_size)
    shard_up = shard_up.astype(F32)

    sent, grad_resid_one, grad_branch = branch_back(
        spot, grad_normed_parts[0], grad_normed_others, grad_resid_two, unit_one, inv_one,
        gain_one[None], mat_out, jnp.stack([grad_vec_down, grad_gain_two, grad_bias_two]),
        grad_vec_up[None], squares, seqs, heads_here, repeats, devices,
    )
    got = lax.all_to_all(sent, ALL, split_axis=0, concat_axis=0, tiled=True)
    small = jnp.sum(got[:, wide:].astype(F32), axis=0)
    small = small[:8] + small[8:]
    vector_sums = lax.dynamic_slice_in_dim(small[:6], my_span * dim_rows % 128, dim_rows, 1)
    shard_vec_up = lax.dynamic_slice_in_dim(small[6], my_block * unit_rows % 128, unit_rows, 0)
    real_count = jnp.maximum(jnp.sum(valid_flags.astype(F32)), 1.0)
    rms = jnp.sqrt(small[7, :4] / (real_count * width))

    branch_parts = gather_parts(grad_branch, "heads")
    grad_mat_out = matmul_tn(
        jnp.concatenate(attn_parts, axis=0), jnp.concatenate(branch_parts, axis=0)
    ).astype(BF16)
    shard_out = scatter_blk(grad_mat_out.reshape(blocks, dim_rows, width)).astype(BF16)
    route = [(j, j % groups * blocks + j // groups) for j in range(devices)]
    shard_out = lax.ppermute(shard_out, ("heads", "blk"), route)
    grads = attend_back(spot, seg_row, seg_key, qkv, got, attn_t, lse)
    got = lax.all_to_all(grads, "blk", split_axis=0, concat_axis=0, tiled=True)
    got = after(got, shard_out)
    own_input, other_input, keep, send = input_grads(
        spot, got, mat_three, token_all, heads_here, groups, repeats
    )
    grad_input = grad_resid_one + own_input
    for k in range(1, groups):
        grad_input = grad_input + swapped(other_input[k - 1], "heads", k).astype(F32)
    grad_input = grad_input.reshape(tokens.shape)
    chip_sums = keep + swapped(send, "blk", 1).astype(F32)
    chip_low = chip_sums.astype(BF16)
    three_grads = chip_sums[0]
    for k in range(1, blocks // 2):
        three_grads = three_grads + swapped(chip_low[k], "blk", 2 * k).astype(F32)
    own_rows = three_grads[: groups * dim_rows].reshape(groups, dim_rows, 3 * width_here)
    own_sums = three_grads[groups * dim_rows, :256].reshape(2, 128)[:, : groups * dim_rows]
    own_sums = jnp.transpose(own_sums.reshape(2, groups, dim_rows), (1, 0, 2))
    row = lax.broadcasted_iota(jnp.int32, (1, 16, 1), 1)
    own_sums = jnp.concatenate(
        [
            own_sums.reshape(groups, 2 * dim_rows),
            jnp.zeros((groups, 3 * width_here - 2 * dim_rows), F32),
        ],
        axis=1,
    )
    own_sums = jnp.where(row == 0, own_sums[:, None, :], 0.0)
    own = jnp.concatenate([own_rows, own_sums], axis=1).astype(BF16)
    own = after(own, shard_up)
    own = lax.all_to_all(own, "heads", split_axis=0, concat_axis=0, tiled=True).astype(F32)
    shard_sums = jnp.sum(own[:, dim_rows, : 2 * dim_rows], axis=0)
    shards_three = [
        jnp.transpose(
            own[:, :dim_rows, which * width_here : (which + 1) * width_here], (1, 0, 2)
        ).reshape(dim_rows, width)
        for which in range(3)
    ]

    return (
        output,
        grad_input,
        shards_three[0],
        shards_three[1],
        shards_three[2],
        shard_out.astype(F32),
        shard_up,
        shard_down,
        shard_sums[:dim_rows],
        shard_sums[dim_rows:],
        vector_sums[0],
        shard_vec_up,
        vector_sums[3],
        vector_sums[1],
        vector_sums[2],
        vector_sums[4],
        vector_sums[5],
        rms,
    )


def solution(mesh):
    token_spec = P(None, ALL, None)
    matrix_spec = P(ALL, None)
    vector_spec = P(ALL)
    return jax.shard_map(
        per_device,
        mesh=mesh,
        in_specs=(token_spec,) * 2 + (P(),) * 2 + (matrix_spec,) * 6 + (vector_spec,) * 9,
        out_specs=(token_spec,) * 2 + (matrix_spec,) * 6 + (vector_spec,) * 9 + (P(),),
        check_vma=False,
    )
```

time: 424 us -> 384 us (0.906); the launches traced: 416 us -> 383 us
  blocking collectives: 21.6 us -> 0 us
  other arithmetic: 36.3 us -> 18.5 us
  matrix products: 36 us -> 23.7 us
  Pallas kernels: 27.4 us -> 39.5 us
  starting transfers between devices: 63.9 us -> 74.8 us
  local copies, waits for them, and re-layouts: 54.5 us -> 44.7 us
  between operations: 16.3 us -> 20.9 us
    all_to_all x2 -> x0, blocking collectives: 21.6 us -> none  [the longest x1 13.6 us: per_device(): lax.all_to_all(second, 'heads', split_axis=0, concat_axis=0, tiled=True)]
    slice x13 -> x22, local copies, waits for them, and re-layouts: 3.86 us -> 20.2 us  [the longest x4 6.69 us: per_device(): normed_parts = [part[:, :width] for part in joint_parts]]
    pallas_call x0 -> x4, Pallas kernels: none -> 10.4 us  [the longest x1 2.85 us: project(): pl.pallas_call(functools.partial(project_kernel, groups, heads_here, repe...]
    ppermute x33, starting transfers between devices: 38.2 us -> 47.7 us  [swapped(): return lax.ppermute(block, axis, [(i, i ^ mask) for i in range(count)])]
    all_to_all x1, waiting for transfers between devices: 0.01 us -> 7.49 us  [per_device(): lax.all_to_all(first, 'heads', split_axis=0, concat_axis=0, tiled=True)]
    another operation x19 -> x0, local copies, waits for them, and re-layouts: 7.4 us -> none  [the longest x1 2.89 us: per_device(): attn_tok.reshape(rows, blocks, groups, dim_rows)]
    reduce_sum x9 -> x3, other arithmetic: 7.72 us -> 0.89 us  [the longest x1 0.67 us: per_device(): last = jnp.sum(local_flags * jnp.sum(ffn * ffn, axis=1, keepdims=True))]
    reshape x11 -> x0, local copies, waits for them, and re-layouts: 6.55 us -> none  [the longest x2 2.66 us: per_device(): sent = grad_attn.reshape(seqs, 2, wide, groups, heads_here, HEAD_DIM)]
  transfers between devices with their start and end apart: 43 -> 44, of which waited for: 24 -> 26; matrix products, arithmetic and copies ran while one was open for 25% -> 15% of each run, Pallas kernels for 7% -> 10%
where the time goes in v3:
time: 384 us; the launch traced here: 383 us
  waiting for transfers between devices  161 us (42%)
  starting transfers between devices  74.8 us (19%)
  local copies, waits for them, and re-layouts  44.7 us (12%)
  Pallas kernels  39.5 us (10%)
  matrix products  23.7 us (6%)
  between operations  20.9 us (5%)
  other arithmetic  18.5 us (5%)
    ppermute x33, waiting for transfers between devices, swapped(): return lax.ppermute(block, axis, [(i, i ^ mask) for i in range(count)])  97.6 us
    ppermute x33, starting transfers between devices, swapped(): return lax.ppermute(block, axis, [(i, i ^ mask) for i in range(count)])  47.7 us
    all_to_all x1, waiting for transfers between devices, per_device(): qkv = lax.all_to_all(sent, 'blk', split_axis=0, concat_axis=0, tiled=True)  24.5 us
    all_to_all x2, waiting for transfers between devices, per_device(): got = lax.all_to_all(sent, ALL, split_axis=0, concat_axis=0, tiled=True)  21.3 us
    pallas_call x1, Pallas kernels, attend_back(): pl.pallas_call(attend_back_kernel, grid_spec=pltpu.PrefetchScalarGridSpec...  17.2 us
    pallas_call x1, Pallas kernels, attend(): pl.pallas_call(attend_kernel, grid_spec=pltpu.PrefetchScalarGridSpec(num_...  11.9 us
    dot_general x8, matrix products, matmul(): return jnp.dot(left, right, preferred_element_type=F32)  10.8 us
    unnamed x106, local copies, waits for them, and re-layouts  10.7 us
  transfers between devices with their start and end apart: 44, of which 26 were waited for; matrix products, arithmetic and copies ran while one was open for 15% of the time, Pallas kernels for 10%

profile of v3, /device:TPU:0, one launch (start us, length us, event | category | flops | bytes accessed | tf_op | source)
XLA Modules:
  0.0 382.6 jit_solution(8708710068389713000)
XLA Ops:
  12.0 5.2 %all-to-all-start = ((bf16[4,32,1920]{2,1,0:T(8,128)(2,1)}), bf16[4,32,1920]{2,1,0:T(8,128)(2,1)S(1)}, u32[]{:S(2)}, u32[]{:S(2)}) async-start(bf16[4,32,1920]{2,1,0:T(8,128)(2,1)} %pad_maximum_fusion.2), calls=%async_computation | async-start | bytes 983040 | tf_op jit(solution)/shard_map/all_to_all | solution.py:735
  17.3 7.5 %all-to-all-done = bf16[4,32,1920]{2,1,0:T(8,128)(2,1)S(1)} async-done(((bf16[4,32,1920]{2,1,0:T(8,128)(2,1)}), bf16[4,32,1920]{2,1,0:T(8,128)(2,1)S(1)}, u32[]{:S(2)}, u32[]{:S(2)}) %all-to-all-start) | async-done | bytes 491552 | tf_op jit(solution)/shard_map/all_to_all | solution.py:735
  30.2 6.7 %collective-permute-done.2.refs_3_ = bf16[128,1024]{1,0:T(8,128)(2,1)S(1)} collective-permute-done((bf16[128,1024]{1,0:T(8,128)(2,1)S(1)}, bf16[128,1024]{1,0:T(8,128)(2,1)S(1)}, u32[]{:S(2)}, u32[]{:S(2)}) %collective-permute-start.2) | collective-permute-done | bytes 262176 | tf_op jit(solution)/shard_map/ppermute | solution.py:42
  48.3 5.2 %collective-permute-done.5 = bf16[128,896]{1,0:T(8,128)(2,1)S(1)} collective-permute-done((bf16[128,896]{1,0:T(8,128)(2,1)S(1)}, bf16[128,896]{1,0:T(8,128)(2,1)S(1)}, u32[]{:S(2)}, u32[]{:S(2)}) %collective-permute-start.5) | collective-permute-done | bytes 229408 | tf_op jit(solution)/shard_map/ppermute | solution.py:42
  53.5 15.2 %collective-permute-done.4 = bf16[128,896]{1,0:T(8,128)(2,1)S(1)} collective-permute-done((bf16[128,896]{1,0:T(8,128)(2,1)S(1)}, bf16[128,896]{1,0:T(8,128)(2,1)S(1)}, u32[]{:S(2)}, u32[]{:S(2)}) %collective-permute-start.4) | collective-permute-done | bytes 229408 | tf_op jit(solution)/shard_map/ppermute | solution.py:42
  76.4 3.9 %all-to-all-start.1 = ((bf16[8,384,128]{2,1,0:T(8,128)(2,1)}), bf16[8,384,128]{2,1,0:T(8,128)(2,1)S(1)}, u32[]{:S(2)}, u32[]{:S(2)}) async-start(bf16[8,384,128]{2,1,0:T(8,128)(2,1)} %get-tuple-element.36), calls=%async_computation.1 | async-start | bytes 1572864 | tf_op jit(solution)/shard_map/all_to_all | solution.py:753
  80.4 24.5 %all-to-all-done.1.qkv_ref = bf16[8,384,128]{2,1,0:T(8,128)(2,1)S(1)} async-done(((bf16[8,384,128]{2,1,0:T(8,128)(2,1)}), bf16[8,384,128]{2,1,0:T(8,128)(2,1)S(1)}, u32[]{:S(2)}, u32[]{:S(2)}) %all-to-all-start.1) | async-done | bytes 786464 | tf_op jit(solution)/shard_map/all_to_all | solution.py:753
  108.7 11.9 %shard_map.323 = (bf16[32,32,128]{2,1,0:T(8,128)(2,1)}, f32[64,2048]{1,0:T(8,128)S(1)}, f32[8,1,256]{2,1,0:T(1,128)S(1)}) custom-call(s32[4]{0:T(128)S(1)} %pad_add_fusion.spot_ref, s32[8,1,256]{2,1,0:T(1,128)S(1)} %bitcast.215, s32[2048,128]{1,0:T(8,128)S(1)} %broadcast_in_dim.31.seg_key_ref, bf16[8,384,128]{2,1,0:T(8,128)(2,1)S(1)} %all-to-all-done.1.qkv_ref), custom_call_target="tpu_custom_call" | custom-call | tf_op jit(solution)/shard_map/pallas_call | solution.py:205
  129.8 11.8 %all-to-all-done.2.got_ref = bf16[32,32,128]{2,1,0:T(8,128)(2,1)} async-done(((bf16[32,32,128]{2,1,0:T(8,128)(2,1)}), bf16[32,32,128]{2,1,0:T(8,128)(2,1)}, u32[]{:S(2)}, u32[]{:S(2)}) %all-to-all-start.2) | async-done | bytes 262176 | tf_op jit(solution)/shard_map/all_to_all | solution.py:785
  150.9 6.3 %collective-permute-done.11 = bf16[128,1280]{1,0:T(8,128)(2,1)} collective-permute-done((bf16[128,1280]{1,0:T(8,128)(2,1)}, bf16[128,1280]{1,0:T(8,128)(2,1)}, u32[]{:S(2)}, u32[]{:S(2)}) %collective-permute-start.11) | collective-permute-done | bytes 327712 | tf_op jit(solution)/shard_map/ppermute | solution.py:42
  182.5 3.9 %collective-permute-done.10 = bf16[128,1024]{1,0:T(8,128)(2,1)S(1)} collective-permute-done((bf16[128,1024]{1,0:T(8,128)(2,1)S(1)}, bf16[128,1024]{1,0:T(8,128)(2,1)S(1)}, u32[]{:S(2)}, u32[]{:S(2)}) %collective-permute-start.10) | collective-permute-done | bytes 262176 | tf_op jit(solution)/shard_map/ppermute | solution.py:42
  193.9 5.8 %collective-permute-done.15 = bf16[128,1024]{1,0:T(8,128)(2,1)S(1)} collective-permute-done((bf16[128,1024]{1,0:T(8,128)(2,1)S(1)}, bf16[128,1024]{1,0:T(8,128)(2,1)S(1)}, u32[]{:S(2)}, u32[]{:S(2)}) %collective-permute-start.15) | collective-permute-done | bytes 262176 | tf_op jit(solution)/shard_map/ppermute | solution.py:42
  224.8 6.1 %collective-permute-done.17.refs_10_ = bf16[128,1024]{1,0:T(8,128)(2,1)S(1)} collective-permute-done((bf16[128,1024]{1,0:T(8,128)(2,1)S(1)}, bf16[128,1024]{1,0:T(8,128)(2,1)S(1)}, u32[]{:S(2)}, u32[]{:S(2)}) %collective-permute-start.17) | collective-permute-done | bytes 262176 | tf_op jit(solution)/shard_map/ppermute | solution.py:42
  253.9 9.5 %all-to-all-done.3.up_ref = bf16[32,48,128]{2,1,0:T(8,128)(2,1)S(1)} async-done(((bf16[32,48,128]{2,1,0:T(8,128)(2,1)}), bf16[32,48,128]{2,1,0:T(8,128)(2,1)S(1)}, u32[]{:S(2)}, u32[]{:S(2)}) %all-to-all-start.3) | async-done | bytes 393248 | tf_op jit(solution)/shard_map/all_to_all | solution.py:854
  263.3 17.2 %shard_map.326 = bf16[8,384,128]{2,1,0:T(8,128)(2,1)} custom-call(s32[4]{0:T(128)S(1)} %pad_add_fusion.spot_ref, s32[8,1,256]{2,1,0:T(1,128)S(1)} %bitcast.216, s32[2048,128]{1,0:T(8,128)S(1)} %broadcast_in_dim.31.seg_key_ref, bf16[8,384,128]{2,1,0:T(8,128)(2,1)S(1)} %copy-done.3, bf16[32,48,128]{2,1,0:T(8,128)(2,1)S(1)} %all-to-all-done.3.up_ref, ...), custom_call_target="tpu_custom_call" | custom-call | tf_op jit(solution)/shard_map/pallas_call | solution.py:306
  288.7 3.7 collective-permute-start.25
  294.4 9.4 %collective-permute-done.25 = bf16[32,1024]{1,0:T(8,128)(2,1)S(1)} collective-permute-done((bf16[32,1024]{1,0:T(8,128)(2,1)}, bf16[32,1024]{1,0:T(8,128)(2,1)S(1)}, u32[]{:S(2)}, u32[]{:S(2)}) %collective-permute-start.25) | collective-permute-done | bytes 65568 | tf_op jit(solution)/shard_map/ppermute | solution.py:42
  303.7 6.9 %collective-permute-done.24 = bf16[32,1024]{1,0:T(8,128)(2,1)S(1)} collective-permute-done((bf16[32,1024]{1,0:T(8,128)(2,1)}, bf16[32,1024]{1,0:T(8,128)(2,1)S(1)}, u32[]{:S(2)}, u32[]{:S(2)}) %collective-permute-start.24) | collective-permute-done | bytes 65568 | tf_op jit(solution)/shard_map/ppermute | solution.py:42
  318.4 5.8 %collective-permute-start.30 = (bf16[4,144,768]{2,1,0:T(8,128)(2,1)S(1)}, bf16[4,144,768]{2,1,0:T(8,128)(2,1)S(1)}, u32[]{:S(2)}, u32[]{:S(2)}) collective-permute-start(bf16[4,144,768]{2,1,0:T(8,128)(2,1)S(1)} %get-tuple-element.53), channel_id=1, source_target_pairs={{0,1},{1,0},{2,3},{3,2},{4,5},{5,4},{6,7},{7,6},{8,9},{9,8},{10,11... | collective-permute-start | bytes 2654216 | tf_op jit(solution)/shard_map/ppermute | solution.py:42
  326.6 4.9 %collective-permute-start.33 = (bf16[144,768]{1,0:T(8,128)(2,1)S(1)}, bf16[144,768]{1,0:T(8,128)(2,1)S(1)}, u32[]{:S(2)}, u32[]{:S(2)}) collective-permute-start(bf16[144,768]{1,0:T(8,128)(2,1)S(1)} %get-tuple-element.77), channel_id=1, source_target_pairs={{0,6},{1,7},{2,4},{3,5},{4,2},{5,3},{6,0},{7,1},{8,14},{9,15},{10,... | collective-permute-start | bytes 663560 | tf_op jit(solution)/shard_map/ppermute | solution.py:42
  333.0 4.7 %collective-permute-start.29 = (bf16[128,1024]{1,0:T(8,128)(2,1)}, bf16[128,1024]{1,0:T(8,128)(2,1)S(1)}, u32[]{:S(2)}, u32[]{:S(2)}) collective-permute-start(bf16[128,1024]{1,0:T(8,128)(2,1)} %get-tuple-element.80), channel_id=1, source_target_pairs={{0,24},{8,16},{16,8},{24,0},{1,25},{9,17},{17,9},{25,1},{2,26},{10... | collective-permute-start | bytes 786440 | tf_op jit(solution)/shard_map/ppermute | solution.py:42
  338.5 12.3 %collective-permute-done.32 = bf16[144,768]{1,0:T(8,128)(2,1)S(1)} collective-permute-done((bf16[144,768]{1,0:T(8,128)(2,1)S(1)}, bf16[144,768]{1,0:T(8,128)(2,1)S(1)}, u32[]{:S(2)}, u32[]{:S(2)}) %collective-permute-start.32) | collective-permute-done | bytes 221216 | tf_op jit(solution)/shard_map/ppermute | solution.py:42
  356.7 5.2 %all-to-all-done.5 = bf16[4,32,1024]{2,1,0:T(8,128)(2,1)S(1)} async-done(((bf16[4,32,1024]{2,1,0:T(8,128)(2,1)}), bf16[4,32,1024]{2,1,0:T(8,128)(2,1)S(1)}, u32[]{:S(2)}, u32[]{:S(2)}) %all-to-all-start.5) | async-done | bytes 262176 | tf_op jit(solution)/shard_map/all_to_all | solution.py:837
  369.0 4.4 %all-to-all-done.6 = bf16[4,48,768]{2,1,0:T(8,128)(2,1)S(1)} async-done(((bf16[4,48,768]{2,1,0:T(8,128)(2,1)}), bf16[4,48,768]{2,1,0:T(8,128)(2,1)S(1)}, u32[]{:S(2)}, u32[]{:S(2)}) %all-to-all-start.6) | async-done | bytes 294944 | tf_op jit(solution)/shard_map/all_to_all | solution.py:898
  (310 shorter events, 163.7 us)
Async XLA Ops:
  12.0 12.8 %all-to-all-start = ((bf16[4,32,1920]{2,1,0:T(8,128)(2,1)}), bf16[4,32,1920]{2,1,0:T(8,128)(2,1)S(1)}, u32[]{:S(2)}, u32[]{:S(2)}) async-start(bf16[4,32,1920]{2,1,0:T(8,128)(2,1)} %pad_maximum_fusion.2), calls=%async_computation | async-start | bytes 983040 | tf_op jit(solution)/shard_map/all_to_all | solution.py:735
  17.1 108.0 %all-gather.3.cloned.1.call-start = ((), (), s32[]{:S(2)}) async-start(), calls=%async_computation.8 | async-start | bytes 2433024 | tf_op jit(solution)/shard_map/all_gather | solution.py:741
  28.2 12.5 %collective-permute-start.1 = (bf16[128,1024]{1,0:T(8,128)(2,1)S(1)}, bf16[128,1024]{1,0:T(8,128)(2,1)S(1)}, u32[]{:S(2)}, u32[]{:S(2)}) collective-permute-start(bf16[128,1024]{1,0:T(8,128)(2,1)S(1)} %bitcast.211), channel_id=1, source_target_pairs={{0,16},{8,24},{16,0},{24,8},{1,17},{9,25},{17,1},{25,9},{2,18},{10... | collective-permute-start | bytes 786440 | tf_op jit(solution)/shard_map/ppermute | solution.py:42
  29.6 12.2 %collective-permute-start = (bf16[128,1024]{1,0:T(8,128)(2,1)S(1)}, bf16[128,1024]{1,0:T(8,128)(2,1)S(1)}, u32[]{:S(2)}, u32[]{:S(2)}) collective-permute-start(bf16[128,1024]{1,0:T(8,128)(2,1)S(1)} %bitcast.212), channel_id=1, source_target_pairs={{0,8},{8,0},{16,24},{24,16},{1,9},{9,1},{17,25},{25,17},{2,10},{10... | collective-permute-start | bytes 786440 | tf_op jit(solution)/shard_map/ppermute | solution.py:42
  46.8 21.9 %collective-permute-start.4 = (bf16[128,896]{1,0:T(8,128)(2,1)S(1)}, bf16[128,896]{1,0:T(8,128)(2,1)S(1)}, u32[]{:S(2)}, u32[]{:S(2)}) collective-permute-start(bf16[128,896]{1,0:T(8,128)(2,1)S(1)} %fusion.106), channel_id=1, source_target_pairs={{0,4},{1,5},{2,6},{3,7},{4,0},{5,1},{6,2},{7,3},{8,12},{9,13},{10,... | collective-permute-start | bytes 688136 | tf_op jit(solution)/shard_map/ppermute | solution.py:42
  46.8 21.9 %collective-permute-start.3 = (bf16[128,896]{1,0:T(8,128)(2,1)S(1)}, bf16[128,896]{1,0:T(8,128)(2,1)S(1)}, u32[]{:S(2)}, u32[]{:S(2)}) collective-permute-start(bf16[128,896]{1,0:T(8,128)(2,1)S(1)} %fusion.106), channel_id=1, source_target_pairs={{0,2},{1,3},{2,0},{3,1},{4,6},{5,7},{6,4},{7,5},{8,10},{9,11},{10,... | collective-permute-start | bytes 688136 | tf_op jit(solution)/shard_map/ppermute | solution.py:42
  76.4 28.5 %all-to-all-start.1 = ((bf16[8,384,128]{2,1,0:T(8,128)(2,1)}), bf16[8,384,128]{2,1,0:T(8,128)(2,1)S(1)}, u32[]{:S(2)}, u32[]{:S(2)}) async-start(bf16[8,384,128]{2,1,0:T(8,128)(2,1)} %get-tuple-element.36), calls=%async_computation.1 | async-start | bytes 1572864 | tf_op jit(solution)/shard_map/all_to_all | solution.py:753
  80.3 85.5 %all-gather.5.cloned.1.call-start = ((), (), s32[]{:S(2)}) async-start(), calls=%async_computation.9 | async-start | bytes 4718592 | tf_op jit(solution)/shard_map/all_gather | solution.py:764
  121.5 20.1 %all-to-all-start.2 = ((bf16[32,32,128]{2,1,0:T(8,128)(2,1)}), bf16[32,32,128]{2,1,0:T(8,128)(2,1)}, u32[]{:S(2)}, u32[]{:S(2)}) async-start(bf16[32,32,128]{2,1,0:T(8,128)(2,1)} %get-tuple-element.37), calls=%async_computation.2 | async-start | bytes 524288 | tf_op jit(solution)/shard_map/all_to_all | solution.py:785
  124.8 226.4 %reduce-scatter.2.cloned.1.call-start = ((), (), s32[]{:S(2)}) async-start(), calls=%async_computation.10 | async-start | bytes 4718592 | tf_op jit(solution)/shard_map/reduce_scatter | solution.py:833
  147.8 14.8 %collective-permute-start.9 = (bf16[128,1280]{1,0:T(8,128)(2,1)}, bf16[128,1280]{1,0:T(8,128)(2,1)}, u32[]{:S(2)}, u32[]{:S(2)}) collective-permute-start(bf16[128,1280]{1,0:T(8,128)(2,1)} %get-tuple-element.74), channel_id=1, source_target_pairs={{0,16},{8,24},{16,0},{24,8},{1,17},{9,25},{17,1},{25,9},{2,18},{10... | collective-permute-start | bytes 983048 | tf_op jit(solution)/shard_map/ppermute | solution.py:42
  148.3 15.9 %collective-permute-start.7 = (bf16[128,1280]{1,0:T(8,128)(2,1)}, bf16[128,1280]{1,0:T(8,128)(2,1)}, u32[]{:S(2)}, u32[]{:S(2)}) collective-permute-start(bf16[128,1280]{1,0:T(8,128)(2,1)} %get-tuple-element.72), channel_id=1, source_target_pairs={{0,8},{8,0},{16,24},{24,16},{1,9},{9,1},{17,25},{25,17},{2,10},{10... | collective-permute-start | bytes 983048 | tf_op jit(solution)/shard_map/ppermute | solution.py:42
  190.8 12.7 %collective-permute-start.14 = (bf16[128,1024]{1,0:T(8,128)(2,1)S(1)}, bf16[128,1024]{1,0:T(8,128)(2,1)S(1)}, u32[]{:S(2)}, u32[]{:S(2)}) collective-permute-start(bf16[128,1024]{1,0:T(8,128)(2,1)S(1)} %get-tuple-element.65), channel_id=1, source_target_pairs={{0,16},{8,24},{16,0},{24,8},{1,17},{9,25},{17,1},{25,9},{2,18},{10... | collective-permute-start | bytes 786440 | tf_op jit(solution)/shard_map/ppermute | solution.py:42
  217.3 13.6 %collective-permute-start.17 = (bf16[128,1024]{1,0:T(8,128)(2,1)S(1)}, bf16[128,1024]{1,0:T(8,128)(2,1)S(1)}, u32[]{:S(2)}, u32[]{:S(2)}) collective-permute-start(bf16[128,1024]{1,0:T(8,128)(2,1)S(1)} %convolution_convert_fusion.4), channel_id=1, source_target_pairs={{0,16},{8,24},{16,0},{24,8},{1,17},{9,25},{17,1},{25,9},{2,18},{10... | collective-permute-start | bytes 786440 | tf_op jit(solution)/shard_map/ppermute | solution.py:42
  241.1 22.2 %all-to-all-start.3 = ((bf16[32,48,128]{2,1,0:T(8,128)(2,1)}), bf16[32,48,128]{2,1,0:T(8,128)(2,1)S(1)}, u32[]{:S(2)}, u32[]{:S(2)}) async-start(bf16[32,48,128]{2,1,0:T(8,128)(2,1)} %get-tuple-element.44), calls=%async_computation.3 | async-start | bytes 786432 | tf_op jit(solution)/shard_map/all_to_all | solution.py:854
  280.5 33.9 %all-to-all-start.4 = ((bf16[8,384,128]{2,1,0:T(8,128)(2,1)}), bf16[8,384,128]{2,1,0:T(8,128)(2,1)S(1)}, u32[]{:S(2)}, u32[]{:S(2)}) async-start(bf16[8,384,128]{2,1,0:T(8,128)(2,1)} %shard_map.326), calls=%async_computation.4 | async-start | bytes 1572864 | tf_op jit(solution)/shard_map/all_to_all | solution.py:870
  288.7 15.0 %collective-permute-start.25 = (bf16[32,1024]{1,0:T(8,128)(2,1)}, bf16[32,1024]{1,0:T(8,128)(2,1)S(1)}, u32[]{:S(2)}, u32[]{:S(2)}) collective-permute-start(bf16[32,1024]{1,0:T(8,128)(2,1)} %get-tuple-element.93), channel_id=1, source_target_pairs={{0,6},{1,7},{2,4},{3,5},{4,2},{5,3},{6,0},{7,1},{8,14},{9,15},{10,... | collective-permute-start | bytes 196616 | tf_op jit(solution)/shard_map/ppermute | solution.py:42
  292.4 18.3 %collective-permute-start.24 = (bf16[32,1024]{1,0:T(8,128)(2,1)}, bf16[32,1024]{1,0:T(8,128)(2,1)S(1)}, u32[]{:S(2)}, u32[]{:S(2)}) collective-permute-start(bf16[32,1024]{1,0:T(8,128)(2,1)} %get-tuple-element.94), channel_id=1, source_target_pairs={{0,4},{1,5},{2,6},{3,7},{4,0},{5,1},{6,2},{7,3},{8,12},{9,13},{10,... | collective-permute-start | bytes 196616 | tf_op jit(solution)/shard_map/ppermute | solution.py:42
  292.4 18.3 %collective-permute-start.23 = (bf16[32,1024]{1,0:T(8,128)(2,1)S(1)}, bf16[32,1024]{1,0:T(8,128)(2,1)}, u32[]{:S(2)}, u32[]{:S(2)}) collective-permute-start(bf16[32,1024]{1,0:T(8,128)(2,1)S(1)} %get-tuple-element.92), channel_id=1, source_target_pairs={{0,2},{1,3},{2,0},{3,1},{4,6},{5,7},{6,4},{7,5},{8,10},{9,11},{10,... | collective-permute-start | bytes 196616 | tf_op jit(solution)/shard_map/ppermute | solution.py:42
  331.5 19.3 %collective-permute-start.32 = (bf16[144,768]{1,0:T(8,128)(2,1)S(1)}, bf16[144,768]{1,0:T(8,128)(2,1)S(1)}, u32[]{:S(2)}, u32[]{:S(2)}) collective-permute-start(bf16[144,768]{1,0:T(8,128)(2,1)S(1)} %get-tuple-element.78), channel_id=1, source_target_pairs={{0,4},{1,5},{2,6},{3,7},{4,0},{5,1},{6,2},{7,3},{8,12},{9,13},{10,... | collective-permute-start | bytes 663560 | tf_op jit(solution)/shard_map/ppermute | solution.py:42
  331.5 19.3 %collective-permute-start.31 = (bf16[144,768]{1,0:T(8,128)(2,1)S(1)}, bf16[144,768]{1,0:T(8,128)(2,1)S(1)}, u32[]{:S(2)}, u32[]{:S(2)}) collective-permute-start(bf16[144,768]{1,0:T(8,128)(2,1)S(1)} %get-tuple-element.76), channel_id=1, source_target_pairs={{0,2},{1,3},{2,0},{3,1},{4,6},{5,7},{6,4},{7,5},{8,10},{9,11},{10,... | collective-permute-start | bytes 663560 | tf_op jit(solution)/shard_map/ppermute | solution.py:42
  333.0 34.9 %collective-permute-start.29 = (bf16[128,1024]{1,0:T(8,128)(2,1)}, bf16[128,1024]{1,0:T(8,128)(2,1)S(1)}, u32[]{:S(2)}, u32[]{:S(2)}) collective-permute-start(bf16[128,1024]{1,0:T(8,128)(2,1)} %get-tuple-element.80), channel_id=1, source_target_pairs={{0,24},{8,16},{16,8},{24,0},{1,25},{9,17},{17,9},{25,1},{2,26},{10... | collective-permute-start | bytes 786440 | tf_op jit(solution)/shard_map/ppermute | solution.py:42
  337.8 30.2 %collective-permute-start.28 = (bf16[128,1024]{1,0:T(8,128)(2,1)}, bf16[128,1024]{1,0:T(8,128)(2,1)S(1)}, u32[]{:S(2)}, u32[]{:S(2)}) collective-permute-start(bf16[128,1024]{1,0:T(8,128)(2,1)} %get-tuple-element.81), channel_id=1, source_target_pairs={{0,16},{8,24},{16,0},{24,8},{1,17},{9,25},{17,1},{25,9},{2,18},{10... | collective-permute-start | bytes 786440 | tf_op jit(solution)/shard_map/ppermute | solution.py:42
  337.9 30.1 %collective-permute-start.27 = (bf16[128,1024]{1,0:T(8,128)(2,1)S(1)}, bf16[128,1024]{1,0:T(8,128)(2,1)S(1)}, u32[]{:S(2)}, u32[]{:S(2)}) collective-permute-start(bf16[128,1024]{1,0:T(8,128)(2,1)S(1)} %get-tuple-element.79), channel_id=1, source_target_pairs={{0,8},{8,0},{16,24},{24,16},{1,9},{9,1},{17,25},{25,17},{2,10},{10... | collective-permute-start | bytes 786440 | tf_op jit(solution)/shard_map/ppermute | solution.py:42
  (68 other events, 666.5 us)
Sparse Core Ops, SparseCore 0:
  26.8 67.0 all-gather.2
  108.1 50.9 all-gather.4
  210.9 55.1 reduce-scatter.1

commit v4 on v3

--- a/solution.py
+++ b/solution.py
@@ -347,10 +347,11 @@
 
 def join_kernel(
     seqs, heads_here, repeats, spot_ref, got_ref, tokens_ref, flags_ref, mat_ref, vectors_ref,
-    sent_ref, normed_ref, unit_ref, inv_ref, squares_ref, attn,
+    *refs,
 ):
+    sents, (normed_ref, unit_ref, inv_ref, squares_ref, attn) = refs[:-5], refs[-5:]
     my_group, part = spot_ref[1], spot_ref[3]
-    groups = sent_ref.shape[0]
+    groups = len(sents)
     wide = got_ref.shape[1]
     width = tokens_ref.shape[1]
     width_here = heads_here * HEAD_DIM
@@ -377,12 +378,12 @@
     inv_ref[...] = jnp.broadcast_to(inv_std, inv_ref.shape)
     low = normed.astype(BF16)
     for k in range(groups):
-        sent_ref[k, :, 0:width] = low
+        sents[k][:, 0:width] = low
         for group in range(groups):
 
             @pl.when((my_group ^ k) == group)
             def _():
-                sent_ref[k, :, width:] = attn[:, group * width_here : (group + 1) * width_here]
+                sents[k][:, width:] = attn[:, group * width_here : (group + 1) * width_here]
 
     lane = lax.broadcasted_iota(jnp.int32, squares_ref.shape, 1)
     total = jnp.zeros(squares_ref.shape, F32)
@@ -399,9 +400,9 @@
     return pl.pallas_call(
         functools.partial(join_kernel, seqs, heads_here, repeats),
         in_specs=[pl.BlockSpec(memory_space=pltpu.SMEM)] + [vmem] * 5,
-        out_specs=[vmem] * 5,
-        out_shape=[
-            jax.ShapeDtypeStruct((groups, rows, width + heads_here * HEAD_DIM), BF16),
+        out_specs=[vmem] * (groups + 4),
+        out_shape=[jax.ShapeDtypeStruct((rows, width + heads_here * HEAD_DIM), BF16)] * groups
+        + [
             jax.ShapeDtypeStruct((rows, width), F32),
             jax.ShapeDtypeStruct((rows, width), F32),
             jax.ShapeDtypeStruct((rows, 128), F32),
@@ -410,6 +411,47 @@
         scratch_shapes=[pltpu.VMEM((rows, width), BF16)],
         compiler_params=pltpu.CompilerParams(vmem_limit_bytes=32 * 1024 * 1024),
     )(spot, got, tokens, flags, mat_out, vectors)
+
+
+def middle_kernel(others, *refs):
+    own_ref, normed_ref, vectors_ref, flags_ref, up_ref, squares_ref = refs[:6]
+    parts = refs[6 : 6 + others]
+    out_ref, resid_ref, low_ref, early_ref, total_ref = refs[6 + others :]
+    ffn = own_ref[...]
+    for part in parts:
+        ffn = ffn + part[...].astype(F32)
+    ffn = ffn + vectors_ref[1:2, :]
+    gain = vectors_ref[4:5, :]
+    normed, unit, inv_std = layer_norm(normed_ref[...] + ffn, gain, vectors_ref[5:6, :])
+    out_ref[...] = normed.astype(BF16)
+    upstream = up_ref[...].astype(F32)
+    grad_resid = norm_back(upstream, unit, inv_std, gain)
+    resid_ref[...] = grad_resid
+    low = grad_resid.astype(BF16)
+    low_ref[...] = low
+    early_ref[0:1, :] = jnp.sum(low.astype(F32), axis=0, keepdims=True)
+    early_ref[1:2, :] = jnp.sum(upstream * unit, axis=0, keepdims=True)
+    early_ref[2:3, :] = jnp.sum(upstream, axis=0, keepdims=True)
+    size = flags_ref[...] * jnp.sum(ffn * ffn, axis=1, keepdims=True)
+    lane = lax.broadcasted_iota(jnp.int32, total_ref.shape, 1)
+    total_ref[...] = squares_ref[...] + jnp.where(
+        lane == 3, jnp.sum(size, axis=0, keepdims=True), 0.0
+    )
+
+
+def middle(own, others, normed, vectors, flags, upstream, squares):
+    rows, width = own.shape
+    return whole_call(
+        functools.partial(middle_kernel, len(others)),
+        [
+            jax.ShapeDtypeStruct((rows, width), BF16),
+            jax.ShapeDtypeStruct((rows, width), F32),
+            jax.ShapeDtypeStruct((rows, width), BF16),
+            jax.ShapeDtypeStruct((8, width), F32),
+            jax.ShapeDtypeStruct((1, 128), F32),
+        ],
+        (own, normed, vectors, flags, upstream, squares, *others),
+    )
 
 
 def branch_back_kernel(
@@ -487,8 +529,27 @@
     )(spot, own, resid, unit, inv_std, gain, mat_out, early, up_sums, squares, *others)
 
 
+def pack_kernel(*refs):
+    out_ref = refs[-1]
+    rows = [jnp.zeros((1, 128), F32) for _ in range(out_ref.shape[0])]
+    start = 0
+    for ref in refs[:-1]:
+        size = ref.shape[1]
+        pieces = [ref[...].astype(F32)]
+        if start % 128:
+            pieces = [jnp.zeros((1, start % 128), F32)] + pieces
+        if start % 128 + size < 128:
+            pieces = pieces + [jnp.zeros((1, 128 - start % 128 - size), F32)]
+        piece = jnp.concatenate(pieces, axis=1) if len(pieces) > 1 else pieces[0]
+        rows[start // 128] = rows[start // 128] + piece
+        start += size
+    out_ref[...] = jnp.concatenate(rows, axis=0).astype(BF16)
+
+
 def project_kernel(groups, heads_here, repeats, spot_ref, *refs):
-    tokens, (mine_ref, other_ref, sent_ref, all_ref, mat_ref, values) = refs[:groups], refs[groups:]
+    tokens, (mine_ref, other_ref, sent_ref, all_ref, mat_ref, short_ref, values) = (
+        refs[:groups], refs[groups:]
+    )
     my_block, my_group = spot_ref[0], spot_ref[1]
     halves, chip_rows, _ = mine_ref.shape
     blocks = 2 * halves
@@ -512,6 +573,15 @@
         def _():
             mat_ref[spot, :] = other_ref[place // 2, :, 0 : 3 * width_here]
 
+    for b in range(blocks):
+        place = my_block ^ b
+        vectors = jnp.where(
+            place % 2 == 0,
+            mine_ref[place // 2, :, 3 * width_here :].astype(F32),
+            other_ref[place // 2, :, 3 * width_here :].astype(F32),
+        )
+        for group in range(groups):
+            short_ref[b * groups + group] = vectors[group * dim_rows : group * dim_rows + 8]
     lane = lax.broadcasted_iota(jnp.int32, (1, 128), 1)
     tiles = width_here // 128
     biases = [[jnp.zeros((1, 128), F32) for _ in range(tiles)] for _ in range(2)]
@@ -562,11 +632,12 @@
     return pl.pallas_call(
         functools.partial(project_kernel, groups, heads_here, repeats),
         in_specs=[pl.BlockSpec(memory_space=pltpu.SMEM)] + [vmem] * (groups + 2),
-        out_specs=[vmem] * 3,
+        out_specs=[vmem] * 4,
         out_shape=[
             jax.ShapeDtypeStruct((blocks, block_rows * 3 // 2, 128), BF16),
             jax.ShapeDtypeStruct((groups * rows, width), BF16),
             jax.ShapeDtypeStruct((width, 3 * heads_here * HEAD_DIM), BF16),
+            jax.ShapeDtypeStruct((blocks * groups, 8, 128), F32),
         ],
         scratch_shapes=[pltpu.VMEM((groups * rows, heads_here * HEAD_DIM), F32)],
         compiler_params=pltpu.CompilerParams(vmem_limit_bytes=40 * 1024 * 1024),
@@ -672,6 +743,186 @@
     )(spot, got, mat_three, token_all)
 
 
+def whole_call(kernel, out_shape, arguments, scratch=(), megabytes=40):
+    vmem = pl.BlockSpec(memory_space=pltpu.VMEM)
+    return pl.pallas_call(
+        kernel,
+        in_specs=[vmem] * len(arguments),
+        out_specs=[vmem] * len(out_shape),
+        out_shape=out_shape,
+        scratch_shapes=list(scratch),
+        compiler_params=pltpu.CompilerParams(vmem_limit_bytes=megabytes * 1024 * 1024),
+    )(*arguments)
+
+
+def ffn_kernel(sent_ref, up_ref, down_ref, bias_ref, out_ref, act_ref, slope_ref):
+    hidden = matmul(sent_ref[:, : up_ref.shape[0]], up_ref[...]) + bias_ref[...]
+    cdf_part = 0.5 * (1.0 + lax.erf(hidden * 0.7071067811865476))
+    act = (hidden * cdf_part).astype(BF16)
+    act_ref[...] = act
+    slope_ref[...] = cdf_part + hidden * (
+        jnp.exp(-0.5 * hidden * hidden) * 0.3989422804014327
+    )
+    out_ref[...] = matmul(act, down_ref[...]).astype(out_ref.dtype)
+
+
+def ffn_part(sent, mat_up, mat_down, vec_up, kind):
+    rows = sent.shape[0]
+    units, width = mat_down.shape
+    return whole_call(
+        ffn_kernel,
+        [
+            jax.ShapeDtypeStruct((rows, width), kind),
+            jax.ShapeDtypeStruct((rows, units), BF16),
+            jax.ShapeDtypeStruct((rows, units), F32),
+        ],
+        (sent, mat_up, mat_down, vec_up),
+    )
+
+
+def ffn_back_kernel(grad_ref, slope_ref, up_ref, down_ref, out_ref, hidden_ref):
+    grad_hidden = (matmul_nt(grad_ref[...], down_ref[...]) * slope_ref[...]).astype(BF16)
+    hidden_ref[...] = grad_hidden
+    out_ref[...] = matmul_nt(grad_hidden, up_ref[...]).astype(out_ref.dtype)
+
+
+def ffn_back_part(grad, slope, mat_up, mat_down, kind):
+    rows, width = grad.shape
+    return whole_call(
+        ffn_back_kernel,
+        [
+            jax.ShapeDtypeStruct((rows, width), kind),
+            jax.ShapeDtypeStruct(slope.shape, BF16),
+        ],
+        (grad, slope, mat_up, mat_down),
+    )
+
+
+def ffn_grads_kernel(groups, blocks, *refs):
+    acts, grads, sents, hiddens = [refs[i * groups : (i + 1) * groups] for i in range(4)]
+    *outs, sums_ref, left, right = refs[4 * groups :]
+    rows, width = grads[0].shape
+    units = acts[0].shape[1]
+    for k in range(groups):
+        spot = slice(k * rows, (k + 1) * rows)
+        left[spot, 0:units] = acts[k][...]
+        right[spot, 0:width] = grads[k][...]
+    result = matmul_tn(left[:, 0:units], right[:, 0:width])
+    chunk = units // blocks
+    for b in range(blocks):
+        outs[0][b, 0:chunk, :] = result[b * chunk : (b + 1) * chunk].astype(BF16)
+    for k in range(groups):
+        spot = slice(k * rows, (k + 1) * rows)
+        left[spot, 0:width] = sents[k][:, 0:width]
+        right[spot, 0:units] = hiddens[k][...]
+    result = matmul_tn(left[:, 0:width], right[:, 0:units])
+    chunk = width // blocks
+    for b in range(blocks):
+        block = result[b * chunk : (b + 1) * chunk].astype(BF16)
+        if len(outs) == 1:
+            outs[0][b, units // blocks :, :] = block
+        else:
+            outs[1][b] = block
+    sums_ref[...] = jnp.sum(right[:, 0:units].astype(F32), axis=0, keepdims=True)
+
+
+def ffn_grads_call(acts, grads, sents, hiddens, blocks):
+    groups = len(acts)
+    rows, width = grads[0].shape
+    units = acts[0].shape[1]
+    big = pltpu.VMEM((groups * rows, max(units, width)), BF16)
+    if units == width:
+        shapes = [jax.ShapeDtypeStruct((blocks, (units + width) // blocks, width), BF16)]
+    else:
+        shapes = [
+            jax.ShapeDtypeStruct((blocks, units // blocks, width), BF16),
+            jax.ShapeDtypeStruct((blocks, width // blocks, units), BF16),
+        ]
+    return whole_call(
+        functools.partial(ffn_grads_kernel, groups, blocks),
+        shapes + [jax.ShapeDtypeStruct((1, units), F32)],
+        (*acts, *grads, *sents, *hiddens),
+        (big, big),
+    )
+
+
+def split_kernel(own_ref, *outs):
+    groups = own_ref.shape[0]
+    dim_rows = outs[0].shape[0]
+    columns = own_ref.shape[2] // 3
+    total = jnp.zeros(outs[3].shape, F32)
+    for group in range(groups):
+        block = own_ref[group].astype(F32)
+        for which in range(3):
+            outs[which][:, group * columns : (group + 1) * columns] = block[
+                :dim_rows, which * columns : (which + 1) * columns
+            ]
+        total = total + block[dim_rows : dim_rows + 8, 0:128]
+    outs[3][...] = total
+
+
+def split_columns(own, dim_rows):
+    groups, _, columns = own.shape
+    matrix = jax.ShapeDtypeStruct((dim_rows, groups * columns // 3), F32)
+    return whole_call(split_kernel, [matrix] * 3 + [jax.ShapeDtypeStruct((8, 128), F32)], (own,))
+
+
+def place_kernel(groups, blocks, spot_ref, *refs):
+    parts, out_ref = refs[:groups], refs[groups]
+    chunk = parts[0].shape[1] // blocks
+    for k in range(groups):
+        for group in range(groups):
+
+            @pl.when((spot_ref[1] ^ k) == group)
+            def _():
+                for b in range(blocks):
+                    start = (b * groups + group) * chunk
+                    out_ref[:, start : start + chunk] = parts[k][
+                        :, b * chunk : (b + 1) * chunk
+                    ].astype(F32)
+
+
+def place_columns(spot, parts, blocks):
+    groups = len(parts)
+    rows, columns = parts[0].shape
+    chunk = columns // blocks
+    if chunk % 128:
+        whole = xor_order(jnp.stack(parts), 0, spot[1]).reshape(groups, rows, blocks, chunk)
+        return jnp.transpose(whole, (1, 2, 0, 3)).reshape(rows, groups * columns).astype(F32)
+    vmem = pl.BlockSpec(memory_space=pltpu.VMEM)
+    return pl.pallas_call(
+        functools.partial(place_kernel, groups, blocks),
+        in_specs=[pl.BlockSpec(memory_space=pltpu.SMEM)] + [vmem] * groups,
+        out_specs=vmem,
+        out_shape=jax.ShapeDtypeStruct((rows, groups * columns), F32),
+    )(spot, *parts)
+
+
+def out_grads_kernel(groups, *refs):
+    sents, grads, (out_ref, left, right) = refs[:groups], refs[groups : 2 * groups], refs[2 * groups :]
+    rows, width = grads[0].shape
+    for k in range(groups):
+        spot = slice(k * rows, (k + 1) * rows)
+        left[spot, :] = sents[k][:, width:]
+        right[spot, :] = grads[k][...]
+    out_ref[...] = matmul_tn(left[...], right[...]).astype(BF16)
+
+
+def out_grads_call(sents, grads):
+    groups = len(sents)
+    rows, width = grads[0].shape
+    columns = sents[0].shape[1] - width
+    return whole_call(
+        functools.partial(out_grads_kernel, groups),
+        [jax.ShapeDtypeStruct((columns, width), BF16)],
+        (*sents, *grads),
+        (
+            pltpu.VMEM((groups * rows, columns), BF16),
+            pltpu.VMEM((groups * rows, width), BF16),
+        ),
+    )[0]
+
+
 def per_device(
     tokens,
     cotangent,
@@ -722,11 +973,12 @@
         [w.reshape(dim_rows, groups, width_here) for w in (w_query, w_key, w_value)], axis=-1
     )
     w_three = jnp.transpose(w_three, (1, 0, 2))
-    def lanes_of(pieces):
-        flat = jnp.concatenate(pieces)
-        return jnp.pad(flat, (0, dim_rows * 128 - flat.shape[0])).reshape(dim_rows, 128)
-
-    vectors = lanes_of([b_query, b_value])
+    short = [b_query, b_value, b_out, b_fc2, gain_attn, bias_attn, gain_ffn, bias_ffn, b_fc1]
+    vectors = whole_call(
+        pack_kernel,
+        [jax.ShapeDtypeStruct((dim_rows, 128), BF16)],
+        [item[None] for item in short],
+    )[0]
     w_up = w_fc1.reshape(dim_rows, blocks, groups, unit_rows)
     w_up = jnp.transpose(w_up, (2, 0, 1, 3)).reshape(groups, dim_rows, units_here)
     first = jnp.concatenate(
@@ -736,30 +988,27 @@
     first = first.reshape(groups * dim_rows, first.shape[-1])
     second = first[:, 3 * width_here + 128 :].reshape(-1, width)
     second = jnp.concatenate([second, w_fc2])
-    third = lanes_of([b_out, b_fc2, gain_attn, bias_attn, gain_ffn, bias_ffn, b_fc1])
-    third = after(jnp.concatenate([w_out, third], axis=1), first)
-    third = lax.all_gather(third, ALL, axis=0, tiled=False)
+    mat_out = lax.all_gather(w_out, ALL, axis=0, tiled=True)
 
     first = first[:, : 3 * width_here + 128]
     for part in token_parts[1:]:
-        first = after(first, part)
+        second = after(second, part)
     mine, other = gather_blk_parts(first, second)
     part_blocks = blocks // repeats
     first_turn = my_block % repeats * (parts_length // QUERY_ROWS)
     spot = jnp.stack([my_block, my_group, first_turn, my_block // part_blocks]).astype(jnp.int32)
-    sent, token_all, mat_three = project(
+    sent, token_all, mat_three, short = project(
         spot, token_parts, mine, other, seqs, heads_here, repeats
     )
     qkv = lax.all_to_all(sent, "blk", split_axis=0, concat_axis=0, tiled=True)
 
 
-    mat_out = third[..., :width].reshape(width, width)
-    vectors = third[..., width:].reshape(devices, dim_rows * 128)[:, : 6 * dim_rows + unit_rows]
-    short = jnp.transpose(vectors[:, : 6 * dim_rows].reshape(devices, 6, dim_rows), (1, 0, 2))
-    short = short.reshape(6, width).astype(F32)
+    vectors = short.reshape(devices, 8 * 128)
+    vec_up = vectors[:, 8 * dim_rows : 8 * dim_rows + unit_rows].reshape(blocks, groups, unit_rows)
+    vec_up = lax.dynamic_index_in_dim(vec_up, my_group, 1, False).reshape(units_here)
+    short = vectors[:, 2 * dim_rows : 8 * dim_rows].reshape(devices, 6, dim_rows)
+    short = jnp.transpose(short, (1, 0, 2)).reshape(6, width)
     vec_out, vec_down, gain_one, bias_one, gain_two, bias_two = [short[i] for i in range(6)]
-    vec_up = vectors[:, 6 * dim_rows :].reshape(blocks, groups, unit_rows)
-    vec_up = lax.dynamic_index_in_dim(vec_up, my_group, 1, False).reshape(units_here).astype(F32)
 
     second = lax.all_gather(after(second, qkv), "blk", axis=0, tiled=False)
     up_rows = groups * dim_rows * units_here // width
@@ -786,70 +1035,50 @@
     my_span = my_block * groups + my_group
     local_flags = lax.dynamic_slice_in_dim(valid_flags, my_span * span, span, 1)
     local_flags = local_flags.reshape(rows, 1).astype(F32)
-    sent, normed_one, unit_one, inv_one, squares = join(
+    *sent, normed_one, unit_one, inv_one, squares = join(
         spot, got, token_rows, local_flags, mat_out, short, seqs, heads_here, repeats
     )
     joint_parts = [sent[0]] + [swapped(sent[k], "heads", k) for k in range(1, groups)]
-    normed_parts = [part[:, :width] for part in joint_parts]
-    attn_parts = [part[:, width:] for part in joint_parts]
-    hidden_parts = [matmul(part, mat_up) + vec_up for part in normed_parts]
-    act_parts = [jax.nn.gelu(part, approximate=False).astype(BF16) for part in hidden_parts]
-    ffn_parts = [matmul(part, mat_down) for part in act_parts]
-    ffn = scatter_parts(ffn_parts, "heads") + vec_down
-    normed_two, unit_two, inv_two = layer_norm(normed_one + ffn, gain_two, bias_two)
-    output = normed_two.astype(BF16).reshape(tokens.shape)
-    last = jnp.sum(local_flags * jnp.sum(ffn * ffn, axis=1, keepdims=True))
-    squares = squares + jnp.where(jnp.arange(128) == 3, last, 0.0)[None]
-
-    upstream = cotangent.reshape(rows, width).astype(F32)
-    grad_gain_two = jnp.sum(upstream * unit_two, axis=0)
-    grad_bias_two = jnp.sum(upstream, axis=0)
-    grad_resid_two = norm_back(upstream, unit_two, inv_two, gain_two)
-    grad_ffn = grad_resid_two.astype(BF16)
-    grad_vec_down = jnp.sum(grad_ffn.astype(F32), axis=0)
+    ffn_results = [
+        ffn_part(part, mat_up, mat_down, vec_up[None], F32 if k == 0 else BF16)
+        for k, part in enumerate(joint_parts)
+    ]
+    ffn_others = [swapped(ffn_results[k][0], "heads", k) for k in range(1, groups)]
+    output, grad_resid_two, grad_ffn, early, squares = middle(
+        ffn_results[0][0], ffn_others, normed_one, short, local_flags,
+        cotangent.reshape(rows, width), squares,
+    )
+    output = output.reshape(tokens.shape)
     grad_ffn_parts = gather_parts(grad_ffn, "heads")
-    grad_hidden_parts = [
-        (matmul_nt(part, mat_down) * gelu_slope(hidden)).astype(BF16)
-        for part, hidden in zip(grad_ffn_parts, hidden_parts)
+    grad_results = [
+        ffn_back_part(part, item[2], mat_up, mat_down, F32 if k == 0 else BF16)
+        for k, (part, item) in enumerate(zip(grad_ffn_parts, ffn_results))
     ]
-    grad_normed_parts = [matmul_nt(part, mat_up) for part in grad_hidden_parts]
-    grad_normed_others = [
-        swapped(grad_normed_parts[k].astype(BF16), "heads", k) for k in range(1, groups)
+    grad_normed_parts = [item[0] for item in grad_results]
+    grad_normed_others = [swapped(grad_normed_parts[k], "heads", k) for k in range(1, groups)]
+    *ffn_grads, grad_vec_up = ffn_grads_call(
+        [item[1] for item in ffn_results],
+        grad_ffn_parts,
+        joint_parts,
+        [after(grad_results[0][1], grad_normed_others[-1])] + [item[1] for item in grad_results[1:]],
+        blocks,
+    )
+    ffn_grads = [
+        lax.psum_scatter(
+            item.reshape(-1, item.shape[-1]), "blk", scatter_dimension=0, tiled=True
+        )
+        for item in ffn_grads
     ]
-    grad_ffn_all = jnp.concatenate(grad_ffn_parts, axis=0)
-    grad_hidden = jnp.concatenate(grad_hidden_parts, axis=0)
-    grad_vec_up = jnp.sum(grad_hidden.astype(F32), axis=0)
-    act_low = jnp.concatenate(act_parts, axis=0)
-    normed_all = jnp.concatenate(normed_parts, axis=0)
-    grad_mat_down = matmul_tn(act_low, grad_ffn_all).astype(BF16)
-    grad_mat_up = matmul_tn(normed_all, grad_hidden).astype(BF16)
-    ffn_grads = jnp.concatenate(
-        [
-            grad_mat_down.reshape(blocks, unit_rows, width),
-            grad_mat_up.reshape(blocks, -1, width),
-        ],
-        axis=1,
-    )
-    ffn_grads = lax.psum_scatter(
-        ffn_grads.reshape(-1, width), "blk", scatter_dimension=0, tiled=True
-    )
-    shard_down = ffn_grads[:unit_rows].astype(F32)
-    shard_up = lax.all_to_all(
-        ffn_grads[unit_rows:].reshape(groups, dim_rows, units_here),
-        "heads",
-        split_axis=0,
-        concat_axis=0,
-        tiled=True,
-    )
-    shard_up = jnp.transpose(
-        shard_up.reshape(groups, dim_rows, blocks, unit_rows), (1, 2, 0, 3)
-    ).reshape(dim_rows, hidden_size)
-    shard_up = shard_up.astype(F32)
+    if units_here == width:
+        shard_down, shard_up = ffn_grads[0][:unit_rows], ffn_grads[0][unit_rows:]
+    else:
+        shard_down, shard_up = ffn_grads
+    shard_down = shard_down.astype(F32)
 
     sent, grad_resid_one, grad_branch = branch_back(
         spot, grad_normed_parts[0], grad_normed_others, grad_resid_two, unit_one, inv_one,
-        gain_one[None], mat_out, jnp.stack([grad_vec_down, grad_gain_two, grad_bias_two]),
-        grad_vec_up[None], squares, seqs, heads_here, repeats, devices,
+        gain_one[None], mat_out, early,
+        grad_vec_up, squares, seqs, heads_here, repeats, devices,
     )
     got = lax.all_to_all(sent, ALL, split_axis=0, concat_axis=0, tiled=True)
     small = jnp.sum(got[:, wide:].astype(F32), axis=0)
@@ -859,16 +1088,17 @@
     real_count = jnp.maximum(jnp.sum(valid_flags.astype(F32)), 1.0)
     rms = jnp.sqrt(small[7, :4] / (real_count * width))
 
-    branch_parts = gather_parts(grad_branch, "heads")
-    grad_mat_out = matmul_tn(
-        jnp.concatenate(attn_parts, axis=0), jnp.concatenate(branch_parts, axis=0)
-    ).astype(BF16)
-    shard_out = scatter_blk(grad_mat_out.reshape(blocks, dim_rows, width)).astype(BF16)
+    grads = attend_back(spot, seg_row, seg_key, qkv, got, attn_t, lse)
+    branch_parts = gather_parts(after(grad_branch, grads), "heads")
+    grad_mat_out = out_grads_call(joint_parts, branch_parts)
+    got = lax.all_to_all(grads, "blk", split_axis=0, concat_axis=0, tiled=True)
+    shard_out = scatter_blk(after(grad_mat_out, got).reshape(blocks, dim_rows, width)).astype(BF16)
     route = [(j, j % groups * blocks + j // groups) for j in range(devices)]
     shard_out = lax.ppermute(shard_out, ("heads", "blk"), route)
-    grads = attend_back(spot, seg_row, seg_key, qkv, got, attn_t, lse)
-    got = lax.all_to_all(grads, "blk", split_axis=0, concat_axis=0, tiled=True)
-    got = after(got, shard_out)
+    shard_up = after(shard_up, got).reshape(groups, dim_rows, units_here)
+    shard_up = xor_order(shard_up, 0, my_group)
+    up_parts = [shard_up[0]] + [swapped(shard_up[k], "heads", k) for k in range(1, groups)]
+    shard_up = place_columns(spot, up_parts, blocks)
     own_input, other_input, keep, send = input_grads(
         spot, got, mat_three, token_all, heads_here, groups, repeats
     )
@@ -894,15 +1124,11 @@
     )
     own_sums = jnp.where(row == 0, own_sums[:, None, :], 0.0)
     own = jnp.concatenate([own_rows, own_sums], axis=1).astype(BF16)
-    own = after(own, shard_up)
-    own = lax.all_to_all(own, "heads", split_axis=0, concat_axis=0, tiled=True).astype(F32)
-    shard_sums = jnp.sum(own[:, dim_rows, : 2 * dim_rows], axis=0)
-    shards_three = [
-        jnp.transpose(
-            own[:, :dim_rows, which * width_here : (which + 1) * width_here], (1, 0, 2)
-        ).reshape(dim_rows, width)
-        for which in range(3)
-    ]
+    for part in up_parts[1:]:
+        own = after(own, part)
+    own = lax.all_to_all(own, "heads", split_axis=0, concat_axis=0, tiled=True)
+    shards_three = split_columns(own, dim_rows)
+    shard_sums = shards_three[3][0]
 
     return (
         output,
@@ -914,7 +1140,7 @@
         shard_up,
         shard_down,
         shard_sums[:dim_rows],
-        shard_sums[dim_rows:],
+        shard_sums[dim_rows : 2 * dim_rows],
         vector_sums[0],
         shard_vec_up,
         vector_sums[3],

time: 384 us -> 350 us (0.911)
  waiting for transfers between devices: 161 us -> 120 us
  matrix products: 23.7 us -> 0 us
  blocking collectives: 0 us -> 22.3 us
  Pallas kernels: 39.5 us -> 56 us
  other arithmetic: 18.5 us -> 10.4 us
    ppermute x33 -> x36, waiting for transfers between devices: 97.6 us -> 62.6 us  [swapped(): return lax.ppermute(block, axis, [(i, i ^ mask) for i in range(count)])]
    dot_general x19 -> x0, matrix products: 23.7 us -> none  [the longest x8 10.8 us: matmul(): return jnp.dot(left, right, preferred_element_type=F32)]
    all_to_all x0 -> x1, blocking collectives: none -> 22.3 us  [per_device(): got = lax.all_to_all(sent, ALL, split_axis=0, concat_axis=0, tiled=True)]
    pallas_call x0 -> x14, Pallas kernels: none -> 16.4 us  [the longest x13 14.5 us: whole_call(): pl.pallas_call(kernel, in_specs=[vmem] * len(arguments), out_specs=[vmem]...]
    unnamed x106 -> x124, local copies, waits for them, and re-layouts: 10.7 us -> 25.8 us
    slice x12 -> x3, local copies, waits for them, and re-layouts: 13.6 us -> 0.66 us  [the longest x1 0.58 us: per_device(): shard_sums[dim_rows:2 * dim_rows]]
    all_gather x1, waiting for transfers between devices: 0.01 us -> 9.81 us  [per_device(): second = lax.all_gather(after(second, qkv), 'blk', axis=0, tiled=False)]
    all_to_all x2 -> x1, waiting for transfers between devices: 9.65 us -> 2.51 us  [per_device(): own = lax.all_to_all(own, 'heads', split_axis=0, concat_axis=0, tiled=True)]
  transfers between devices with their start and end apart: 44 -> 45, of which waited for: 26 -> 25; matrix products, arithmetic and copies ran while one was open for 15% -> 8% of each run, Pallas kernels for 10% -> 15%
where the time goes in v4:
time: 350 us; the launch traced here: 348 us
  waiting for transfers between devices  120 us (34%)
  starting transfers between devices  71.3 us (20%)
  Pallas kernels  56 us (16%)
  local copies, waits for them, and re-layouts  45.4 us (13%)
  between operations  22.7 us (6%)
  blocking collectives  22.3 us (6%)
  other arithmetic  10.4 us (3%)
    ppermute x36, waiting for transfers between devices, swapped(): return lax.ppermute(block, axis, [(i, i ^ mask) for i in range(count)])  62.6 us
    ppermute x36, starting transfers between devices, swapped(): return lax.ppermute(block, axis, [(i, i ^ mask) for i in range(count)])  47 us
    unnamed x124, local copies, waits for them, and re-layouts  25.8 us
    all_to_all x1, blocking collectives, per_device(): got = lax.all_to_all(sent, ALL, split_axis=0, concat_axis=0, tiled=True)  22.3 us
    all_to_all x1, waiting for transfers between devices, per_device(): qkv = lax.all_to_all(sent, 'blk', split_axis=0, concat_axis=0, tiled=True)  21.3 us
    pallas_call x1, Pallas kernels, attend_back(): pl.pallas_call(attend_back_kernel, grid_spec=pltpu.PrefetchScalarGridSpec...  17.2 us
    all_to_all x1, waiting for transfers between devices, per_device(): got = lax.all_to_all(sent, ALL, split_axis=0, concat_axis=0, tiled=True)  15.3 us
    pallas_call x13, Pallas kernels, whole_call(): pl.pallas_call(kernel, in_specs=[vmem] * len(arguments), out_specs=[vmem]...  14.5 us
  transfers between devices with their start and end apart: 45, of which 25 were waited for; matrix products, arithmetic and copies ran while one was open for 8% of the time, Pallas kernels for 15%

profile of v4, /device:TPU:0, one launch (start us, length us, event | category | flops | bytes accessed | tf_op | source)
XLA Modules:
  0.0 348.2 jit_solution(14845738711995044758)
XLA Ops:
  17.9 5.2 %all-to-all-start = ((bf16[4,32,1920]{2,1,0:T(8,128)(2,1)}), bf16[4,32,1920]{2,1,0:T(8,128)(2,1)S(1)}, u32[]{:S(2)}, u32[]{:S(2)}) async-start(bf16[4,32,1920]{2,1,0:T(8,128)(2,1)} %pad_maximum_fusion), calls=%async_computation | async-start | bytes 983040 | tf_op jit(solution)/shard_map/all_to_all | solution.py:987
  23.0 2.9 collective-permute-start.2
  26.5 6.9 %all-to-all-done = bf16[4,32,1920]{2,1,0:T(8,128)(2,1)S(1)} async-done(((bf16[4,32,1920]{2,1,0:T(8,128)(2,1)}), bf16[4,32,1920]{2,1,0:T(8,128)(2,1)S(1)}, u32[]{:S(2)}, u32[]{:S(2)}) %all-to-all-start) | async-done | bytes 491552 | tf_op jit(solution)/shard_map/all_to_all | solution.py:987
  33.4 5.3 %collective-permute-start.4 = (bf16[128,896]{1,0:T(8,128)(2,1)S(1)}, bf16[128,896]{1,0:T(8,128)(2,1)S(1)}, u32[]{:S(2)}, u32[]{:S(2)}) collective-permute-start(bf16[128,896]{1,0:T(8,128)(2,1)S(1)} %get-tuple-element.139), channel_id=1, source_target_pairs={{0,4},{1,5},{2,6},{3,7},{4,0},{5,1},{6,2},{7,3},{8,12},{9,13},{10,... | collective-permute-start | bytes 688136 | tf_op jit(solution)/shard_map/ppermute | solution.py:42
  47.0 7.8 %collective-permute-done.4 = bf16[128,896]{1,0:T(8,128)(2,1)S(1)} collective-permute-done((bf16[128,896]{1,0:T(8,128)(2,1)S(1)}, bf16[128,896]{1,0:T(8,128)(2,1)S(1)}, u32[]{:S(2)}, u32[]{:S(2)}) %collective-permute-start.4) | collective-permute-done | bytes 229408 | tf_op jit(solution)/shard_map/ppermute | solution.py:42
  57.5 2.8 shard_map.323
  62.6 5.4 %all-to-all-start.1 = ((bf16[8,384,128]{2,1,0:T(8,128)(2,1)}), bf16[8,384,128]{2,1,0:T(8,128)(2,1)S(1)}, u32[]{:S(2)}, u32[]{:S(2)}) async-start(bf16[8,384,128]{2,1,0:T(8,128)(2,1)} %get-tuple-element.71), calls=%async_computation.1 | async-start | bytes 1572864 | tf_op jit(solution)/shard_map/all_to_all | solution.py:1003
  68.0 21.3 %all-to-all-done.1.qkv_ref = bf16[8,384,128]{2,1,0:T(8,128)(2,1)S(1)} async-done(((bf16[8,384,128]{2,1,0:T(8,128)(2,1)}), bf16[8,384,128]{2,1,0:T(8,128)(2,1)S(1)}, u32[]{:S(2)}, u32[]{:S(2)}) %all-to-all-start.1) | async-done | bytes 786464 | tf_op jit(solution)/shard_map/all_to_all | solution.py:1003
  93.3 11.9 %shard_map.324 = (bf16[32,32,128]{2,1,0:T(8,128)(2,1)}, f32[64,2048]{1,0:T(8,128)S(1)}, f32[8,1,256]{2,1,0:T(1,128)S(1)}) custom-call(s32[4]{0:T(128)S(1)} %pad_add_fusion.spot_ref, s32[8,1,256]{2,1,0:T(1,128)S(1)} %bitcast.176, s32[2048,128]{1,0:T(8,128)S(1)} %broadcast_in_dim.65.seg_key_ref, bf16[8,384,128]{2,1,0:T(8,128)(2,1)S(1)} %all-to-all-done.1.qkv_ref), custom_call_target="tpu_custom_call" | custom-call | tf_op jit(solution)/shard_map/pallas_call | solution.py:205
  106.0 3.0 all-to-all-start.2
  110.1 15.3 %all-to-all-done.2.got_ref = bf16[32,32,128]{2,1,0:T(8,128)(2,1)S(1)} async-done(((bf16[32,32,128]{2,1,0:T(8,128)(2,1)}), bf16[32,32,128]{2,1,0:T(8,128)(2,1)S(1)}, u32[]{:S(2)}, u32[]{:S(2)}) %all-to-all-start.2) | async-done | bytes 262176 | tf_op jit(solution)/shard_map/all_to_all | solution.py:1034
  133.9 9.8 %all-gather.5.cloned.1.call-done = bf16[8,256,1024]{2,1,0:T(8,128)(2,1)} async-done(((bf16[1,256,1024]{2,1,0:T(8,128)(2,1)}), bf16[8,256,1024]{2,1,0:T(8,128)(2,1)}) %all-gather.5.cloned.1.call-update) | async-done | bytes 4194320 | tf_op jit(solution)/shard_map/all_gather | solution.py:1013
  155.2 3.5 %collective-permute-done.12.refs_8_ = bf16[128,1024]{1,0:T(8,128)(2,1)S(1)} collective-permute-done((bf16[128,1024]{1,0:T(8,128)(2,1)S(1)}, bf16[128,1024]{1,0:T(8,128)(2,1)S(1)}, u32[]{:S(2)}, u32[]{:S(2)}) %collective-permute-start.12) | collective-permute-done | bytes 262176 | tf_op jit(solution)/shard_map/ppermute | solution.py:42
  158.7 4.1 %collective-permute-done.10.refs_7_ = bf16[128,1024]{1,0:T(8,128)(2,1)S(1)} collective-permute-done((bf16[128,1024]{1,0:T(8,128)(2,1)S(1)}, bf16[128,1024]{1,0:T(8,128)(2,1)S(1)}, u32[]{:S(2)}, u32[]{:S(2)}) %collective-permute-start.10) | collective-permute-done | bytes 262176 | tf_op jit(solution)/shard_map/ppermute | solution.py:42
  168.3 6.6 %collective-permute-done.15.grad_ref.refs_7_ = bf16[128,1024]{1,0:T(8,128)(2,1)S(1)} collective-permute-done((bf16[128,1024]{1,0:T(8,128)(2,1)S(1)}, bf16[128,1024]{1,0:T(8,128)(2,1)S(1)}, u32[]{:S(2)}, u32[]{:S(2)}) %collective-permute-start.15) | collective-permute-done | bytes 262176 | tf_op jit(solution)/shard_map/ppermute | solution.py:42
  209.0 22.3 %all_to_all.30.up_ref = bf16[32,48,128]{2,1,0:T(8,128)(2,1)S(1)} all-to-all(bf16[32,48,128]{2,1,0:T(8,128)(2,1)S(1)} %get-tuple-element.109), channel_id=1, replica_groups=mesh['heads'=4,'blk'=8] {'blk','heads'}, dimensions={0} | all-to-all | bytes 786432 | tf_op jit(solution)/shard_map/all_to_all | solution.py:1083
  231.3 17.2 %shard_map.337 = bf16[8,384,128]{2,1,0:T(8,128)(2,1)} custom-call(s32[4]{0:T(128)S(1)} %pad_add_fusion.spot_ref, s32[8,1,256]{2,1,0:T(1,128)S(1)} %bitcast.177, s32[2048,128]{1,0:T(8,128)S(1)} %broadcast_in_dim.65.seg_key_ref, bf16[8,384,128]{2,1,0:T(8,128)(2,1)S(1)} %copy-done.4, bf16[32,48,128]{2,1,0:T(8,128)(2,1)S(1)} %all_to_all.30.up_ref, ...), custom_call_target="tpu_custom_call" | custom-call | tf_op jit(solution)/shard_map/pallas_call | solution.py:306
  248.5 3.5 %all-to-all-start.4 = ((bf16[8,384,128]{2,1,0:T(8,128)(2,1)}), bf16[8,384,128]{2,1,0:T(8,128)(2,1)S(1)}, u32[]{:S(2)}, u32[]{:S(2)}) async-start(bf16[8,384,128]{2,1,0:T(8,128)(2,1)} %shard_map.337), calls=%async_computation.4 | async-start | bytes 1572864 | tf_op jit(solution)/shard_map/all_to_all | solution.py:1094
  260.9 5.4 %collective-permute-done.31.refs_7_ = bf16[128,1024]{1,0:T(8,128)(2,1)S(1)} collective-permute-done((bf16[128,1024]{1,0:T(8,128)(2,1)S(1)}, bf16[128,1024]{1,0:T(8,128)(2,1)S(1)}, u32[]{:S(2)}, u32[]{:S(2)}) %collective-permute-start.31) | collective-permute-done | bytes 262176 | tf_op jit(solution)/shard_map/ppermute | solution.py:42
  266.3 5.0 %collective-permute-done.30.refs_6_ = bf16[128,1024]{1,0:T(8,128)(2,1)S(1)} collective-permute-done((bf16[128,1024]{1,0:T(8,128)(2,1)S(1)}, bf16[128,1024]{1,0:T(8,128)(2,1)S(1)}, u32[]{:S(2)}, u32[]{:S(2)}) %collective-permute-start.30) | collective-permute-done | bytes 262176 | tf_op jit(solution)/shard_map/ppermute | solution.py:42
  295.0 3.6 %collective-permute-done.23 = bf16[144,768]{1,0:T(8,128)(2,1)S(1)} collective-permute-done((bf16[144,768]{1,0:T(8,128)(2,1)S(1)}, bf16[144,768]{1,0:T(8,128)(2,1)S(1)}, u32[]{:S(2)}, u32[]{:S(2)}) %collective-permute-start.23) | collective-permute-done | bytes 221216 | tf_op jit(solution)/shard_map/ppermute | solution.py:42
  299.1 4.6 %collective-permute-done.25 = bf16[144,768]{1,0:T(8,128)(2,1)S(1)} collective-permute-done((bf16[144,768]{1,0:T(8,128)(2,1)S(1)}, bf16[144,768]{1,0:T(8,128)(2,1)S(1)}, u32[]{:S(2)}, u32[]{:S(2)}) %collective-permute-start.25) | collective-permute-done | bytes 221216 | tf_op jit(solution)/shard_map/ppermute | solution.py:42
  303.7 9.3 %collective-permute-done.24 = bf16[144,768]{1,0:T(8,128)(2,1)S(1)} collective-permute-done((bf16[144,768]{1,0:T(8,128)(2,1)S(1)}, bf16[144,768]{1,0:T(8,128)(2,1)S(1)}, u32[]{:S(2)}, u32[]{:S(2)}) %collective-permute-start.24) | collective-permute-done | bytes 221216 | tf_op jit(solution)/shard_map/ppermute | solution.py:42
  327.7 6.5 %all-to-all-start.5 = ((bf16[4,48,768]{2,1,0:T(8,128)(2,1)}), bf16[4,48,768]{2,1,0:T(8,128)(2,1)S(1)}, u32[]{:S(2)}, u32[]{:S(2)}) async-start(bf16[4,48,768]{2,1,0:T(8,128)(2,1)} %fusion.7), calls=%async_computation.6 | async-start | bytes 589824 | tf_op jit(solution)/shard_map/all_to_all | solution.py:1129
  (292 shorter events, 136.3 us)
Async XLA Ops:
  7.2 118.2 %all-gather.3.cloned.1.call-start = ((), (), s32[]{:S(2)}) async-start(), calls=%async_computation.7 | async-start | bytes 2162688 | tf_op jit(solution)/shard_map/all_gather | solution.py:991
  17.9 15.5 %all-to-all-start = ((bf16[4,32,1920]{2,1,0:T(8,128)(2,1)}), bf16[4,32,1920]{2,1,0:T(8,128)(2,1)S(1)}, u32[]{:S(2)}, u32[]{:S(2)}) async-start(bf16[4,32,1920]{2,1,0:T(8,128)(2,1)} %pad_maximum_fusion), calls=%async_computation | async-start | bytes 983040 | tf_op jit(solution)/shard_map/all_to_all | solution.py:987
  23.0 17.3 %collective-permute-start.2 = (bf16[128,1024]{1,0:T(8,128)(2,1)S(1)}, bf16[128,1024]{1,0:T(8,128)(2,1)S(1)}, u32[]{:S(2)}, u32[]{:S(2)}) collective-permute-start(bf16[128,1024]{1,0:T(8,128)(2,1)S(1)} %bitcast.169), channel_id=1, source_target_pairs={{0,24},{8,16},{16,8},{24,0},{1,25},{9,17},{17,9},{25,1},{2,26},{10... | collective-permute-start | bytes 786440 | tf_op jit(solution)/shard_map/ppermute | solution.py:42
  25.9 17.5 %collective-permute-start.1 = (bf16[128,1024]{1,0:T(8,128)(2,1)S(1)}, bf16[128,1024]{1,0:T(8,128)(2,1)S(1)}, u32[]{:S(2)}, u32[]{:S(2)}) collective-permute-start(bf16[128,1024]{1,0:T(8,128)(2,1)S(1)} %bitcast.170), channel_id=1, source_target_pairs={{0,16},{8,24},{16,0},{24,8},{1,17},{9,25},{17,1},{25,9},{2,18},{10... | collective-permute-start | bytes 786440 | tf_op jit(solution)/shard_map/ppermute | solution.py:42
  26.5 18.1 %collective-permute-start = (bf16[128,1024]{1,0:T(8,128)(2,1)S(1)}, bf16[128,1024]{1,0:T(8,128)(2,1)S(1)}, u32[]{:S(2)}, u32[]{:S(2)}) collective-permute-start(bf16[128,1024]{1,0:T(8,128)(2,1)S(1)} %bitcast.171), channel_id=1, source_target_pairs={{0,8},{8,0},{16,24},{24,16},{1,9},{9,1},{17,25},{25,17},{2,10},{10... | collective-permute-start | bytes 786440 | tf_op jit(solution)/shard_map/ppermute | solution.py:42
  33.4 21.3 %collective-permute-start.4 = (bf16[128,896]{1,0:T(8,128)(2,1)S(1)}, bf16[128,896]{1,0:T(8,128)(2,1)S(1)}, u32[]{:S(2)}, u32[]{:S(2)}) collective-permute-start(bf16[128,896]{1,0:T(8,128)(2,1)S(1)} %get-tuple-element.139), channel_id=1, source_target_pairs={{0,4},{1,5},{2,6},{3,7},{4,0},{5,1},{6,2},{7,3},{8,12},{9,13},{10,... | collective-permute-start | bytes 688136 | tf_op jit(solution)/shard_map/ppermute | solution.py:42
  38.8 16.0 %collective-permute-start.3 = (bf16[128,896]{1,0:T(8,128)(2,1)S(1)}, bf16[128,896]{1,0:T(8,128)(2,1)S(1)}, u32[]{:S(2)}, u32[]{:S(2)}) collective-permute-start(bf16[128,896]{1,0:T(8,128)(2,1)S(1)} %get-tuple-element.139), channel_id=1, source_target_pairs={{0,2},{1,3},{2,0},{3,1},{4,6},{5,7},{6,4},{7,5},{8,10},{9,11},{10,... | collective-permute-start | bytes 688136 | tf_op jit(solution)/shard_map/ppermute | solution.py:42
  40.3 14.5 %collective-permute-start.5 = (bf16[128,896]{1,0:T(8,128)(2,1)S(1)}, bf16[128,896]{1,0:T(8,128)(2,1)S(1)}, u32[]{:S(2)}, u32[]{:S(2)}) collective-permute-start(bf16[128,896]{1,0:T(8,128)(2,1)S(1)} %get-tuple-element.139), channel_id=1, source_target_pairs={{0,6},{1,7},{2,4},{3,5},{4,2},{5,3},{6,0},{7,1},{8,14},{9,15},{10,... | collective-permute-start | bytes 688136 | tf_op jit(solution)/shard_map/ppermute | solution.py:42
  62.6 26.8 %all-to-all-start.1 = ((bf16[8,384,128]{2,1,0:T(8,128)(2,1)}), bf16[8,384,128]{2,1,0:T(8,128)(2,1)S(1)}, u32[]{:S(2)}, u32[]{:S(2)}) async-start(bf16[8,384,128]{2,1,0:T(8,128)(2,1)} %get-tuple-element.71), calls=%async_computation.1 | async-start | bytes 1572864 | tf_op jit(solution)/shard_map/all_to_all | solution.py:1003
  67.9 75.8 %all-gather.5.cloned.1.call-start = ((), (), s32[]{:S(2)}) async-start(), calls=%async_computation.8 | async-start | bytes 4718592 | tf_op jit(solution)/shard_map/all_gather | solution.py:1013
  106.0 19.4 %all-to-all-start.2 = ((bf16[32,32,128]{2,1,0:T(8,128)(2,1)}), bf16[32,32,128]{2,1,0:T(8,128)(2,1)S(1)}, u32[]{:S(2)}, u32[]{:S(2)}) async-start(bf16[32,32,128]{2,1,0:T(8,128)(2,1)} %get-tuple-element.72), calls=%async_computation.2 | async-start | bytes 524288 | tf_op jit(solution)/shard_map/all_to_all | solution.py:1034
  109.0 204.2 %reduce-scatter.2.cloned.1.call-start = ((), (), s32[]{:S(2)}) async-start(), calls=%async_computation.9 | async-start | bytes 4718592 | tf_op jit(solution)/shard_map/reduce_scatter | solution.py:1067
  130.4 22.1 %collective-permute-start.7 = (bf16[128,1280]{1,0:T(8,128)(2,1)}, bf16[128,1280]{1,0:T(8,128)(2,1)S(1)}, u32[]{:S(2)}, u32[]{:S(2)}) collective-permute-start(bf16[128,1280]{1,0:T(8,128)(2,1)} %get-tuple-element.78), channel_id=1, source_target_pairs={{0,8},{8,0},{16,24},{24,16},{1,9},{9,1},{17,25},{25,17},{2,10},{10... | collective-permute-start | bytes 983048 | tf_op jit(solution)/shard_map/ppermute | solution.py:42
  131.3 18.8 %collective-permute-start.9 = (bf16[128,1280]{1,0:T(8,128)(2,1)}, bf16[128,1280]{1,0:T(8,128)(2,1)S(1)}, u32[]{:S(2)}, u32[]{:S(2)}) collective-permute-start(bf16[128,1280]{1,0:T(8,128)(2,1)} %get-tuple-element.80), channel_id=1, source_target_pairs={{0,16},{8,24},{16,0},{24,8},{1,17},{9,25},{17,1},{25,9},{2,18},{10... | collective-permute-start | bytes 983048 | tf_op jit(solution)/shard_map/ppermute | solution.py:42
  132.7 15.1 %collective-permute-start.11 = (bf16[128,1280]{1,0:T(8,128)(2,1)}, bf16[128,1280]{1,0:T(8,128)(2,1)S(1)}, u32[]{:S(2)}, u32[]{:S(2)}) collective-permute-start(bf16[128,1280]{1,0:T(8,128)(2,1)} %get-tuple-element.82), channel_id=1, source_target_pairs={{0,24},{8,16},{16,8},{24,0},{1,25},{9,17},{17,9},{25,1},{2,26},{10... | collective-permute-start | bytes 983048 | tf_op jit(solution)/shard_map/ppermute | solution.py:42
  166.9 14.0 %collective-permute-start.14 = (bf16[128,1024]{1,0:T(8,128)(2,1)S(1)}, bf16[128,1024]{1,0:T(8,128)(2,1)S(1)}, u32[]{:S(2)}, u32[]{:S(2)}) collective-permute-start(bf16[128,1024]{1,0:T(8,128)(2,1)S(1)} %get-tuple-element.85.grad_ref.refs_4_), channel_id=1, source_target_pairs={{0,16},{8,24},{16,0},{24,8},{1,17},{9,25},{17,1},{25,9},{2,18},{10... | collective-permute-start | bytes 786440 | tf_op jit(solution)/shard_map/ppermute | solution.py:42
  167.5 14.9 %collective-permute-start.13 = (bf16[128,1024]{1,0:T(8,128)(2,1)S(1)}, bf16[128,1024]{1,0:T(8,128)(2,1)S(1)}, u32[]{:S(2)}, u32[]{:S(2)}) collective-permute-start(bf16[128,1024]{1,0:T(8,128)(2,1)S(1)} %get-tuple-element.85.grad_ref.refs_4_), channel_id=1, source_target_pairs={{0,8},{8,0},{16,24},{24,16},{1,9},{9,1},{17,25},{25,17},{2,10},{10... | collective-permute-start | bytes 786440 | tf_op jit(solution)/shard_map/ppermute | solution.py:42
  248.5 24.4 %all-to-all-start.4 = ((bf16[8,384,128]{2,1,0:T(8,128)(2,1)}), bf16[8,384,128]{2,1,0:T(8,128)(2,1)S(1)}, u32[]{:S(2)}, u32[]{:S(2)}) async-start(bf16[8,384,128]{2,1,0:T(8,128)(2,1)} %shard_map.337), calls=%async_computation.4 | async-start | bytes 1572864 | tf_op jit(solution)/shard_map/all_to_all | solution.py:1094
  258.6 12.7 %collective-permute-start.30 = (bf16[128,1024]{1,0:T(8,128)(2,1)S(1)}, bf16[128,1024]{1,0:T(8,128)(2,1)S(1)}, u32[]{:S(2)}, u32[]{:S(2)}) collective-permute-start(bf16[128,1024]{1,0:T(8,128)(2,1)S(1)} %broadcast_add_fusion.1.refs_4_), channel_id=1, source_target_pairs={{0,16},{8,24},{16,0},{24,8},{1,17},{9,25},{17,1},{25,9},{2,18},{10... | collective-permute-start | bytes 786440 | tf_op jit(solution)/shard_map/ppermute | solution.py:42
  281.7 52.6 %collective-permute-start.19 = (bf16[128,1024]{1,0:T(8,128)(2,1)}, bf16[128,1024]{1,0:T(8,128)(2,1)S(1)}, u32[]{:S(2)}, u32[]{:S(2)}) collective-permute-start(bf16[128,1024]{1,0:T(8,128)(2,1)} %get-tuple-element.133), channel_id=1, source_target_pairs={{0,8},{8,0},{16,24},{24,16},{1,9},{9,1},{17,25},{25,17},{2,10},{10... | collective-permute-start | bytes 786440 | tf_op jit(solution)/shard_map/ppermute | solution.py:42
  283.1 51.1 %collective-permute-start.21 = (bf16[128,1024]{1,0:T(8,128)(2,1)S(1)}, bf16[128,1024]{1,0:T(8,128)(2,1)S(1)}, u32[]{:S(2)}, u32[]{:S(2)}) collective-permute-start(bf16[128,1024]{1,0:T(8,128)(2,1)S(1)} %get-tuple-element.134), channel_id=1, source_target_pairs={{0,24},{8,16},{16,8},{24,0},{1,25},{9,17},{17,9},{25,1},{2,26},{10... | collective-permute-start | bytes 786440 | tf_op jit(solution)/shard_map/ppermute | solution.py:42
  294.6 18.5 %collective-permute-start.24 = (bf16[144,768]{1,0:T(8,128)(2,1)S(1)}, bf16[144,768]{1,0:T(8,128)(2,1)S(1)}, u32[]{:S(2)}, u32[]{:S(2)}) collective-permute-start(bf16[144,768]{1,0:T(8,128)(2,1)S(1)} %get-tuple-element.130), channel_id=1, source_target_pairs={{0,4},{1,5},{2,6},{3,7},{4,0},{5,1},{6,2},{7,3},{8,12},{9,13},{10,... | collective-permute-start | bytes 663560 | tf_op jit(solution)/shard_map/ppermute | solution.py:42
  298.6 35.7 %collective-permute-start.20 = (bf16[128,1024]{1,0:T(8,128)(2,1)S(1)}, bf16[128,1024]{1,0:T(8,128)(2,1)S(1)}, u32[]{:S(2)}, u32[]{:S(2)}) collective-permute-start(bf16[128,1024]{1,0:T(8,128)(2,1)S(1)} %get-tuple-element.135), channel_id=1, source_target_pairs={{0,16},{8,24},{16,0},{24,8},{1,17},{9,25},{17,1},{25,9},{2,18},{10... | collective-permute-start | bytes 786440 | tf_op jit(solution)/shard_map/ppermute | solution.py:42
  327.7 12.6 %all-to-all-start.5 = ((bf16[4,48,768]{2,1,0:T(8,128)(2,1)}), bf16[4,48,768]{2,1,0:T(8,128)(2,1)S(1)}, u32[]{:S(2)}, u32[]{:S(2)}) async-start(bf16[4,48,768]{2,1,0:T(8,128)(2,1)} %fusion.7), calls=%async_computation.6 | async-start | bytes 589824 | tf_op jit(solution)/shard_map/all_to_all | solution.py:1129
  (79 other events, 1066.1 us)
Sparse Core Ops, SparseCore 0:
  10.9 64.8 all-gather.2
  92.6 51.0 all-gather.4
  191.6 55.0 reduce-scatter.1

commit v5 on v4

--- a/solution.py
+++ b/solution.py
@@ -1092,13 +1092,14 @@
     branch_parts = gather_parts(after(grad_branch, grads), "heads")
     grad_mat_out = out_grads_call(joint_parts, branch_parts)
     got = lax.all_to_all(grads, "blk", split_axis=0, concat_axis=0, tiled=True)
+    shard_up = after(shard_up, grads).reshape(groups, dim_rows, units_here)
+    shard_up = xor_order(shard_up, 0, my_group)
+    up_parts = [shard_up[0]] + [swapped(shard_up[k], "heads", k) for k in range(1, groups)]
+    for part in up_parts[1:]:
+        got = after(got, part)
     shard_out = scatter_blk(after(grad_mat_out, got).reshape(blocks, dim_rows, width)).astype(BF16)
     route = [(j, j % groups * blocks + j // groups) for j in range(devices)]
     shard_out = lax.ppermute(shard_out, ("heads", "blk"), route)
-    shard_up = after(shard_up, got).reshape(groups, dim_rows, units_here)
-    shard_up = xor_order(shard_up, 0, my_group)
-    up_parts = [shard_up[0]] + [swapped(shard_up[k], "heads", k) for k in range(1, groups)]
-    shard_up = place_columns(spot, up_parts, blocks)
     own_input, other_input, keep, send = input_grads(
         spot, got, mat_three, token_all, heads_here, groups, repeats
     )
@@ -1124,8 +1125,7 @@
     )
     own_sums = jnp.where(row == 0, own_sums[:, None, :], 0.0)
     own = jnp.concatenate([own_rows, own_sums], axis=1).astype(BF16)
-    for part in up_parts[1:]:
-        own = after(own, part)
+    shard_up = place_columns(after(spot, own), up_parts, blocks)
     own = lax.all_to_all(own, "heads", split_axis=0, concat_axis=0, tiled=True)
     shards_three = split_columns(own, dim_rows)
     shard_sums = shards_three[3][0]

time: 350 us -> 343 us (0.980)
  blocking collectives: 22.3 us -> 0 us
  waiting for transfers between devices: 120 us -> 126 us
  starting transfers between devices: 71.3 us -> 75.2 us
    all_to_all x1 -> x0, blocking collectives: 22.3 us -> none  [per_device(): got = lax.all_to_all(sent, ALL, split_axis=0, concat_axis=0, tiled=True)]
    all_to_all x1 -> x2, waiting for transfers between devices: 15.3 us -> 32.4 us  [per_device(): got = lax.all_to_all(sent, ALL, split_axis=0, concat_axis=0, tiled=True)]
    ppermute x36, waiting for transfers between devices: 62.6 us -> 55.7 us  [swapped(): return lax.ppermute(block, axis, [(i, i ^ mask) for i in range(count)])]
    all_to_all x1 -> x2, starting transfers between devices: 2.97 us -> 6.79 us  [per_device(): got = lax.all_to_all(sent, ALL, split_axis=0, concat_axis=0, tiled=True)]
    unnamed x124 -> x126, local copies, waits for them, and re-layouts: 25.8 us -> 27 us
  transfers between devices with their start and end apart: 45 -> 46, of which waited for: 25 -> 21; matrix products, arithmetic and copies ran while one was open for 8% -> 9% of each run, Pallas kernels for 15% -> 15%
where the time goes in v5:
time: 343 us; the launch traced here: 341 us
  waiting for transfers between devices  126 us (37%)
  starting transfers between devices  75.2 us (22%)
  Pallas kernels  55.8 us (16%)
  local copies, waits for them, and re-layouts  47.8 us (14%)
  between operations  23.4 us (7%)
  other arithmetic  13 us (4%)
    ppermute x36, waiting for transfers between devices, swapped(): return lax.ppermute(block, axis, [(i, i ^ mask) for i in range(count)])  55.7 us
    ppermute x36, starting transfers between devices, swapped(): return lax.ppermute(block, axis, [(i, i ^ mask) for i in range(count)])  49.4 us
    all_to_all x2, waiting for transfers between devices, per_device(): got = lax.all_to_all(sent, ALL, split_axis=0, concat_axis=0, tiled=True)  32.4 us
    unnamed x126, local copies, waits for them, and re-layouts  27 us
    all_to_all x1, waiting for transfers between devices, per_device(): qkv = lax.all_to_all(sent, 'blk', split_axis=0, concat_axis=0, tiled=True)  20.4 us
    pallas_call x1, Pallas kernels, attend_back(): pl.pallas_call(attend_back_kernel, grid_spec=pltpu.PrefetchScalarGridSpec...  17.1 us
    pallas_call x13, Pallas kernels, whole_call(): pl.pallas_call(kernel, in_specs=[vmem] * len(arguments), out_specs=[vmem]...  14.4 us
    pallas_call x1, Pallas kernels, attend(): pl.pallas_call(attend_kernel, grid_spec=pltpu.PrefetchScalarGridSpec(num_...  11.9 us
  transfers between devices with their start and end apart: 46, of which 21 were waited for; matrix products, arithmetic and copies ran while one was open for 9% of the time, Pallas kernels for 15%

profile of v5, /device:TPU:0, one launch (start us, length us, event | category | flops | bytes accessed | tf_op | source)
XLA Modules:
  0.0 341.0 jit_solution(828356961828224007)
XLA Ops:
  17.9 5.2 %all-to-all-start = ((bf16[4,32,1920]{2,1,0:T(8,128)(2,1)}), bf16[4,32,1920]{2,1,0:T(8,128)(2,1)S(1)}, u32[]{:S(2)}, u32[]{:S(2)}) async-start(bf16[4,32,1920]{2,1,0:T(8,128)(2,1)} %pad_maximum_fusion), calls=%async_computation | async-start | bytes 983040 | tf_op jit(solution)/shard_map/all_to_all | solution.py:987
  23.0 2.9 collective-permute-start.2
  26.5 6.9 %all-to-all-done = bf16[4,32,1920]{2,1,0:T(8,128)(2,1)S(1)} async-done(((bf16[4,32,1920]{2,1,0:T(8,128)(2,1)}), bf16[4,32,1920]{2,1,0:T(8,128)(2,1)S(1)}, u32[]{:S(2)}, u32[]{:S(2)}) %all-to-all-start) | async-done | bytes 491552 | tf_op jit(solution)/shard_map/all_to_all | solution.py:987
  33.4 5.3 %collective-permute-start.4 = (bf16[128,896]{1,0:T(8,128)(2,1)S(1)}, bf16[128,896]{1,0:T(8,128)(2,1)S(1)}, u32[]{:S(2)}, u32[]{:S(2)}) collective-permute-start(bf16[128,896]{1,0:T(8,128)(2,1)S(1)} %get-tuple-element.139), channel_id=1, source_target_pairs={{0,4},{1,5},{2,6},{3,7},{4,0},{5,1},{6,2},{7,3},{8,12},{9,13},{10,... | collective-permute-start | bytes 688136 | tf_op jit(solution)/shard_map/ppermute | solution.py:42
  47.0 7.8 %collective-permute-done.4 = bf16[128,896]{1,0:T(8,128)(2,1)S(1)} collective-permute-done((bf16[128,896]{1,0:T(8,128)(2,1)S(1)}, bf16[128,896]{1,0:T(8,128)(2,1)S(1)}, u32[]{:S(2)}, u32[]{:S(2)}) %collective-permute-start.4) | collective-permute-done | bytes 229408 | tf_op jit(solution)/shard_map/ppermute | solution.py:42
  57.5 2.8 shard_map.323
  62.6 5.4 %all-to-all-start.1 = ((bf16[8,384,128]{2,1,0:T(8,128)(2,1)}), bf16[8,384,128]{2,1,0:T(8,128)(2,1)S(1)}, u32[]{:S(2)}, u32[]{:S(2)}) async-start(bf16[8,384,128]{2,1,0:T(8,128)(2,1)} %get-tuple-element.71), calls=%async_computation.1 | async-start | bytes 1572864 | tf_op jit(solution)/shard_map/all_to_all | solution.py:1003
  68.9 20.4 %all-to-all-done.1.qkv_ref = bf16[8,384,128]{2,1,0:T(8,128)(2,1)S(1)} async-done(((bf16[8,384,128]{2,1,0:T(8,128)(2,1)}), bf16[8,384,128]{2,1,0:T(8,128)(2,1)S(1)}, u32[]{:S(2)}, u32[]{:S(2)}) %all-to-all-start.1) | async-done | bytes 786464 | tf_op jit(solution)/shard_map/all_to_all | solution.py:1003
  93.3 11.9 %shard_map.324 = (bf16[32,32,128]{2,1,0:T(8,128)(2,1)}, f32[64,2048]{1,0:T(8,128)S(1)}, f32[8,1,256]{2,1,0:T(1,128)S(1)}) custom-call(s32[4]{0:T(128)S(1)} %pad_add_fusion.spot_ref, s32[8,1,256]{2,1,0:T(1,128)S(1)} %bitcast.178, s32[2048,128]{1,0:T(8,128)S(1)} %broadcast_in_dim.65.seg_key_ref, bf16[8,384,128]{2,1,0:T(8,128)(2,1)S(1)} %all-to-all-done.1.qkv_ref), custom_call_target="tpu_custom_call" | custom-call | tf_op jit(solution)/shard_map/pallas_call | solution.py:205
  106.0 3.0 all-to-all-start.2
  109.6 15.8 %all-to-all-done.2.got_ref = bf16[32,32,128]{2,1,0:T(8,128)(2,1)S(1)} async-done(((bf16[32,32,128]{2,1,0:T(8,128)(2,1)}), bf16[32,32,128]{2,1,0:T(8,128)(2,1)S(1)}, u32[]{:S(2)}, u32[]{:S(2)}) %all-to-all-start.2) | async-done | bytes 262176 | tf_op jit(solution)/shard_map/all_to_all | solution.py:1034
  134.0 9.8 %all-gather.5.cloned.1.call-done = bf16[8,256,1024]{2,1,0:T(8,128)(2,1)} async-done(((bf16[1,256,1024]{2,1,0:T(8,128)(2,1)}), bf16[8,256,1024]{2,1,0:T(8,128)(2,1)}) %all-gather.5.cloned.1.call-update) | async-done | bytes 4194320 | tf_op jit(solution)/shard_map/all_gather | solution.py:1013
  143.8 2.8 fusion.30
  155.1 3.7 %collective-permute-done.12.refs_8_ = bf16[128,1024]{1,0:T(8,128)(2,1)S(1)} collective-permute-done((bf16[128,1024]{1,0:T(8,128)(2,1)S(1)}, bf16[128,1024]{1,0:T(8,128)(2,1)S(1)}, u32[]{:S(2)}, u32[]{:S(2)}) %collective-permute-start.12) | collective-permute-done | bytes 262176 | tf_op jit(solution)/shard_map/ppermute | solution.py:42
  158.9 4.0 %collective-permute-done.10.refs_7_ = bf16[128,1024]{1,0:T(8,128)(2,1)S(1)} collective-permute-done((bf16[128,1024]{1,0:T(8,128)(2,1)S(1)}, bf16[128,1024]{1,0:T(8,128)(2,1)S(1)}, u32[]{:S(2)}, u32[]{:S(2)}) %collective-permute-start.10) | collective-permute-done | bytes 262176 | tf_op jit(solution)/shard_map/ppermute | solution.py:42
  168.3 6.6 %collective-permute-done.15.grad_ref.refs_7_ = bf16[128,1024]{1,0:T(8,128)(2,1)S(1)} collective-permute-done((bf16[128,1024]{1,0:T(8,128)(2,1)S(1)}, bf16[128,1024]{1,0:T(8,128)(2,1)S(1)}, u32[]{:S(2)}, u32[]{:S(2)}) %collective-permute-start.15) | collective-permute-done | bytes 262176 | tf_op jit(solution)/shard_map/ppermute | solution.py:42
  210.4 3.8 %all-to-all-start.3 = ((bf16[32,48,128]{2,1,0:T(8,128)(2,1)}), bf16[32,48,128]{2,1,0:T(8,128)(2,1)S(1)}, u32[]{:S(2)}, u32[]{:S(2)}) async-start(bf16[32,48,128]{2,1,0:T(8,128)(2,1)} %copy-done.28), calls=%async_computation.3 | async-start | bytes 786432 | tf_op jit(solution)/shard_map/all_to_all | solution.py:1083
  216.2 16.6 %all-to-all-done.3.up_ref = bf16[32,48,128]{2,1,0:T(8,128)(2,1)S(1)} async-done(((bf16[32,48,128]{2,1,0:T(8,128)(2,1)}), bf16[32,48,128]{2,1,0:T(8,128)(2,1)S(1)}, u32[]{:S(2)}, u32[]{:S(2)}) %all-to-all-start.3) | async-done | bytes 393248 | tf_op jit(solution)/shard_map/all_to_all | solution.py:1083
  235.7 17.1 %shard_map.337 = bf16[8,384,128]{2,1,0:T(8,128)(2,1)} custom-call(s32[4]{0:T(128)S(1)} %pad_add_fusion.spot_ref, s32[8,1,256]{2,1,0:T(1,128)S(1)} %bitcast.179, s32[2048,128]{1,0:T(8,128)S(1)} %broadcast_in_dim.65.seg_key_ref, bf16[8,384,128]{2,1,0:T(8,128)(2,1)S(1)} %copy-done.5, bf16[32,48,128]{2,1,0:T(8,128)(2,1)S(1)} %all-to-all-done.3.up_ref, ...), custom_call_target="tpu_custom_call" | custom-call | tf_op jit(solution)/shard_map/pallas_call | solution.py:306
  254.1 4.2 %all-to-all-start.4 = ((bf16[8,384,128]{2,1,0:T(8,128)(2,1)}), bf16[8,384,128]{2,1,0:T(8,128)(2,1)}, u32[]{:S(2)}, u32[]{:S(2)}) async-start(bf16[8,384,128]{2,1,0:T(8,128)(2,1)} %shard_map.337), calls=%async_computation.4 | async-start | bytes 1572864 | tf_op jit(solution)/shard_map/all_to_all | solution.py:1094
  271.2 3.7 %collective-permute-done.30.refs_6_ = bf16[128,1024]{1,0:T(8,128)(2,1)S(1)} collective-permute-done((bf16[128,1024]{1,0:T(8,128)(2,1)S(1)}, bf16[128,1024]{1,0:T(8,128)(2,1)S(1)}, u32[]{:S(2)}, u32[]{:S(2)}) %collective-permute-start.30) | collective-permute-done | bytes 262176 | tf_op jit(solution)/shard_map/ppermute | solution.py:42
  305.5 5.4 %collective-permute-done.28 = bf16[144,768]{1,0:T(8,128)(2,1)S(1)} collective-permute-done((bf16[144,768]{1,0:T(8,128)(2,1)S(1)}, bf16[144,768]{1,0:T(8,128)(2,1)S(1)}, u32[]{:S(2)}, u32[]{:S(2)}) %collective-permute-start.28) | collective-permute-done | bytes 221216 | tf_op jit(solution)/shard_map/ppermute | solution.py:42
  311.6 10.5 %collective-permute-done.27 = bf16[144,768]{1,0:T(8,128)(2,1)S(1)} collective-permute-done((bf16[144,768]{1,0:T(8,128)(2,1)S(1)}, bf16[144,768]{1,0:T(8,128)(2,1)S(1)}, u32[]{:S(2)}, u32[]{:S(2)}) %collective-permute-start.27) | collective-permute-done | bytes 221216 | tf_op jit(solution)/shard_map/ppermute | solution.py:42
  323.3 3.5 %all-to-all-start.5 = ((bf16[4,48,768]{2,1,0:T(8,128)(2,1)}), bf16[4,48,768]{2,1,0:T(8,128)(2,1)S(1)}, u32[]{:S(2)}, u32[]{:S(2)}) async-start(bf16[4,48,768]{2,1,0:T(8,128)(2,1)} %pad_maximum_fusion.1), calls=%async_computation.6 | async-start | bytes 589824 | tf_op jit(solution)/shard_map/all_to_all | solution.py:1129
  (298 shorter events, 138.6 us)
Async XLA Ops:
  7.2 118.2 %all-gather.3.cloned.1.call-start = ((), (), s32[]{:S(2)}) async-start(), calls=%async_computation.7 | async-start | bytes 2162688 | tf_op jit(solution)/shard_map/all_gather | solution.py:991
  17.9 15.5 %all-to-all-start = ((bf16[4,32,1920]{2,1,0:T(8,128)(2,1)}), bf16[4,32,1920]{2,1,0:T(8,128)(2,1)S(1)}, u32[]{:S(2)}, u32[]{:S(2)}) async-start(bf16[4,32,1920]{2,1,0:T(8,128)(2,1)} %pad_maximum_fusion), calls=%async_computation | async-start | bytes 983040 | tf_op jit(solution)/shard_map/all_to_all | solution.py:987
  23.0 17.3 %collective-permute-start.2 = (bf16[128,1024]{1,0:T(8,128)(2,1)S(1)}, bf16[128,1024]{1,0:T(8,128)(2,1)S(1)}, u32[]{:S(2)}, u32[]{:S(2)}) collective-permute-start(bf16[128,1024]{1,0:T(8,128)(2,1)S(1)} %bitcast.171), channel_id=1, source_target_pairs={{0,24},{8,16},{16,8},{24,0},{1,25},{9,17},{17,9},{25,1},{2,26},{10... | collective-permute-start | bytes 786440 | tf_op jit(solution)/shard_map/ppermute | solution.py:42
  25.9 17.5 %collective-permute-start.1 = (bf16[128,1024]{1,0:T(8,128)(2,1)S(1)}, bf16[128,1024]{1,0:T(8,128)(2,1)S(1)}, u32[]{:S(2)}, u32[]{:S(2)}) collective-permute-start(bf16[128,1024]{1,0:T(8,128)(2,1)S(1)} %bitcast.172), channel_id=1, source_target_pairs={{0,16},{8,24},{16,0},{24,8},{1,17},{9,25},{17,1},{25,9},{2,18},{10... | collective-permute-start | bytes 786440 | tf_op jit(solution)/shard_map/ppermute | solution.py:42
  26.5 18.1 %collective-permute-start = (bf16[128,1024]{1,0:T(8,128)(2,1)S(1)}, bf16[128,1024]{1,0:T(8,128)(2,1)S(1)}, u32[]{:S(2)}, u32[]{:S(2)}) collective-permute-start(bf16[128,1024]{1,0:T(8,128)(2,1)S(1)} %bitcast.173), channel_id=1, source_target_pairs={{0,8},{8,0},{16,24},{24,16},{1,9},{9,1},{17,25},{25,17},{2,10},{10... | collective-permute-start | bytes 786440 | tf_op jit(solution)/shard_map/ppermute | solution.py:42
  33.4 21.3 %collective-permute-start.4 = (bf16[128,896]{1,0:T(8,128)(2,1)S(1)}, bf16[128,896]{1,0:T(8,128)(2,1)S(1)}, u32[]{:S(2)}, u32[]{:S(2)}) collective-permute-start(bf16[128,896]{1,0:T(8,128)(2,1)S(1)} %get-tuple-element.139), channel_id=1, source_target_pairs={{0,4},{1,5},{2,6},{3,7},{4,0},{5,1},{6,2},{7,3},{8,12},{9,13},{10,... | collective-permute-start | bytes 688136 | tf_op jit(solution)/shard_map/ppermute | solution.py:42
  38.8 16.0 %collective-permute-start.3 = (bf16[128,896]{1,0:T(8,128)(2,1)S(1)}, bf16[128,896]{1,0:T(8,128)(2,1)S(1)}, u32[]{:S(2)}, u32[]{:S(2)}) collective-permute-start(bf16[128,896]{1,0:T(8,128)(2,1)S(1)} %get-tuple-element.139), channel_id=1, source_target_pairs={{0,2},{1,3},{2,0},{3,1},{4,6},{5,7},{6,4},{7,5},{8,10},{9,11},{10,... | collective-permute-start | bytes 688136 | tf_op jit(solution)/shard_map/ppermute | solution.py:42
  40.3 14.5 %collective-permute-start.5 = (bf16[128,896]{1,0:T(8,128)(2,1)S(1)}, bf16[128,896]{1,0:T(8,128)(2,1)S(1)}, u32[]{:S(2)}, u32[]{:S(2)}) collective-permute-start(bf16[128,896]{1,0:T(8,128)(2,1)S(1)} %get-tuple-element.139), channel_id=1, source_target_pairs={{0,6},{1,7},{2,4},{3,5},{4,2},{5,3},{6,0},{7,1},{8,14},{9,15},{10,... | collective-permute-start | bytes 688136 | tf_op jit(solution)/shard_map/ppermute | solution.py:42
  62.6 26.8 %all-to-all-start.1 = ((bf16[8,384,128]{2,1,0:T(8,128)(2,1)}), bf16[8,384,128]{2,1,0:T(8,128)(2,1)S(1)}, u32[]{:S(2)}, u32[]{:S(2)}) async-start(bf16[8,384,128]{2,1,0:T(8,128)(2,1)} %get-tuple-element.71), calls=%async_computation.1 | async-start | bytes 1572864 | tf_op jit(solution)/shard_map/all_to_all | solution.py:1003
  67.9 75.8 %all-gather.5.cloned.1.call-start = ((), (), s32[]{:S(2)}) async-start(), calls=%async_computation.8 | async-start | bytes 4718592 | tf_op jit(solution)/shard_map/all_gather | solution.py:1013
  106.0 19.4 %all-to-all-start.2 = ((bf16[32,32,128]{2,1,0:T(8,128)(2,1)}), bf16[32,32,128]{2,1,0:T(8,128)(2,1)S(1)}, u32[]{:S(2)}, u32[]{:S(2)}) async-start(bf16[32,32,128]{2,1,0:T(8,128)(2,1)} %get-tuple-element.72), calls=%async_computation.2 | async-start | bytes 524288 | tf_op jit(solution)/shard_map/all_to_all | solution.py:1034
  109.0 154.3 %reduce-scatter.2.cloned.1.call-start = ((), (), s32[]{:S(2)}) async-start(), calls=%async_computation.9 | async-start | bytes 4718592 | tf_op jit(solution)/shard_map/reduce_scatter | solution.py:1067
  130.5 22.0 %collective-permute-start.7 = (bf16[128,1280]{1,0:T(8,128)(2,1)}, bf16[128,1280]{1,0:T(8,128)(2,1)S(1)}, u32[]{:S(2)}, u32[]{:S(2)}) collective-permute-start(bf16[128,1280]{1,0:T(8,128)(2,1)} %get-tuple-element.78), channel_id=1, source_target_pairs={{0,8},{8,0},{16,24},{24,16},{1,9},{9,1},{17,25},{25,17},{2,10},{10... | collective-permute-start | bytes 983048 | tf_op jit(solution)/shard_map/ppermute | solution.py:42
  131.3 18.8 %collective-permute-start.9 = (bf16[128,1280]{1,0:T(8,128)(2,1)}, bf16[128,1280]{1,0:T(8,128)(2,1)S(1)}, u32[]{:S(2)}, u32[]{:S(2)}) collective-permute-start(bf16[128,1280]{1,0:T(8,128)(2,1)} %get-tuple-element.80), channel_id=1, source_target_pairs={{0,16},{8,24},{16,0},{24,8},{1,17},{9,25},{17,1},{25,9},{2,18},{10... | collective-permute-start | bytes 983048 | tf_op jit(solution)/shard_map/ppermute | solution.py:42
  132.8 15.0 %collective-permute-start.11 = (bf16[128,1280]{1,0:T(8,128)(2,1)}, bf16[128,1280]{1,0:T(8,128)(2,1)S(1)}, u32[]{:S(2)}, u32[]{:S(2)}) collective-permute-start(bf16[128,1280]{1,0:T(8,128)(2,1)} %get-tuple-element.82), channel_id=1, source_target_pairs={{0,24},{8,16},{16,8},{24,0},{1,25},{9,17},{17,9},{25,1},{2,26},{10... | collective-permute-start | bytes 983048 | tf_op jit(solution)/shard_map/ppermute | solution.py:42
  166.8 14.0 %collective-permute-start.14 = (bf16[128,1024]{1,0:T(8,128)(2,1)S(1)}, bf16[128,1024]{1,0:T(8,128)(2,1)S(1)}, u32[]{:S(2)}, u32[]{:S(2)}) collective-permute-start(bf16[128,1024]{1,0:T(8,128)(2,1)S(1)} %get-tuple-element.85.grad_ref.refs_4_), channel_id=1, source_target_pairs={{0,16},{8,24},{16,0},{24,8},{1,17},{9,25},{17,1},{25,9},{2,18},{10... | collective-permute-start | bytes 786440 | tf_op jit(solution)/shard_map/ppermute | solution.py:42
  167.5 14.8 %collective-permute-start.13 = (bf16[128,1024]{1,0:T(8,128)(2,1)S(1)}, bf16[128,1024]{1,0:T(8,128)(2,1)S(1)}, u32[]{:S(2)}, u32[]{:S(2)}) collective-permute-start(bf16[128,1024]{1,0:T(8,128)(2,1)S(1)} %get-tuple-element.85.grad_ref.refs_4_), channel_id=1, source_target_pairs={{0,8},{8,0},{16,24},{24,16},{1,9},{9,1},{17,25},{25,17},{2,10},{10... | collective-permute-start | bytes 786440 | tf_op jit(solution)/shard_map/ppermute | solution.py:42
  210.4 22.5 %all-to-all-start.3 = ((bf16[32,48,128]{2,1,0:T(8,128)(2,1)}), bf16[32,48,128]{2,1,0:T(8,128)(2,1)S(1)}, u32[]{:S(2)}, u32[]{:S(2)}) async-start(bf16[32,48,128]{2,1,0:T(8,128)(2,1)} %copy-done.28), calls=%async_computation.3 | async-start | bytes 786432 | tf_op jit(solution)/shard_map/all_to_all | solution.py:1083
  254.1 25.7 %all-to-all-start.4 = ((bf16[8,384,128]{2,1,0:T(8,128)(2,1)}), bf16[8,384,128]{2,1,0:T(8,128)(2,1)}, u32[]{:S(2)}, u32[]{:S(2)}) async-start(bf16[8,384,128]{2,1,0:T(8,128)(2,1)} %shard_map.337), calls=%async_computation.4 | async-start | bytes 1572864 | tf_op jit(solution)/shard_map/all_to_all | solution.py:1094
  287.5 39.3 %collective-permute-start.22 = (bf16[128,1024]{1,0:T(8,128)(2,1)}, bf16[128,1024]{1,0:T(8,128)(2,1)}, u32[]{:S(2)}, u32[]{:S(2)}) collective-permute-start(bf16[128,1024]{1,0:T(8,128)(2,1)} %get-tuple-element.133), channel_id=1, source_target_pairs={{0,8},{8,0},{16,24},{24,16},{1,9},{9,1},{17,25},{25,17},{2,10},{10... | collective-permute-start | bytes 786440 | tf_op jit(solution)/shard_map/ppermute | solution.py:42
  289.0 37.8 %collective-permute-start.24 = (bf16[128,1024]{1,0:T(8,128)(2,1)}, bf16[128,1024]{1,0:T(8,128)(2,1)}, u32[]{:S(2)}, u32[]{:S(2)}) collective-permute-start(bf16[128,1024]{1,0:T(8,128)(2,1)} %get-tuple-element.134), channel_id=1, source_target_pairs={{0,24},{8,16},{16,8},{24,0},{1,25},{9,17},{17,9},{25,1},{2,26},{10... | collective-permute-start | bytes 786440 | tf_op jit(solution)/shard_map/ppermute | solution.py:42
  301.6 20.5 %collective-permute-start.27 = (bf16[144,768]{1,0:T(8,128)(2,1)S(1)}, bf16[144,768]{1,0:T(8,128)(2,1)S(1)}, u32[]{:S(2)}, u32[]{:S(2)}) collective-permute-start(bf16[144,768]{1,0:T(8,128)(2,1)S(1)} %get-tuple-element.130), channel_id=1, source_target_pairs={{0,4},{1,5},{2,6},{3,7},{4,0},{5,1},{6,2},{7,3},{8,12},{9,13},{10,... | collective-permute-start | bytes 663560 | tf_op jit(solution)/shard_map/ppermute | solution.py:42
  305.0 21.8 %collective-permute-start.23 = (bf16[128,1024]{1,0:T(8,128)(2,1)}, bf16[128,1024]{1,0:T(8,128)(2,1)S(1)}, u32[]{:S(2)}, u32[]{:S(2)}) collective-permute-start(bf16[128,1024]{1,0:T(8,128)(2,1)} %get-tuple-element.135), channel_id=1, source_target_pairs={{0,16},{8,24},{16,0},{24,8},{1,17},{9,25},{17,1},{25,9},{2,18},{10... | collective-permute-start | bytes 786440 | tf_op jit(solution)/shard_map/ppermute | solution.py:42
  310.9 17.9 %collective-permute-start.36 = (bf16[32,1024]{1,0:T(8,128)(2,1)S(1)}, bf16[32,1024]{1,0:T(8,128)(2,1)S(1)}, u32[]{:S(2)}, u32[]{:S(2)}) collective-permute-start(bf16[32,1024]{1,0:T(8,128)(2,1)S(1)} %fusion.9), channel_id=1, source_target_pairs={{0,0},{1,8},{2,16},{3,24},{4,1},{5,9},{6,17},{7,25},{8,2},{9,10},{... | collective-permute-start | bytes 196616 | tf_op jit(solution)/shard_map/ppermute | solution.py:1102
  (81 other events, 750.7 us)
Sparse Core Ops, SparseCore 0:
  10.9 64.7 all-gather.2
  92.6 51.0 all-gather.4
  191.6 55.0 reduce-scatter.1

commit v6 on v5

--- a/solution.py
+++ b/solution.py
@@ -132,7 +132,7 @@
 
 
 def score_all(turn, seg_query, seg_key_ref, qkv_ref, query_t, scores):
-    sources, rows = qkv_ref.shape[0], qkv_ref.shape[1] * 2 // 3
+    sources, rows = qkv_ref.shape[0], (qkv_ref.shape[1] - 16) * 2 // 3
     per_source = rows // QUERY_ROWS
     query_now = query_t[turn]
     for b in range(sources):
@@ -160,7 +160,7 @@
     query_t, values_t, scores,
 ):
     step = pl.program_id(0)
-    sources, rows = qkv_ref.shape[0], qkv_ref.shape[1] * 2 // 3
+    sources, rows = qkv_ref.shape[0], (qkv_ref.shape[1] - 16) * 2 // 3
     half = rows // 2
 
     @pl.when(step == 0)
@@ -197,7 +197,7 @@
 
 
 def attend(spot, seg_row, seg_key, qkv, wide, query_length):
-    sources, rows = qkv.shape[0], qkv.shape[1] * 2 // 3
+    sources, rows = qkv.shape[0], (qkv.shape[1] - 16) * 2 // 3
     length = sources * rows
     steps = query_length // QUERY_ROWS
     spans = rows // (2 * wide)
@@ -237,7 +237,7 @@
     query_t, keys_t, values, scores, grad_query, grad_key, grad_value,
 ):
     step = pl.program_id(0)
-    sources, rows = qkv_ref.shape[0], qkv_ref.shape[1] * 2 // 3
+    sources, rows = qkv_ref.shape[0], (qkv_ref.shape[1] - 16) * 2 // 3
     half = rows // 2
     lane = lax.broadcasted_iota(jnp.int32, (rows, 128), 1)
 
@@ -298,7 +298,7 @@
 
 
 def attend_back(spot, seg_row, seg_key, qkv, upstream, attn_t, lse):
-    sources, rows = qkv.shape[0], qkv.shape[1] * 2 // 3
+    sources, rows = qkv.shape[0], (qkv.shape[1] - 16) * 2 // 3
     length = sources * rows
     steps = lse.shape[0]
     groups = upstream.shape[0] // sources
@@ -319,7 +319,9 @@
                 pl.BlockSpec((HEAD_DIM, QUERY_ROWS), lambda i, spot: (0, i)),
                 pl.BlockSpec((1, 1, QUERY_ROWS), lambda i, spot: (i, 0, 0)),
             ],
-            out_specs=pl.BlockSpec(qkv.shape, lambda i, spot: (0, 0, 0)),
+            out_specs=pl.BlockSpec(
+                (sources, rows * 3 // 2, 128), lambda i, spot: (0, 0, 0)
+            ),
             scratch_shapes=[
                 pltpu.VMEM((length // QUERY_ROWS, 128, QUERY_ROWS), BF16),
                 pltpu.VMEM((HEAD_DIM, length), BF16),
@@ -330,7 +332,7 @@
                 pltpu.VMEM((length, 128), F32),
             ],
         ),
-        out_shape=jax.ShapeDtypeStruct(qkv.shape, BF16),
+        out_shape=jax.ShapeDtypeStruct((sources, rows * 3 // 2, 128), BF16),
         compiler_params=pltpu.CompilerParams(vmem_limit_bytes=vmem_limit(length)),
     )(spot, seg_row, seg_key, qkv, upstream, attn_t, lse)
 
@@ -529,38 +531,28 @@
     )(spot, own, resid, unit, inv_std, gain, mat_out, early, up_sums, squares, *others)
 
 
-def pack_kernel(*refs):
-    out_ref = refs[-1]
-    rows = [jnp.zeros((1, 128), F32) for _ in range(out_ref.shape[0])]
-    start = 0
-    for ref in refs[:-1]:
-        size = ref.shape[1]
-        pieces = [ref[...].astype(F32)]
-        if start % 128:
-            pieces = [jnp.zeros((1, start % 128), F32)] + pieces
-        if start % 128 + size < 128:
-            pieces = pieces + [jnp.zeros((1, 128 - start % 128 - size), F32)]
-        piece = jnp.concatenate(pieces, axis=1) if len(pieces) > 1 else pieces[0]
-        rows[start // 128] = rows[start // 128] + piece
-        start += size
-    out_ref[...] = jnp.concatenate(rows, axis=0).astype(BF16)
-
-
 def project_kernel(groups, heads_here, repeats, spot_ref, *refs):
-    tokens, (mine_ref, other_ref, sent_ref, all_ref, mat_ref, short_ref, values) = (
-        refs[:groups], refs[groups:]
-    )
+    tokens, (mine_ref, other_ref, sent_ref, all_ref, mat_ref, values) = refs[:groups], refs[groups:]
     my_block, my_group = spot_ref[0], spot_ref[1]
     halves, chip_rows, _ = mine_ref.shape
     blocks = 2 * halves
     dim_rows = chip_rows // groups
-    rows, width = tokens[0].shape
+    rows, width = all_ref.shape[0] // groups, all_ref.shape[1]
     width_here = heads_here * HEAD_DIM
     seqs = sent_ref.shape[0] // (repeats * heads_here)
     span = rows // seqs
     block_rows = span * groups
+    each = 16 // groups
+    row = lax.broadcasted_iota(jnp.int32, (16, 128), 0)
+    short = jnp.zeros((16, 128), F32)
     for k in range(groups):
-        all_ref[k * rows : (k + 1) * rows, :] = tokens[k][...]
+        all_ref[k * rows : (k + 1) * rows, :] = tokens[k][0:rows, :]
+        vectors = tokens[k][rows : rows + 16, :].astype(F32)
+        for i in range(each):
+            piece = vectors[0:1, i * 128 : (i + 1) * 128]
+            short = short + jnp.where(row == (my_group ^ k) * each + i, piece, 0.0)
+    for place in range(sent_ref.shape[0]):
+        sent_ref[place, block_rows * 3 // 2 :, :] = short.astype(BF16)
     for b in range(blocks):
         place = my_block ^ b
         spot = slice(b * chip_rows, (b + 1) * chip_rows)
@@ -573,15 +565,6 @@
         def _():
             mat_ref[spot, :] = other_ref[place // 2, :, 0 : 3 * width_here]
 
-    for b in range(blocks):
-        place = my_block ^ b
-        vectors = jnp.where(
-            place % 2 == 0,
-            mine_ref[place // 2, :, 3 * width_here :].astype(F32),
-            other_ref[place // 2, :, 3 * width_here :].astype(F32),
-        )
-        for group in range(groups):
-            short_ref[b * groups + group] = vectors[group * dim_rows : group * dim_rows + 8]
     lane = lax.broadcasted_iota(jnp.int32, (1, 128), 1)
     tiles = width_here // 128
     biases = [[jnp.zeros((1, 128), F32) for _ in range(tiles)] for _ in range(2)]
@@ -626,18 +609,18 @@
 def project(spot, token_parts, mine, other, seqs, heads_here, repeats):
     groups = len(token_parts)
     rows, width = token_parts[0].shape
+    rows -= 16
     blocks = seqs * heads_here * repeats
     block_rows = rows // seqs * groups
     vmem = pl.BlockSpec(memory_space=pltpu.VMEM)
     return pl.pallas_call(
         functools.partial(project_kernel, groups, heads_here, repeats),
         in_specs=[pl.BlockSpec(memory_space=pltpu.SMEM)] + [vmem] * (groups + 2),
-        out_specs=[vmem] * 4,
+        out_specs=[vmem] * 3,
         out_shape=[
-            jax.ShapeDtypeStruct((blocks, block_rows * 3 // 2, 128), BF16),
+            jax.ShapeDtypeStruct((blocks, block_rows * 3 // 2 + 16, 128), BF16),
             jax.ShapeDtypeStruct((groups * rows, width), BF16),
             jax.ShapeDtypeStruct((width, 3 * heads_here * HEAD_DIM), BF16),
-            jax.ShapeDtypeStruct((blocks * groups, 8, 128), F32),
         ],
         scratch_shapes=[pltpu.VMEM((groups * rows, heads_here * HEAD_DIM), F32)],
         compiler_params=pltpu.CompilerParams(vmem_limit_bytes=40 * 1024 * 1024),
@@ -968,17 +951,21 @@
     wide = span // 2
 
     token_rows = tokens.reshape(rows, width)
-    token_parts = gather_parts(token_rows, "heads")
+    short = jnp.concatenate(
+        [b_out, b_fc2, gain_attn, bias_attn, gain_ffn, bias_ffn, b_fc1]
+    )
+    short_size = short.shape[0]
+    short = jnp.pad(short, (0, 16 * width - short_size)).reshape(16, width)
+    token_parts = gather_parts(jnp.concatenate([token_rows, short]), "heads")
     w_three = jnp.concatenate(
         [w.reshape(dim_rows, groups, width_here) for w in (w_query, w_key, w_value)], axis=-1
     )
     w_three = jnp.transpose(w_three, (1, 0, 2))
-    short = [b_query, b_value, b_out, b_fc2, gain_attn, bias_attn, gain_ffn, bias_ffn, b_fc1]
-    vectors = whole_call(
-        pack_kernel,
-        [jax.ShapeDtypeStruct((dim_rows, 128), BF16)],
-        [item[None] for item in short],
-    )[0]
+    def lanes_of(pieces):
+        flat = jnp.concatenate(pieces)
+        return jnp.pad(flat, (0, dim_rows * 128 - flat.shape[0])).reshape(dim_rows, 128)
+
+    vectors = lanes_of([b_query, b_value])
     w_up = w_fc1.reshape(dim_rows, blocks, groups, unit_rows)
     w_up = jnp.transpose(w_up, (2, 0, 1, 3)).reshape(groups, dim_rows, units_here)
     first = jnp.concatenate(
@@ -997,23 +984,29 @@
     part_blocks = blocks // repeats
     first_turn = my_block % repeats * (parts_length // QUERY_ROWS)
     spot = jnp.stack([my_block, my_group, first_turn, my_block // part_blocks]).astype(jnp.int32)
-    sent, token_all, mat_three, short = project(
+    sent, token_all, mat_three = project(
         spot, token_parts, mine, other, seqs, heads_here, repeats
     )
     qkv = lax.all_to_all(sent, "blk", split_axis=0, concat_axis=0, tiled=True)
 
 
-    vectors = short.reshape(devices, 8 * 128)
-    vec_up = vectors[:, 8 * dim_rows : 8 * dim_rows + unit_rows].reshape(blocks, groups, unit_rows)
-    vec_up = lax.dynamic_index_in_dim(vec_up, my_group, 1, False).reshape(units_here)
-    short = vectors[:, 2 * dim_rows : 8 * dim_rows].reshape(devices, 6, dim_rows)
-    short = jnp.transpose(short, (1, 0, 2)).reshape(6, width)
+    vectors = qkv[:, block_rows * 3 // 2 :, :].reshape(devices, 16 // groups * 128)[:, :short_size]
+    vec_up = vectors[:, 6 * dim_rows : 6 * dim_rows + unit_rows]
+    vec_up = vec_up.reshape(blocks, groups, unit_rows)
+    vec_up = lax.dynamic_index_in_dim(vec_up, my_group, 1, False).reshape(units_here).astype(F32)
+    short = jnp.transpose(vectors[:, : 6 * dim_rows].reshape(devices, 6, dim_rows), (1, 0, 2))
+    short = short.reshape(6, width).astype(F32)
     vec_out, vec_down, gain_one, bias_one, gain_two, bias_two = [short[i] for i in range(6)]
 
-    second = lax.all_gather(after(second, qkv), "blk", axis=0, tiled=False)
-    up_rows = groups * dim_rows * units_here // width
-    mat_up = second[:, :up_rows].reshape(width, units_here)
-    mat_down = second[:, up_rows:].reshape(units_here, width)
+    second = after(second, sent)
+    if units_here == width:
+        second = lax.all_gather(second.reshape(2, unit_rows, width), "blk", axis=1, tiled=True)
+        mat_up, mat_down = second[0], second[1]
+    else:
+        second = lax.all_gather(second, "blk", axis=0, tiled=False)
+        up_rows = groups * dim_rows * units_here // width
+        mat_up = second[:, :up_rows].reshape(width, units_here)
+        mat_down = second[:, up_rows:].reshape(units_here, width)
 
     my_pair = my_block // repeats
     my_part = my_block % repeats
@@ -1095,8 +1088,7 @@
     shard_up = after(shard_up, grads).reshape(groups, dim_rows, units_here)
     shard_up = xor_order(shard_up, 0, my_group)
     up_parts = [shard_up[0]] + [swapped(shard_up[k], "heads", k) for k in range(1, groups)]
-    for part in up_parts[1:]:
-        got = after(got, part)
+    got = after(got, up_parts[-1])
     shard_out = scatter_blk(after(grad_mat_out, got).reshape(blocks, dim_rows, width)).astype(BF16)
     route = [(j, j % groups * blocks + j // groups) for j in range(devices)]
     shard_out = lax.ppermute(shard_out, ("heads", "blk"), route)

time: 343 us -> 341 us (level); the launches traced: 341 us -> 336 us
  waiting for transfers between devices: 126 us -> 138 us
  starting transfers between devices: 75.2 us -> 65.7 us
  local copies, waits for them, and re-layouts: 47.8 us -> 41.1 us
    ppermute x36, starting transfers between devices: 49.4 us -> 40.2 us  [swapped(): return lax.ppermute(block, axis, [(i, i ^ mask) for i in range(count)])]
    ppermute x36, waiting for transfers between devices: 55.7 us -> 61.9 us  [swapped(): return lax.ppermute(block, axis, [(i, i ^ mask) for i in range(count)])]
    all_gather x1, waiting for transfers between devices: 9.8 us -> 4.11 us  [per_device(): lax.all_gather(second.reshape(2, unit_rows, width), 'blk', axis=1, tiled=...]
    unnamed x126 -> x119, local copies, waits for them, and re-layouts: 27 us -> 21.9 us
    all_to_all x1, waiting for transfers between devices: 20.4 us -> 25.2 us  [per_device(): qkv = lax.all_to_all(sent, 'blk', split_axis=0, concat_axis=0, tiled=True)]
    slice x12 -> x10, local copies, waits for them, and re-layouts: 6.99 us -> 6.58 us  [after(): spot = lax.slice(other, (0,) * other.ndim, (1,) * other.ndim).reshape(())]
    pallas_call x13 -> x12, Pallas kernels: 14.4 us -> 14.4 us  [whole_call(): pl.pallas_call(kernel, in_specs=[vmem] * len(arguments), out_specs=[vmem]...]
  transfers between devices with their start and end apart: 46 -> 46, of which waited for: 21 -> 27; matrix products, arithmetic and copies ran while one was open for 9% -> 9% of each run, Pallas kernels for 15% -> 15%
where the time goes in v6:
time: 341 us; the launch traced here: 336 us
  waiting for transfers between devices  138 us (40%)
  starting transfers between devices  65.7 us (19%)
  Pallas kernels  55.9 us (16%)
  local copies, waits for them, and re-layouts  41.1 us (12%)
  between operations  22 us (6%)
  other arithmetic  12.8 us (4%)
    ppermute x36, waiting for transfers between devices, swapped(): return lax.ppermute(block, axis, [(i, i ^ mask) for i in range(count)])  61.9 us
    ppermute x36, starting transfers between devices, swapped(): return lax.ppermute(block, axis, [(i, i ^ mask) for i in range(count)])  40.2 us
    all_to_all x2, waiting for transfers between devices, per_device(): got = lax.all_to_all(sent, ALL, split_axis=0, concat_axis=0, tiled=True)  33.4 us
    all_to_all x1, waiting for transfers between devices, per_device(): qkv = lax.all_to_all(sent, 'blk', split_axis=0, concat_axis=0, tiled=True)  25.2 us
    unnamed x119, local copies, waits for them, and re-layouts  21.9 us
    pallas_call x1, Pallas kernels, attend_back(): pl.pallas_call(attend_back_kernel, grid_spec=pltpu.PrefetchScalarGridSpec...  17.2 us
    pallas_call x12, Pallas kernels, whole_call(): pl.pallas_call(kernel, in_specs=[vmem] * len(arguments), out_specs=[vmem]...  14.4 us
    pallas_call x1, Pallas kernels, attend(): pl.pallas_call(attend_kernel, grid_spec=pltpu.PrefetchScalarGridSpec(num_...  11.9 us
  transfers between devices with their start and end apart: 46, of which 27 were waited for; matrix products, arithmetic and copies ran while one was open for 9% of the time, Pallas kernels for 15%

profile of v6, /device:TPU:0, one launch (start us, length us, event | category | flops | bytes accessed | tf_op | source)
XLA Modules:
  0.0 335.5 jit_solution(16028360260464408200)
XLA Ops:
  12.7 5.2 %all-to-all-start = ((bf16[4,32,1920]{2,1,0:T(8,128)(2,1)}), bf16[4,32,1920]{2,1,0:T(8,128)(2,1)S(1)}, u32[]{:S(2)}, u32[]{:S(2)}) async-start(bf16[4,32,1920]{2,1,0:T(8,128)(2,1)} %pad_maximum_fusion), calls=%async_computation | async-start | bytes 983040 | tf_op jit(solution)/shard_map/all_to_all | solution.py:974
  18.1 3.0 collective-permute-start.2
  21.7 10.2 %all-to-all-done = bf16[4,32,1920]{2,1,0:T(8,128)(2,1)S(1)} async-done(((bf16[4,32,1920]{2,1,0:T(8,128)(2,1)}), bf16[4,32,1920]{2,1,0:T(8,128)(2,1)S(1)}, u32[]{:S(2)}, u32[]{:S(2)}) %all-to-all-start) | async-done | bytes 491552 | tf_op jit(solution)/shard_map/all_to_all | solution.py:974
  44.2 3.7 %collective-permute-done.4 = bf16[128,896]{1,0:T(8,128)(2,1)S(1)} collective-permute-done((bf16[128,896]{1,0:T(8,128)(2,1)S(1)}, bf16[128,896]{1,0:T(8,128)(2,1)S(1)}, u32[]{:S(2)}, u32[]{:S(2)}) %collective-permute-start.4) | collective-permute-done | bytes 229408 | tf_op jit(solution)/shard_map/ppermute | solution.py:42
  50.5 2.8 shard_map.322
  58.3 6.2 %all-to-all-start.1 = ((bf16[8,400,128]{2,1,0:T(8,128)(2,1)}), bf16[8,400,128]{2,1,0:T(8,128)(2,1)S(1)}, u32[]{:S(2)}, u32[]{:S(2)}) async-start(bf16[8,400,128]{2,1,0:T(8,128)(2,1)} %get-tuple-element.70), calls=%async_computation.1 | async-start | bytes 1638400 | tf_op jit(solution)/shard_map/all_to_all | solution.py:990
  65.2 25.2 %all-to-all-done.1.qkv_ref = bf16[8,400,128]{2,1,0:T(8,128)(2,1)S(1)} async-done(((bf16[8,400,128]{2,1,0:T(8,128)(2,1)}), bf16[8,400,128]{2,1,0:T(8,128)(2,1)S(1)}, u32[]{:S(2)}, u32[]{:S(2)}) %all-to-all-start.1) | async-done | bytes 819232 | tf_op jit(solution)/shard_map/all_to_all | solution.py:990
  90.9 11.9 %shard_map.323 = (bf16[32,32,128]{2,1,0:T(8,128)(2,1)}, f32[64,2048]{1,0:T(8,128)S(1)}, f32[8,1,256]{2,1,0:T(1,128)S(1)}) custom-call(s32[4]{0:T(128)S(1)} %pad_add_fusion.spot_ref, s32[8,1,256]{2,1,0:T(1,128)S(1)} %bitcast.142, s32[2048,128]{1,0:T(8,128)S(1)} %broadcast_in_dim.21.seg_key_ref, bf16[8,400,128]{2,1,0:T(8,128)(2,1)S(1)} %all-to-all-done.1.qkv_ref), custom_call_target="tpu_custom_call" | custom-call | tf_op jit(solution)/shard_map/pallas_call | solution.py:205
  103.6 2.9 all-to-all-start.2
  106.9 16.8 %all-to-all-done.2.got_ref = bf16[32,32,128]{2,1,0:T(8,128)(2,1)S(1)} async-done(((bf16[32,32,128]{2,1,0:T(8,128)(2,1)}), bf16[32,32,128]{2,1,0:T(8,128)(2,1)S(1)}, u32[]{:S(2)}, u32[]{:S(2)}) %all-to-all-start.2) | async-done | bytes 262176 | tf_op jit(solution)/shard_map/all_to_all | solution.py:1027
  132.2 4.1 %all-gather.5.cloned.1.call-done = bf16[2,1024,1024]{2,1,0:T(8,128)(2,1)} async-done(((bf16[2,128,1024]{2,1,0:T(8,128)(2,1)}), bf16[2,1024,1024]{2,1,0:T(8,128)(2,1)}) %all-gather.5.cloned.1.call-update) | async-done | bytes 4194320 | tf_op jit(solution)/shard_map/all_gather | solution.py:1003
  139.0 7.1 %collective-permute-done.11.sent_ref.refs_11_.refs_3_ = bf16[128,1280]{1,0:T(8,128)(2,1)S(1)} collective-permute-done((bf16[128,1280]{1,0:T(8,128)(2,1)}, bf16[128,1280]{1,0:T(8,128)(2,1)S(1)}, u32[]{:S(2)}, u32[]{:S(2)}) %collective-permute-start.11) | collective-permute-done | bytes 327712 | tf_op jit(solution)/shard_map/ppermute | solution.py:42
  153.5 3.8 %collective-permute-done.12.refs_8_ = bf16[128,1024]{1,0:T(8,128)(2,1)S(1)} collective-permute-done((bf16[128,1024]{1,0:T(8,128)(2,1)S(1)}, bf16[128,1024]{1,0:T(8,128)(2,1)S(1)}, u32[]{:S(2)}, u32[]{:S(2)}) %collective-permute-start.12) | collective-permute-done | bytes 262176 | tf_op jit(solution)/shard_map/ppermute | solution.py:42
  157.3 3.8 %collective-permute-done.10.refs_7_ = bf16[128,1024]{1,0:T(8,128)(2,1)S(1)} collective-permute-done((bf16[128,1024]{1,0:T(8,128)(2,1)S(1)}, bf16[128,1024]{1,0:T(8,128)(2,1)S(1)}, u32[]{:S(2)}, u32[]{:S(2)}) %collective-permute-start.10) | collective-permute-done | bytes 262176 | tf_op jit(solution)/shard_map/ppermute | solution.py:42
  166.5 6.6 %collective-permute-done.15.grad_ref.refs_7_ = bf16[128,1024]{1,0:T(8,128)(2,1)S(1)} collective-permute-done((bf16[128,1024]{1,0:T(8,128)(2,1)S(1)}, bf16[128,1024]{1,0:T(8,128)(2,1)S(1)}, u32[]{:S(2)}, u32[]{:S(2)}) %collective-permute-start.15) | collective-permute-done | bytes 262176 | tf_op jit(solution)/shard_map/ppermute | solution.py:42
  208.0 2.8 all-to-all-start.3
  212.9 16.6 %all-to-all-done.3.up_ref = bf16[32,48,128]{2,1,0:T(8,128)(2,1)S(1)} async-done(((bf16[32,48,128]{2,1,0:T(8,128)(2,1)}), bf16[32,48,128]{2,1,0:T(8,128)(2,1)S(1)}, u32[]{:S(2)}, u32[]{:S(2)}) %all-to-all-start.3) | async-done | bytes 393248 | tf_op jit(solution)/shard_map/all_to_all | solution.py:1076
  232.3 17.2 %shard_map.336 = bf16[8,384,128]{2,1,0:T(8,128)(2,1)} custom-call(s32[4]{0:T(128)S(1)} %pad_add_fusion.spot_ref, s32[8,1,256]{2,1,0:T(1,128)S(1)} %bitcast.143, s32[2048,128]{1,0:T(8,128)S(1)} %broadcast_in_dim.21.seg_key_ref, bf16[8,400,128]{2,1,0:T(8,128)(2,1)S(1)} %copy-done.5, bf16[32,48,128]{2,1,0:T(8,128)(2,1)S(1)} %all-to-all-done.3.up_ref, ...), custom_call_target="tpu_custom_call" | custom-call | tf_op jit(solution)/shard_map/pallas_call | solution.py:306
  250.8 4.2 %all-to-all-start.4 = ((bf16[8,384,128]{2,1,0:T(8,128)(2,1)}), bf16[8,384,128]{2,1,0:T(8,128)(2,1)}, u32[]{:S(2)}, u32[]{:S(2)}) async-start(bf16[8,384,128]{2,1,0:T(8,128)(2,1)} %shard_map.336), calls=%async_computation.4 | async-start | bytes 1572864 | tf_op jit(solution)/shard_map/all_to_all | solution.py:1087
  265.9 5.5 %collective-permute-done.28.refs_6_ = bf16[128,1024]{1,0:T(8,128)(2,1)S(1)} collective-permute-done((bf16[128,1024]{1,0:T(8,128)(2,1)S(1)}, bf16[128,1024]{1,0:T(8,128)(2,1)S(1)}, u32[]{:S(2)}, u32[]{:S(2)}) %collective-permute-start.28) | collective-permute-done | bytes 262176 | tf_op jit(solution)/shard_map/ppermute | solution.py:42
  278.9 2.7 shard_map.337
  296.2 6.1 %collective-permute-done.24 = bf16[144,768]{1,0:T(8,128)(2,1)S(1)} collective-permute-done((bf16[144,768]{1,0:T(8,128)(2,1)S(1)}, bf16[144,768]{1,0:T(8,128)(2,1)S(1)}, u32[]{:S(2)}, u32[]{:S(2)}) %collective-permute-start.24) | collective-permute-done | bytes 221216 | tf_op jit(solution)/shard_map/ppermute | solution.py:42
  304.3 9.4 %collective-permute-done.25 = bf16[144,768]{1,0:T(8,128)(2,1)S(1)} collective-permute-done((bf16[144,768]{1,0:T(8,128)(2,1)S(1)}, bf16[144,768]{1,0:T(8,128)(2,1)S(1)}, u32[]{:S(2)}, u32[]{:S(2)}) %collective-permute-start.25) | collective-permute-done | bytes 221216 | tf_op jit(solution)/shard_map/ppermute | solution.py:42
  315.5 3.5 %all-to-all-start.5 = ((bf16[4,48,768]{2,1,0:T(8,128)(2,1)}), bf16[4,48,768]{2,1,0:T(8,128)(2,1)S(1)}, u32[]{:S(2)}, u32[]{:S(2)}) async-start(bf16[4,48,768]{2,1,0:T(8,128)(2,1)} %pad_maximum_fusion.2), calls=%async_computation.6 | async-start | bytes 589824 | tf_op jit(solution)/shard_map/all_to_all | solution.py:1121
  (297 shorter events, 132.0 us)
Async XLA Ops:
  7.2 116.5 %all-gather.3.cloned.1.call-start = ((), (), s32[]{:S(2)}) async-start(), calls=%async_computation.7 | async-start | bytes 2162688 | tf_op jit(solution)/shard_map/all_gather | solution.py:978
  12.7 19.3 %all-to-all-start = ((bf16[4,32,1920]{2,1,0:T(8,128)(2,1)}), bf16[4,32,1920]{2,1,0:T(8,128)(2,1)S(1)}, u32[]{:S(2)}, u32[]{:S(2)}) async-start(bf16[4,32,1920]{2,1,0:T(8,128)(2,1)} %pad_maximum_fusion), calls=%async_computation | async-start | bytes 983040 | tf_op jit(solution)/shard_map/all_to_all | solution.py:974
  17.9 118.5 %all-gather.5.cloned.1.call-start = ((), (), s32[]{:S(2)}) async-start(), calls=%async_computation.8 | async-start | bytes 4718592 | tf_op jit(solution)/shard_map/all_gather | solution.py:1003
  18.1 18.2 %collective-permute-start.2 = (bf16[144,1024]{1,0:T(8,128)(2,1)S(1)}, bf16[144,1024]{1,0:T(8,128)(2,1)S(1)}, u32[]{:S(2)}, u32[]{:S(2)}) collective-permute-start(bf16[144,1024]{1,0:T(8,128)(2,1)S(1)} %pad_maximum_fusion.1.refs_0_), channel_id=1, source_target_pairs={{0,24},{8,16},{16,8},{24,0},{1,25},{9,17},{17,9},{25,1},{2,26},{10... | collective-permute-start | bytes 884744 | tf_op jit(solution)/shard_map/ppermute | solution.py:42
  21.1 18.3 %collective-permute-start.1 = (bf16[144,1024]{1,0:T(8,128)(2,1)S(1)}, bf16[144,1024]{1,0:T(8,128)(2,1)S(1)}, u32[]{:S(2)}, u32[]{:S(2)}) collective-permute-start(bf16[144,1024]{1,0:T(8,128)(2,1)S(1)} %pad_maximum_fusion.1.refs_0_), channel_id=1, source_target_pairs={{0,16},{8,24},{16,0},{24,8},{1,17},{9,25},{17,1},{25,9},{2,18},{10... | collective-permute-start | bytes 884744 | tf_op jit(solution)/shard_map/ppermute | solution.py:42
  21.6 19.0 %collective-permute-start = (bf16[144,1024]{1,0:T(8,128)(2,1)S(1)}, bf16[144,1024]{1,0:T(8,128)(2,1)S(1)}, u32[]{:S(2)}, u32[]{:S(2)}) collective-permute-start(bf16[144,1024]{1,0:T(8,128)(2,1)S(1)} %pad_maximum_fusion.1.refs_0_), channel_id=1, source_target_pairs={{0,8},{8,0},{16,24},{24,16},{1,9},{9,1},{17,25},{25,17},{2,10},{10... | collective-permute-start | bytes 884744 | tf_op jit(solution)/shard_map/ppermute | solution.py:42
  32.0 15.8 %collective-permute-start.4 = (bf16[128,896]{1,0:T(8,128)(2,1)S(1)}, bf16[128,896]{1,0:T(8,128)(2,1)S(1)}, u32[]{:S(2)}, u32[]{:S(2)}) collective-permute-start(bf16[128,896]{1,0:T(8,128)(2,1)S(1)} %get-tuple-element.137), channel_id=1, source_target_pairs={{0,4},{1,5},{2,6},{3,7},{4,0},{5,1},{6,2},{7,3},{8,12},{9,13},{10,... | collective-permute-start | bytes 688136 | tf_op jit(solution)/shard_map/ppermute | solution.py:42
  34.7 13.2 %collective-permute-start.3 = (bf16[128,896]{1,0:T(8,128)(2,1)S(1)}, bf16[128,896]{1,0:T(8,128)(2,1)S(1)}, u32[]{:S(2)}, u32[]{:S(2)}) collective-permute-start(bf16[128,896]{1,0:T(8,128)(2,1)S(1)} %get-tuple-element.137), channel_id=1, source_target_pairs={{0,2},{1,3},{2,0},{3,1},{4,6},{5,7},{6,4},{7,5},{8,10},{9,11},{10,... | collective-permute-start | bytes 688136 | tf_op jit(solution)/shard_map/ppermute | solution.py:42
  58.3 32.1 %all-to-all-start.1 = ((bf16[8,400,128]{2,1,0:T(8,128)(2,1)}), bf16[8,400,128]{2,1,0:T(8,128)(2,1)S(1)}, u32[]{:S(2)}, u32[]{:S(2)}) async-start(bf16[8,400,128]{2,1,0:T(8,128)(2,1)} %get-tuple-element.70), calls=%async_computation.1 | async-start | bytes 1638400 | tf_op jit(solution)/shard_map/all_to_all | solution.py:990
  103.6 20.1 %all-to-all-start.2 = ((bf16[32,32,128]{2,1,0:T(8,128)(2,1)}), bf16[32,32,128]{2,1,0:T(8,128)(2,1)S(1)}, u32[]{:S(2)}, u32[]{:S(2)}) async-start(bf16[32,32,128]{2,1,0:T(8,128)(2,1)} %get-tuple-element.71), calls=%async_computation.2 | async-start | bytes 524288 | tf_op jit(solution)/shard_map/all_to_all | solution.py:1027
  106.5 153.4 %reduce-scatter.2.cloned.1.call-start = ((), (), s32[]{:S(2)}) async-start(), calls=%async_computation.9 | async-start | bytes 4718592 | tf_op jit(solution)/shard_map/reduce_scatter | solution.py:1060
  128.7 22.1 %collective-permute-start.7 = (bf16[128,1280]{1,0:T(8,128)(2,1)}, bf16[128,1280]{1,0:T(8,128)(2,1)S(1)}, u32[]{:S(2)}, u32[]{:S(2)}) collective-permute-start(bf16[128,1280]{1,0:T(8,128)(2,1)} %get-tuple-element.76), channel_id=1, source_target_pairs={{0,8},{8,0},{16,24},{24,16},{1,9},{9,1},{17,25},{25,17},{2,10},{10... | collective-permute-start | bytes 983048 | tf_op jit(solution)/shard_map/ppermute | solution.py:42
  129.6 18.8 %collective-permute-start.9 = (bf16[128,1280]{1,0:T(8,128)(2,1)}, bf16[128,1280]{1,0:T(8,128)(2,1)S(1)}, u32[]{:S(2)}, u32[]{:S(2)}) collective-permute-start(bf16[128,1280]{1,0:T(8,128)(2,1)} %get-tuple-element.78), channel_id=1, source_target_pairs={{0,16},{8,24},{16,0},{24,8},{1,17},{9,25},{17,1},{25,9},{2,18},{10... | collective-permute-start | bytes 983048 | tf_op jit(solution)/shard_map/ppermute | solution.py:42
  131.1 15.0 %collective-permute-start.11 = (bf16[128,1280]{1,0:T(8,128)(2,1)}, bf16[128,1280]{1,0:T(8,128)(2,1)S(1)}, u32[]{:S(2)}, u32[]{:S(2)}) collective-permute-start(bf16[128,1280]{1,0:T(8,128)(2,1)} %get-tuple-element.80), channel_id=1, source_target_pairs={{0,24},{8,16},{16,8},{24,0},{1,25},{9,17},{17,9},{25,1},{2,26},{10... | collective-permute-start | bytes 983048 | tf_op jit(solution)/shard_map/ppermute | solution.py:42
  164.1 14.2 %collective-permute-start.14 = (bf16[128,1024]{1,0:T(8,128)(2,1)S(1)}, bf16[128,1024]{1,0:T(8,128)(2,1)S(1)}, u32[]{:S(2)}, u32[]{:S(2)}) collective-permute-start(bf16[128,1024]{1,0:T(8,128)(2,1)S(1)} %get-tuple-element.83.grad_ref.refs_4_), channel_id=1, source_target_pairs={{0,16},{8,24},{16,0},{24,8},{1,17},{9,25},{17,1},{25,9},{2,18},{10... | collective-permute-start | bytes 786440 | tf_op jit(solution)/shard_map/ppermute | solution.py:42
  165.6 14.3 %collective-permute-start.13 = (bf16[128,1024]{1,0:T(8,128)(2,1)S(1)}, bf16[128,1024]{1,0:T(8,128)(2,1)S(1)}, u32[]{:S(2)}, u32[]{:S(2)}) collective-permute-start(bf16[128,1024]{1,0:T(8,128)(2,1)S(1)} %get-tuple-element.83.grad_ref.refs_4_), channel_id=1, source_target_pairs={{0,8},{8,0},{16,24},{24,16},{1,9},{9,1},{17,25},{25,17},{2,10},{10... | collective-permute-start | bytes 786440 | tf_op jit(solution)/shard_map/ppermute | solution.py:42
  208.0 21.5 %all-to-all-start.3 = ((bf16[32,48,128]{2,1,0:T(8,128)(2,1)}), bf16[32,48,128]{2,1,0:T(8,128)(2,1)S(1)}, u32[]{:S(2)}, u32[]{:S(2)}) async-start(bf16[32,48,128]{2,1,0:T(8,128)(2,1)} %copy-done.28), calls=%async_computation.3 | async-start | bytes 786432 | tf_op jit(solution)/shard_map/all_to_all | solution.py:1076
  250.8 25.2 %all-to-all-start.4 = ((bf16[8,384,128]{2,1,0:T(8,128)(2,1)}), bf16[8,384,128]{2,1,0:T(8,128)(2,1)}, u32[]{:S(2)}, u32[]{:S(2)}) async-start(bf16[8,384,128]{2,1,0:T(8,128)(2,1)} %shard_map.336), calls=%async_computation.4 | async-start | bytes 1572864 | tf_op jit(solution)/shard_map/all_to_all | solution.py:1087
  258.2 13.2 %collective-permute-start.28 = (bf16[128,1024]{1,0:T(8,128)(2,1)S(1)}, bf16[128,1024]{1,0:T(8,128)(2,1)S(1)}, u32[]{:S(2)}, u32[]{:S(2)}) collective-permute-start(bf16[128,1024]{1,0:T(8,128)(2,1)S(1)} %broadcast_add_fusion.3.refs_4_), channel_id=1, source_target_pairs={{0,16},{8,24},{16,0},{24,8},{1,17},{9,25},{17,1},{25,9},{2,18},{10... | collective-permute-start | bytes 786440 | tf_op jit(solution)/shard_map/ppermute | solution.py:42
  282.7 42.5 %collective-permute-start.36 = (bf16[32,1024]{1,0:T(8,128)(2,1)}, bf16[32,1024]{1,0:T(8,128)(2,1)S(1)}, u32[]{:S(2)}, u32[]{:S(2)}) collective-permute-start(bf16[32,1024]{1,0:T(8,128)(2,1)} %get-tuple-element.138), channel_id=1, source_target_pairs={{0,16},{8,24},{16,0},{24,8},{1,17},{9,25},{17,1},{25,9},{2,18},{10... | collective-permute-start | bytes 196616 | tf_op jit(solution)/shard_map/ppermute | solution.py:42
  284.2 41.0 %collective-permute-start.35 = (bf16[32,1024]{1,0:T(8,128)(2,1)S(1)}, bf16[32,1024]{1,0:T(8,128)(2,1)}, u32[]{:S(2)}, u32[]{:S(2)}) collective-permute-start(bf16[32,1024]{1,0:T(8,128)(2,1)S(1)} %get-tuple-element.139), channel_id=1, source_target_pairs={{0,8},{8,0},{16,24},{24,16},{1,9},{9,1},{17,25},{25,17},{2,10},{10... | collective-permute-start | bytes 196616 | tf_op jit(solution)/shard_map/ppermute | solution.py:42
  295.5 18.2 %collective-permute-start.25 = (bf16[144,768]{1,0:T(8,128)(2,1)S(1)}, bf16[144,768]{1,0:T(8,128)(2,1)S(1)}, u32[]{:S(2)}, u32[]{:S(2)}) collective-permute-start(bf16[144,768]{1,0:T(8,128)(2,1)S(1)} %get-tuple-element.128), channel_id=1, source_target_pairs={{0,4},{1,5},{2,6},{3,7},{4,0},{5,1},{6,2},{7,3},{8,12},{9,13},{10,... | collective-permute-start | bytes 663560 | tf_op jit(solution)/shard_map/ppermute | solution.py:42
  302.3 16.6 %collective-permute-start.20 = (bf16[128,1024]{1,0:T(8,128)(2,1)S(1)}, bf16[128,1024]{1,0:T(8,128)(2,1)S(1)}, u32[]{:S(2)}, u32[]{:S(2)}) collective-permute-start(bf16[128,1024]{1,0:T(8,128)(2,1)S(1)} %get-tuple-element.131), channel_id=1, source_target_pairs={{0,8},{8,0},{16,24},{24,16},{1,9},{9,1},{17,25},{25,17},{2,10},{10... | collective-permute-start | bytes 786440 | tf_op jit(solution)/shard_map/ppermute | solution.py:42
  303.5 16.1 %collective-permute-start.22 = (bf16[128,1024]{1,0:T(8,128)(2,1)S(1)}, bf16[128,1024]{1,0:T(8,128)(2,1)S(1)}, u32[]{:S(2)}, u32[]{:S(2)}) collective-permute-start(bf16[128,1024]{1,0:T(8,128)(2,1)S(1)} %get-tuple-element.132), channel_id=1, source_target_pairs={{0,24},{8,16},{16,8},{24,0},{1,25},{9,17},{17,9},{25,1},{2,26},{10... | collective-permute-start | bytes 786440 | tf_op jit(solution)/shard_map/ppermute | solution.py:42
  (78 other events, 724.6 us)
Sparse Core Ops, SparseCore 0:
  10.9 69.3 all-gather.2
  82.5 53.7 all-gather.4
  189.3 53.5 reduce-scatter.1

commit v7 on v6

--- a/solution.py
+++ b/solution.py
@@ -351,7 +351,7 @@
     seqs, heads_here, repeats, spot_ref, got_ref, tokens_ref, flags_ref, mat_ref, vectors_ref,
     *refs,
 ):
-    sents, (normed_ref, unit_ref, inv_ref, squares_ref, attn) = refs[:-5], refs[-5:]
+    sents, (low_ref, normed_ref, unit_ref, inv_ref, squares_ref, attn) = refs[:-6], refs[-6:]
     my_group, part = spot_ref[1], spot_ref[3]
     groups = len(sents)
     wide = got_ref.shape[1]
@@ -378,14 +378,13 @@
     normed_ref[...] = normed
     unit_ref[...] = unit
     inv_ref[...] = jnp.broadcast_to(inv_std, inv_ref.shape)
-    low = normed.astype(BF16)
+    low_ref[...] = normed.astype(BF16)
     for k in range(groups):
-        sents[k][:, 0:width] = low
         for group in range(groups):
 
             @pl.when((my_group ^ k) == group)
             def _():
-                sents[k][:, width:] = attn[:, group * width_here : (group + 1) * width_here]
+                sents[k][...] = attn[:, group * width_here : (group + 1) * width_here]
 
     lane = lax.broadcasted_iota(jnp.int32, squares_ref.shape, 1)
     total = jnp.zeros(squares_ref.shape, F32)
@@ -402,9 +401,10 @@
     return pl.pallas_call(
         functools.partial(join_kernel, seqs, heads_here, repeats),
         in_specs=[pl.BlockSpec(memory_space=pltpu.SMEM)] + [vmem] * 5,
-        out_specs=[vmem] * (groups + 4),
-        out_shape=[jax.ShapeDtypeStruct((rows, width + heads_here * HEAD_DIM), BF16)] * groups
+        out_specs=[vmem] * (groups + 5),
+        out_shape=[jax.ShapeDtypeStruct((rows, heads_here * HEAD_DIM), BF16)] * groups
         + [
+            jax.ShapeDtypeStruct((rows, width), BF16),
             jax.ShapeDtypeStruct((rows, width), F32),
             jax.ShapeDtypeStruct((rows, width), F32),
             jax.ShapeDtypeStruct((rows, 128), F32),
@@ -886,7 +886,7 @@
     rows, width = grads[0].shape
     for k in range(groups):
         spot = slice(k * rows, (k + 1) * rows)
-        left[spot, :] = sents[k][:, width:]
+        left[spot, :] = sents[k][...]
         right[spot, :] = grads[k][...]
     out_ref[...] = matmul_tn(left[...], right[...]).astype(BF16)
 
@@ -894,7 +894,7 @@
 def out_grads_call(sents, grads):
     groups = len(sents)
     rows, width = grads[0].shape
-    columns = sents[0].shape[1] - width
+    columns = sents[0].shape[1]
     return whole_call(
         functools.partial(out_grads_kernel, groups),
         [jax.ShapeDtypeStruct((columns, width), BF16)],
@@ -1028,10 +1028,10 @@
     my_span = my_block * groups + my_group
     local_flags = lax.dynamic_slice_in_dim(valid_flags, my_span * span, span, 1)
     local_flags = local_flags.reshape(rows, 1).astype(F32)
-    *sent, normed_one, unit_one, inv_one, squares = join(
+    *attn_sent, normed_low, normed_one, unit_one, inv_one, squares = join(
         spot, got, token_rows, local_flags, mat_out, short, seqs, heads_here, repeats
     )
-    joint_parts = [sent[0]] + [swapped(sent[k], "heads", k) for k in range(1, groups)]
+    joint_parts = gather_parts(normed_low, "heads")
     ffn_results = [
         ffn_part(part, mat_up, mat_down, vec_up[None], F32 if k == 0 else BF16)
         for k, part in enumerate(joint_parts)
@@ -1081,9 +1081,13 @@
     real_count = jnp.maximum(jnp.sum(valid_flags.astype(F32)), 1.0)
     rms = jnp.sqrt(small[7, :4] / (real_count * width))
 
+    attn_parts = [attn_sent[0]] + [
+        swapped(after(attn_sent[k], grad_branch), "heads", k) for k in range(1, groups)
+    ]
+    got = after(got, attn_parts[-1])
     grads = attend_back(spot, seg_row, seg_key, qkv, got, attn_t, lse)
     branch_parts = gather_parts(after(grad_branch, grads), "heads")
-    grad_mat_out = out_grads_call(joint_parts, branch_parts)
+    grad_mat_out = out_grads_call(attn_parts, branch_parts)
     got = lax.all_to_all(grads, "blk", split_axis=0, concat_axis=0, tiled=True)
     shard_up = after(shard_up, grads).reshape(groups, dim_rows, units_here)
     shard_up = xor_order(shard_up, 0, my_group)

time: 341 us -> 336 us (0.985)
  waiting for transfers between devices: 138 us -> 125 us
  starting transfers between devices: 65.7 us -> 70 us
  local copies, waits for them, and re-layouts: 41.1 us -> 44.9 us
    all_to_all x2, waiting for transfers between devices: 33.4 us -> 26.2 us  [per_device(): got = lax.all_to_all(sent, ALL, split_axis=0, concat_axis=0, tiled=True)]
    ppermute x36 -> x39, starting transfers between devices: 40.2 us -> 45.3 us  [swapped(): return lax.ppermute(block, axis, [(i, i ^ mask) for i in range(count)])]
    all_gather x1, waiting for transfers between devices: 4.11 us -> 0.69 us  [per_device(): lax.all_gather(second.reshape(2, unit_rows, width), 'blk', axis=1, tiled=...]
    ppermute x36 -> x39, waiting for transfers between devices: 61.9 us -> 59.8 us  [swapped(): return lax.ppermute(block, axis, [(i, i ^ mask) for i in range(count)])]
    unnamed x119 -> x117, local copies, waits for them, and re-layouts: 21.9 us -> 23.8 us
    slice x10 -> x12, local copies, waits for them, and re-layouts: 6.58 us -> 7.65 us  [after(): spot = lax.slice(other, (0,) * other.ndim, (1,) * other.ndim).reshape(())]
  transfers between devices with their start and end apart: 46 -> 49, of which waited for: 27 -> 26; matrix products, arithmetic and copies ran while one was open for 9% -> 10% of each run, Pallas kernels for 15% -> 15%
where the time goes in v7:
time: 336 us; the launch traced here: 331 us
  waiting for transfers between devices  125 us (37%)
  starting transfers between devices  70 us (21%)
  Pallas kernels  54.9 us (16%)
  local copies, waits for them, and re-layouts  44.9 us (13%)
  between operations  23.5 us (7%)
  other arithmetic  13.1 us (4%)
    ppermute x39, waiting for transfers between devices, swapped(): return lax.ppermute(block, axis, [(i, i ^ mask) for i in range(count)])  59.8 us
    ppermute x39, starting transfers between devices, swapped(): return lax.ppermute(block, axis, [(i, i ^ mask) for i in range(count)])  45.3 us
    all_to_all x2, waiting for transfers between devices, per_device(): got = lax.all_to_all(sent, ALL, split_axis=0, concat_axis=0, tiled=True)  26.2 us
    all_to_all x1, waiting for transfers between devices, per_device(): qkv = lax.all_to_all(sent, 'blk', split_axis=0, concat_axis=0, tiled=True)  24.6 us
    unnamed x117, local copies, waits for them, and re-layouts  23.8 us
    pallas_call x1, Pallas kernels, attend_back(): pl.pallas_call(attend_back_kernel, grid_spec=pltpu.PrefetchScalarGridSpec...  17.2 us
    pallas_call x12, Pallas kernels, whole_call(): pl.pallas_call(kernel, in_specs=[vmem] * len(arguments), out_specs=[vmem]...  14.4 us
    pallas_call x1, Pallas kernels, attend(): pl.pallas_call(attend_kernel, grid_spec=pltpu.PrefetchScalarGridSpec(num_...  11.9 us
  transfers between devices with their start and end apart: 49, of which 26 were waited for; matrix products, arithmetic and copies ran while one was open for 10% of the time, Pallas kernels for 15%

profile of v7, /device:TPU:0, one launch (start us, length us, event | category | flops | bytes accessed | tf_op | source)
XLA Modules:
  0.0 331.1 jit_solution(15393885814523812451)
XLA Ops:
  12.7 5.2 %all-to-all-start = ((bf16[4,32,1920]{2,1,0:T(8,128)(2,1)}), bf16[4,32,1920]{2,1,0:T(8,128)(2,1)S(1)}, u32[]{:S(2)}, u32[]{:S(2)}) async-start(bf16[4,32,1920]{2,1,0:T(8,128)(2,1)} %pad_maximum_fusion), calls=%async_computation | async-start | bytes 983040 | tf_op jit(solution)/shard_map/all_to_all | solution.py:974
  18.1 3.0 collective-permute-start.2
  21.7 10.2 %all-to-all-done = bf16[4,32,1920]{2,1,0:T(8,128)(2,1)S(1)} async-done(((bf16[4,32,1920]{2,1,0:T(8,128)(2,1)}), bf16[4,32,1920]{2,1,0:T(8,128)(2,1)S(1)}, u32[]{:S(2)}, u32[]{:S(2)}) %all-to-all-start) | async-done | bytes 491552 | tf_op jit(solution)/shard_map/all_to_all | solution.py:974
  32.0 2.7 collective-permute-start.4
  43.3 4.5 %collective-permute-done.4 = bf16[128,896]{1,0:T(8,128)(2,1)S(1)} collective-permute-done((bf16[128,896]{1,0:T(8,128)(2,1)S(1)}, bf16[128,896]{1,0:T(8,128)(2,1)S(1)}, u32[]{:S(2)}, u32[]{:S(2)}) %collective-permute-start.4) | collective-permute-done | bytes 229408 | tf_op jit(solution)/shard_map/ppermute | solution.py:42
  59.7 6.2 %all-to-all-start.1 = ((bf16[8,400,128]{2,1,0:T(8,128)(2,1)}), bf16[8,400,128]{2,1,0:T(8,128)(2,1)S(1)}, u32[]{:S(2)}, u32[]{:S(2)}) async-start(bf16[8,400,128]{2,1,0:T(8,128)(2,1)} %copy-done.12), calls=%async_computation.1 | async-start | bytes 1638400 | tf_op jit(solution)/shard_map/all_to_all | solution.py:990
  66.5 24.6 %all-to-all-done.1.qkv_ref = bf16[8,400,128]{2,1,0:T(8,128)(2,1)S(1)} async-done(((bf16[8,400,128]{2,1,0:T(8,128)(2,1)}), bf16[8,400,128]{2,1,0:T(8,128)(2,1)S(1)}, u32[]{:S(2)}, u32[]{:S(2)}) %all-to-all-start.1) | async-done | bytes 819232 | tf_op jit(solution)/shard_map/all_to_all | solution.py:990
  91.6 11.9 %shard_map.323 = (bf16[32,32,128]{2,1,0:T(8,128)(2,1)}, f32[64,2048]{1,0:T(8,128)S(1)}, f32[8,1,256]{2,1,0:T(1,128)S(1)}) custom-call(s32[4]{0:T(128)S(1)} %pad_add_fusion.spot_ref, s32[8,1,256]{2,1,0:T(1,128)S(1)} %bitcast.144, s32[2048,128]{1,0:T(8,128)S(1)} %broadcast_in_dim.21.seg_key_ref, bf16[8,400,128]{2,1,0:T(8,128)(2,1)S(1)} %all-to-all-done.1.qkv_ref), custom_call_target="tpu_custom_call" | custom-call | tf_op jit(solution)/shard_map/pallas_call | solution.py:205
  107.9 17.2 %all-to-all-done.2.got_ref = bf16[32,32,128]{2,1,0:T(8,128)(2,1)S(1)} async-done(((bf16[32,32,128]{2,1,0:T(8,128)(2,1)}), bf16[32,32,128]{2,1,0:T(8,128)(2,1)S(1)}, u32[]{:S(2)}, u32[]{:S(2)}) %all-to-all-start.2) | async-done | bytes 262176 | tf_op jit(solution)/shard_map/all_to_all | solution.py:1027
  135.4 2.7 slice_bitcast_fusion
  138.1 7.6 %collective-permute-done.7.sent_ref.refs_9_ = bf16[128,1024]{1,0:T(8,128)(2,1)S(1)} collective-permute-done((bf16[128,1024]{1,0:T(8,128)(2,1)S(1)}, bf16[128,1024]{1,0:T(8,128)(2,1)S(1)}, u32[]{:S(2)}, u32[]{:S(2)}) %collective-permute-start.7) | collective-permute-done | bytes 262176 | tf_op jit(solution)/shard_map/ppermute | solution.py:42
  153.0 2.8 collective-permute-done.8.refs_6_
  155.8 5.2 %collective-permute-done.10.refs_7_ = bf16[128,1024]{1,0:T(8,128)(2,1)S(1)} collective-permute-done((bf16[128,1024]{1,0:T(8,128)(2,1)S(1)}, bf16[128,1024]{1,0:T(8,128)(2,1)S(1)}, u32[]{:S(2)}, u32[]{:S(2)}) %collective-permute-start.10) | collective-permute-done | bytes 262176 | tf_op jit(solution)/shard_map/ppermute | solution.py:42
  167.6 6.7 %collective-permute-done.15.grad_ref.refs_7_ = bf16[128,1024]{1,0:T(8,128)(2,1)S(1)} collective-permute-done((bf16[128,1024]{1,0:T(8,128)(2,1)S(1)}, bf16[128,1024]{1,0:T(8,128)(2,1)S(1)}, u32[]{:S(2)}, u32[]{:S(2)}) %collective-permute-start.15) | collective-permute-done | bytes 262176 | tf_op jit(solution)/shard_map/ppermute | solution.py:42
  202.7 3.0 shard_map.335
  207.2 2.9 all-to-all-start.3
  219.7 9.1 %all-to-all-done.3 = bf16[32,48,128]{2,1,0:T(8,128)(2,1)S(1)} async-done(((bf16[32,48,128]{2,1,0:T(8,128)(2,1)}), bf16[32,48,128]{2,1,0:T(8,128)(2,1)S(1)}, u32[]{:S(2)}, u32[]{:S(2)}) %all-to-all-start.3) | async-done | bytes 393248 | tf_op jit(solution)/shard_map/all_to_all | solution.py:1076
  229.5 17.2 %shard_map.336 = bf16[8,384,128]{2,1,0:T(8,128)(2,1)} custom-call(s32[4]{0:T(128)S(1)} %pad_add_fusion.spot_ref, s32[8,1,256]{2,1,0:T(1,128)S(1)} %bitcast.145, s32[2048,128]{1,0:T(8,128)S(1)} %broadcast_in_dim.21.seg_key_ref, bf16[8,400,128]{2,1,0:T(8,128)(2,1)S(1)} %copy-done.5, bf16[32,48,128]{2,1,0:T(8,128)(2,1)S(1)} %broadcast_add_fusion.3.up_ref, ...), custom_call_target="tpu_custom_call" | custom-call | tf_op jit(solution)/shard_map/pallas_call | solution.py:306
  247.9 3.5 %all-to-all-start.4 = ((bf16[8,384,128]{2,1,0:T(8,128)(2,1)}), bf16[8,384,128]{2,1,0:T(8,128)(2,1)S(1)}, u32[]{:S(2)}, u32[]{:S(2)}) async-start(bf16[8,384,128]{2,1,0:T(8,128)(2,1)} %shard_map.336), calls=%async_computation.4 | async-start | bytes 1572864 | tf_op jit(solution)/shard_map/all_to_all | solution.py:1091
  262.2 5.5 %collective-permute-done.31.refs_6_ = bf16[128,1024]{1,0:T(8,128)(2,1)S(1)} collective-permute-done((bf16[128,1024]{1,0:T(8,128)(2,1)S(1)}, bf16[128,1024]{1,0:T(8,128)(2,1)S(1)}, u32[]{:S(2)}, u32[]{:S(2)}) %collective-permute-start.31) | collective-permute-done | bytes 262176 | tf_op jit(solution)/shard_map/ppermute | solution.py:42
  274.1 2.7 shard_map.337
  292.3 5.7 %collective-permute-done.25 = bf16[144,768]{1,0:T(8,128)(2,1)S(1)} collective-permute-done((bf16[144,768]{1,0:T(8,128)(2,1)S(1)}, bf16[144,768]{1,0:T(8,128)(2,1)S(1)}, u32[]{:S(2)}, u32[]{:S(2)}) %collective-permute-start.25) | collective-permute-done | bytes 221216 | tf_op jit(solution)/shard_map/ppermute | solution.py:42
  300.1 9.7 %collective-permute-done.26 = bf16[144,768]{1,0:T(8,128)(2,1)S(1)} collective-permute-done((bf16[144,768]{1,0:T(8,128)(2,1)S(1)}, bf16[144,768]{1,0:T(8,128)(2,1)S(1)}, u32[]{:S(2)}, u32[]{:S(2)}) %collective-permute-start.26) | collective-permute-done | bytes 221216 | tf_op jit(solution)/shard_map/ppermute | solution.py:42
  311.5 3.5 %all-to-all-start.5 = ((bf16[4,48,768]{2,1,0:T(8,128)(2,1)}), bf16[4,48,768]{2,1,0:T(8,128)(2,1)S(1)}, u32[]{:S(2)}, u32[]{:S(2)}) async-start(bf16[4,48,768]{2,1,0:T(8,128)(2,1)} %pad_maximum_fusion.2), calls=%async_computation.6 | async-start | bytes 589824 | tf_op jit(solution)/shard_map/all_to_all | solution.py:1125
  (307 shorter events, 134.3 us)
Async XLA Ops:
  7.2 117.8 %all-gather.3.cloned.1.call-start = ((), (), s32[]{:S(2)}) async-start(), calls=%async_computation.7 | async-start | bytes 2162688 | tf_op jit(solution)/shard_map/all_gather | solution.py:978
  12.7 19.3 %all-to-all-start = ((bf16[4,32,1920]{2,1,0:T(8,128)(2,1)}), bf16[4,32,1920]{2,1,0:T(8,128)(2,1)S(1)}, u32[]{:S(2)}, u32[]{:S(2)}) async-start(bf16[4,32,1920]{2,1,0:T(8,128)(2,1)} %pad_maximum_fusion), calls=%async_computation | async-start | bytes 983040 | tf_op jit(solution)/shard_map/all_to_all | solution.py:974
  17.9 117.5 %all-gather.5.cloned.1.call-start = ((), (), s32[]{:S(2)}) async-start(), calls=%async_computation.8 | async-start | bytes 4718592 | tf_op jit(solution)/shard_map/all_gather | solution.py:1003
  18.1 18.2 %collective-permute-start.2 = (bf16[144,1024]{1,0:T(8,128)(2,1)S(1)}, bf16[144,1024]{1,0:T(8,128)(2,1)S(1)}, u32[]{:S(2)}, u32[]{:S(2)}) collective-permute-start(bf16[144,1024]{1,0:T(8,128)(2,1)S(1)} %pad_maximum_fusion.1.refs_0_), channel_id=1, source_target_pairs={{0,24},{8,16},{16,8},{24,0},{1,25},{9,17},{17,9},{25,1},{2,26},{10... | collective-permute-start | bytes 884744 | tf_op jit(solution)/shard_map/ppermute | solution.py:42
  21.1 18.3 %collective-permute-start.1 = (bf16[144,1024]{1,0:T(8,128)(2,1)S(1)}, bf16[144,1024]{1,0:T(8,128)(2,1)S(1)}, u32[]{:S(2)}, u32[]{:S(2)}) collective-permute-start(bf16[144,1024]{1,0:T(8,128)(2,1)S(1)} %pad_maximum_fusion.1.refs_0_), channel_id=1, source_target_pairs={{0,16},{8,24},{16,0},{24,8},{1,17},{9,25},{17,1},{25,9},{2,18},{10... | collective-permute-start | bytes 884744 | tf_op jit(solution)/shard_map/ppermute | solution.py:42
  21.7 19.0 %collective-permute-start = (bf16[144,1024]{1,0:T(8,128)(2,1)S(1)}, bf16[144,1024]{1,0:T(8,128)(2,1)S(1)}, u32[]{:S(2)}, u32[]{:S(2)}) collective-permute-start(bf16[144,1024]{1,0:T(8,128)(2,1)S(1)} %pad_maximum_fusion.1.refs_0_), channel_id=1, source_target_pairs={{0,8},{8,0},{16,24},{24,16},{1,9},{9,1},{17,25},{25,17},{2,10},{10... | collective-permute-start | bytes 884744 | tf_op jit(solution)/shard_map/ppermute | solution.py:42
  32.0 15.8 %collective-permute-start.4 = (bf16[128,896]{1,0:T(8,128)(2,1)S(1)}, bf16[128,896]{1,0:T(8,128)(2,1)S(1)}, u32[]{:S(2)}, u32[]{:S(2)}) collective-permute-start(bf16[128,896]{1,0:T(8,128)(2,1)S(1)} %get-tuple-element.139), channel_id=1, source_target_pairs={{0,4},{1,5},{2,6},{3,7},{4,0},{5,1},{6,2},{7,3},{8,12},{9,13},{10,... | collective-permute-start | bytes 688136 | tf_op jit(solution)/shard_map/ppermute | solution.py:42
  34.7 13.2 %collective-permute-start.3 = (bf16[128,896]{1,0:T(8,128)(2,1)S(1)}, bf16[128,896]{1,0:T(8,128)(2,1)S(1)}, u32[]{:S(2)}, u32[]{:S(2)}) collective-permute-start(bf16[128,896]{1,0:T(8,128)(2,1)S(1)} %get-tuple-element.139), channel_id=1, source_target_pairs={{0,2},{1,3},{2,0},{3,1},{4,6},{5,7},{6,4},{7,5},{8,10},{9,11},{10,... | collective-permute-start | bytes 688136 | tf_op jit(solution)/shard_map/ppermute | solution.py:42
  59.7 31.5 %all-to-all-start.1 = ((bf16[8,400,128]{2,1,0:T(8,128)(2,1)}), bf16[8,400,128]{2,1,0:T(8,128)(2,1)S(1)}, u32[]{:S(2)}, u32[]{:S(2)}) async-start(bf16[8,400,128]{2,1,0:T(8,128)(2,1)} %copy-done.12), calls=%async_computation.1 | async-start | bytes 1638400 | tf_op jit(solution)/shard_map/all_to_all | solution.py:990
  104.9 20.1 %all-to-all-start.2 = ((bf16[32,32,128]{2,1,0:T(8,128)(2,1)}), bf16[32,32,128]{2,1,0:T(8,128)(2,1)S(1)}, u32[]{:S(2)}, u32[]{:S(2)}) async-start(bf16[32,32,128]{2,1,0:T(8,128)(2,1)} %get-tuple-element.72), calls=%async_computation.2 | async-start | bytes 524288 | tf_op jit(solution)/shard_map/all_to_all | solution.py:1027
  107.5 148.8 %reduce-scatter.2.cloned.1.call-start = ((), (), s32[]{:S(2)}) async-start(), calls=%async_computation.9 | async-start | bytes 4718592 | tf_op jit(solution)/shard_map/reduce_scatter | solution.py:1060
  131.2 17.7 %collective-permute-start.11 = (bf16[128,1024]{1,0:T(8,128)(2,1)S(1)}, bf16[128,1024]{1,0:T(8,128)(2,1)S(1)}, u32[]{:S(2)}, u32[]{:S(2)}) collective-permute-start(bf16[128,1024]{1,0:T(8,128)(2,1)S(1)} %get-tuple-element.73.sent_ref.refs_8_), channel_id=1, source_target_pairs={{0,24},{8,16},{16,8},{24,0},{1,25},{9,17},{17,9},{25,1},{2,26},{10... | collective-permute-start | bytes 786440 | tf_op jit(solution)/shard_map/ppermute | solution.py:42
  132.8 14.6 %collective-permute-start.9 = (bf16[128,1024]{1,0:T(8,128)(2,1)S(1)}, bf16[128,1024]{1,0:T(8,128)(2,1)S(1)}, u32[]{:S(2)}, u32[]{:S(2)}) collective-permute-start(bf16[128,1024]{1,0:T(8,128)(2,1)S(1)} %get-tuple-element.73.sent_ref.refs_8_), channel_id=1, source_target_pairs={{0,16},{8,24},{16,0},{24,8},{1,17},{9,25},{17,1},{25,9},{2,18},{10... | collective-permute-start | bytes 786440 | tf_op jit(solution)/shard_map/ppermute | solution.py:42
  165.5 14.1 %collective-permute-start.14 = (bf16[128,1024]{1,0:T(8,128)(2,1)S(1)}, bf16[128,1024]{1,0:T(8,128)(2,1)S(1)}, u32[]{:S(2)}, u32[]{:S(2)}) collective-permute-start(bf16[128,1024]{1,0:T(8,128)(2,1)S(1)} %get-tuple-element.81.grad_ref.refs_4_), channel_id=1, source_target_pairs={{0,16},{8,24},{16,0},{24,8},{1,17},{9,25},{17,1},{25,9},{2,18},{10... | collective-permute-start | bytes 786440 | tf_op jit(solution)/shard_map/ppermute | solution.py:42
  167.3 13.8 %collective-permute-start.13 = (bf16[128,1024]{1,0:T(8,128)(2,1)S(1)}, bf16[128,1024]{1,0:T(8,128)(2,1)S(1)}, u32[]{:S(2)}, u32[]{:S(2)}) collective-permute-start(bf16[128,1024]{1,0:T(8,128)(2,1)S(1)} %get-tuple-element.81.grad_ref.refs_4_), channel_id=1, source_target_pairs={{0,8},{8,0},{16,24},{24,16},{1,9},{9,1},{17,25},{25,17},{2,10},{10... | collective-permute-start | bytes 786440 | tf_op jit(solution)/shard_map/ppermute | solution.py:42
  207.2 21.6 %all-to-all-start.3 = ((bf16[32,48,128]{2,1,0:T(8,128)(2,1)}), bf16[32,48,128]{2,1,0:T(8,128)(2,1)S(1)}, u32[]{:S(2)}, u32[]{:S(2)}) async-start(bf16[32,48,128]{2,1,0:T(8,128)(2,1)} %get-tuple-element.105), calls=%async_computation.3 | async-start | bytes 786432 | tf_op jit(solution)/shard_map/all_to_all | solution.py:1076
  216.9 42.0 %collective-permute-start.29 = (bf16[128,256]{1,0:T(8,128)(2,1)S(1)}, bf16[128,256]{1,0:T(8,128)(2,1)S(1)}, u32[]{:S(2)}, u32[]{:S(2)}) collective-permute-start(bf16[128,256]{1,0:T(8,128)(2,1)S(1)} %broadcast_add_fusion.6), channel_id=1, source_target_pairs={{0,16},{8,24},{16,0},{24,8},{1,17},{9,25},{17,1},{25,9},{2,18},{10... | collective-permute-start | bytes 196616 | tf_op jit(solution)/shard_map/ppermute | solution.py:42
  217.4 44.4 %collective-permute-start.28 = (bf16[128,256]{1,0:T(8,128)(2,1)S(1)}, bf16[128,256]{1,0:T(8,128)(2,1)S(1)}, u32[]{:S(2)}, u32[]{:S(2)}) collective-permute-start(bf16[128,256]{1,0:T(8,128)(2,1)S(1)} %broadcast_add_fusion.7), channel_id=1, source_target_pairs={{0,8},{8,0},{16,24},{24,16},{1,9},{9,1},{17,25},{25,17},{2,10},{10... | collective-permute-start | bytes 196616 | tf_op jit(solution)/shard_map/ppermute | solution.py:42
  247.9 24.4 %all-to-all-start.4 = ((bf16[8,384,128]{2,1,0:T(8,128)(2,1)}), bf16[8,384,128]{2,1,0:T(8,128)(2,1)S(1)}, u32[]{:S(2)}, u32[]{:S(2)}) async-start(bf16[8,384,128]{2,1,0:T(8,128)(2,1)} %shard_map.336), calls=%async_computation.4 | async-start | bytes 1572864 | tf_op jit(solution)/shard_map/all_to_all | solution.py:1091
  277.9 43.4 %collective-permute-start.39 = (bf16[32,1024]{1,0:T(8,128)(2,1)}, bf16[32,1024]{1,0:T(8,128)(2,1)}, u32[]{:S(2)}, u32[]{:S(2)}) collective-permute-start(bf16[32,1024]{1,0:T(8,128)(2,1)} %get-tuple-element.140), channel_id=1, source_target_pairs={{0,16},{8,24},{16,0},{24,8},{1,17},{9,25},{17,1},{25,9},{2,18},{10... | collective-permute-start | bytes 196616 | tf_op jit(solution)/shard_map/ppermute | solution.py:42
  279.4 41.9 %collective-permute-start.38 = (bf16[32,1024]{1,0:T(8,128)(2,1)S(1)}, bf16[32,1024]{1,0:T(8,128)(2,1)}, u32[]{:S(2)}, u32[]{:S(2)}) collective-permute-start(bf16[32,1024]{1,0:T(8,128)(2,1)S(1)} %get-tuple-element.141), channel_id=1, source_target_pairs={{0,8},{8,0},{16,24},{24,16},{1,9},{9,1},{17,25},{25,17},{2,10},{10... | collective-permute-start | bytes 196616 | tf_op jit(solution)/shard_map/ppermute | solution.py:42
  291.6 18.2 %collective-permute-start.26 = (bf16[144,768]{1,0:T(8,128)(2,1)S(1)}, bf16[144,768]{1,0:T(8,128)(2,1)S(1)}, u32[]{:S(2)}, u32[]{:S(2)}) collective-permute-start(bf16[144,768]{1,0:T(8,128)(2,1)S(1)} %get-tuple-element.130), channel_id=1, source_target_pairs={{0,4},{1,5},{2,6},{3,7},{4,0},{5,1},{6,2},{7,3},{8,12},{9,13},{10,... | collective-permute-start | bytes 663560 | tf_op jit(solution)/shard_map/ppermute | solution.py:42
  298.0 17.0 %collective-permute-start.21 = (bf16[128,1024]{1,0:T(8,128)(2,1)}, bf16[128,1024]{1,0:T(8,128)(2,1)S(1)}, u32[]{:S(2)}, u32[]{:S(2)}) collective-permute-start(bf16[128,1024]{1,0:T(8,128)(2,1)} %get-tuple-element.133), channel_id=1, source_target_pairs={{0,8},{8,0},{16,24},{24,16},{1,9},{9,1},{17,25},{25,17},{2,10},{10... | collective-permute-start | bytes 786440 | tf_op jit(solution)/shard_map/ppermute | solution.py:42
  299.6 16.0 %collective-permute-start.23 = (bf16[128,1024]{1,0:T(8,128)(2,1)}, bf16[128,1024]{1,0:T(8,128)(2,1)S(1)}, u32[]{:S(2)}, u32[]{:S(2)}) collective-permute-start(bf16[128,1024]{1,0:T(8,128)(2,1)} %get-tuple-element.134), channel_id=1, source_target_pairs={{0,24},{8,16},{16,8},{24,0},{1,25},{9,17},{17,9},{25,1},{2,26},{10... | collective-permute-start | bytes 786440 | tf_op jit(solution)/shard_map/ppermute | solution.py:42
  (80 other events, 622.4 us)
Sparse Core Ops, SparseCore 0:
  10.9 69.4 all-gather.2
  82.6 52.7 all-gather.4
  189.1 54.5 reduce-scatter.1
